TPU v7x, 32 devices: a whole 2x2x4 slice. The times are simulated.
32 devices in a mesh: wrap: 8 (over y, x, core), span: 4 (over z).
Axes of the slice: x: 2, y: 2, z: 4, core: 2. Of those that a mesh axis runs over, the one named last changes fastest.
Arguments:
- density: float32 [128, 16, 512], P('wrap', None, 'span'), may hold values from 0.8 to 1.2
- velocity: float32 [3, 128, 16, 512], P(None, 'wrap', None, 'span'), may hold values from -0.4 to 0.4
- pressure: float32 [128, 16, 512], P('wrap', None, 'span'), may hold values from 0.7 to 1.4
- metrics: float32 [9, 128, 16, 512], P(None, 'wrap', None, 'span'), may hold values from -0.3 to 0.3
- volume: float32 [128, 16, 512], P('wrap', None, 'span'), may hold values from 0.5 to 2
- wake_partner: int32 [128], P('wrap'), may hold values from 0 to 127, as said below
- iblank: int32 [128, 16, 512], P('wrap', None, 'span'), may hold values 0 or 1
Outputs:
- final_state: float32 [5, 128, 16, 512], P(None, 'wrap', None, 'span')
Inputs may be any that keep to these rules, and one draw needn't show every extreme that they name: For i in i-slab s (rows s * 16 to (s + 1) * 16 - 1, s from 0), wake_partner[i] is one of the rows (n - 1 - s) * 16 to (n - s) * 16 - 1 with n = 8; each of those rows is named once.
All inputs are finite; a program needn't handle non-finite values. No bound on the sum of `iblank` on one device may be relied on, other than what follows from the above.
Results may differ from a plain program's by a relative error of at most 0.0003.
Values sent between devices are 32-bit elements; how exact they have to be, the bound alone decides.
No kernel may reach another device: no remote copies, remote signals or barrier semaphores. Data moves between devices by JAX's collectives and lax.ppermute only.
A program may use at most 64 MiB of HBM per device.

v0:
```python
import jax
import jax.numpy as jnp
from jax import lax
from jax.sharding import PartitionSpec as P

epsilon = 1e-06
viscosity = 0.8
conduction = 1.0
time_step = 0.05


def padded(shard, sides, width):
    for axis, dim in sides:
        size, length = (lax.axis_size(axis), shard.shape[dim])
        up = [(i, (i + 1) % size) for i in range(size)]
        down = [(j, i) for i, j in up]
        last = lax.slice_in_dim(shard, length - width, length, axis=dim)
        initial = lax.slice_in_dim(shard, 0, width, axis=dim)
        before = lax.ppermute(last, axis, up)
        after = lax.ppermute(initial, axis, down)
        shard = jnp.concatenate([before, shard, after], axis=dim)
    return shard


def partner(value, axis, distance):
    mask = 2**distance
    pairs = [(source, source ^ mask) for source in range(lax.axis_size(axis))]
    return lax.ppermute(value, axis, pairs)


def window(array, start, length, array_dim):
    return lax.slice_in_dim(array, start, start + length, axis=array_dim)


def reconstruct(first, second, third, fourth, fifth):
    guess_left = (2.0 * first - 7.0 * second + 11.0 * third) / 6.0
    guess_mid = (-second + 5.0 * third + 2.0 * fourth) / 6.0
    guess_right = (2.0 * third + 5.0 * fourth - fifth) / 6.0
    smooth_left = (
        13.0 / 12.0 * (first - 2.0 * second + third) ** 2
        + 0.25 * (first - 4.0 * second + 3.0 * third) ** 2
    )
    smooth_mid = 13.0 / 12.0 * (second - 2.0 * third + fourth) ** 2 + 0.25 * (second - fourth) ** 2
    smooth_right = (
        13.0 / 12.0 * (third - 2.0 * fourth + fifth) ** 2
        + 0.25 * (3.0 * third - 4.0 * fourth + fifth) ** 2
    )
    weight_left = 0.1 / (epsilon + smooth_left) ** 2
    weight_mid = 0.6 / (epsilon + smooth_mid) ** 2
    weight_right = 0.3 / (epsilon + smooth_right) ** 2
    return (weight_left * guess_left + weight_mid * guess_mid + weight_right * guess_right) / (
        weight_left + weight_mid + weight_right
    )


def divergence(state, metric_row, array_dim):
    cells = state.shape[array_dim] - 6
    faces = cells + 1
    density = state[0:1]
    velocity = state[1:4] / density
    speed_sq = jnp.sum(velocity * velocity, axis=0, keepdims=True)
    pressure = 0.4 * (state[4:5] - 0.5 * density * speed_sq)
    contra = jnp.sum(metric_row * velocity, axis=0, keepdims=True)
    metric_sq = jnp.sum(metric_row * metric_row, axis=0, keepdims=True)
    wave_speed = jnp.abs(contra) + jnp.sqrt(1.4 * pressure / density * metric_sq)
    fluxes = jnp.concatenate(
        [
            density * contra,
            state[1:4] * contra + metric_row * pressure,
            (state[4:5] + pressure) * contra,
        ],
        axis=0,
    )
    split_plus = 0.5 * (fluxes + wave_speed * state)
    split_minus = 0.5 * (fluxes - wave_speed * state)
    inviscid = reconstruct(
        window(split_plus, 0, faces, array_dim),
        window(split_plus, 1, faces, array_dim),
        window(split_plus, 2, faces, array_dim),
        window(split_plus, 3, faces, array_dim),
        window(split_plus, 4, faces, array_dim),
    )
    inviscid = inviscid + reconstruct(
        window(split_minus, 5, faces, array_dim),
        window(split_minus, 4, faces, array_dim),
        window(split_minus, 3, faces, array_dim),
        window(split_minus, 2, faces, array_dim),
        window(split_minus, 1, faces, array_dim),
    )
    heat = 0.5 * speed_sq + conduction * pressure / density
    diffused = jnp.concatenate([velocity, heat], axis=0)
    face_metric = 0.5 * (
        window(metric_sq, 2, faces, array_dim) + window(metric_sq, 3, faces, array_dim)
    )
    viscous = (
        viscosity
        * face_metric
        * (window(diffused, 3, faces, array_dim) - window(diffused, 2, faces, array_dim))
    )
    net_flux = jnp.concatenate([-inviscid[0:1], viscous - inviscid[1:5]], axis=0)
    return window(net_flux, 1, cells, array_dim) - window(net_flux, 0, cells, array_dim)


def identity_row(which):
    return jnp.eye(3, dtype=jnp.float32)[which][:, None, None, None]


def conserved(density, velocity, pressure):
    speed_sq = jnp.sum(velocity * velocity, axis=0)
    return jnp.concatenate(
        [
            density[None],
            density[None] * velocity,
            (pressure / 0.4 + 0.5 * density * speed_sq)[None],
        ],
        axis=0,
    )


def fix_ends(extended):
    position = lax.axis_index("wrap")
    slab_count = lax.axis_size("wrap")
    lower_edge = jnp.broadcast_to(extended[:, 3:4], extended[:, 0:3].shape)
    upper_edge = jnp.broadcast_to(extended[:, -4:-3], extended[:, 0:3].shape)
    lower_rim = jnp.where(position == 0, lower_edge, extended[:, 0:3])
    upper_rim = jnp.where(position == slab_count - 1, upper_edge, extended[:, -3:])
    return jnp.concatenate([lower_rim, extended[:, 3:-3], upper_rim], axis=1)


def body(density, velocity, pressure, metrics, volume, wake_partner, iblank):
    state0 = conserved(density, velocity, pressure)
    metric_chord = fix_ends(padded(metrics[0:3], (("wrap", 1),), 3)) + identity_row(0)
    metric_span = padded(metrics[6:9], (("span", 3),), 3) + identity_row(2)
    metric_normal = jnp.pad(
        metrics[3:6] + identity_row(1), ((0, 0), (0, 0), (3, 3), (0, 0)), mode="edge"
    )
    mask = iblank.astype(jnp.float32)[None]

    def evaluate(state):
        extended = fix_ends(padded(state, (("wrap", 1), ("span", 3)), 3))
        padded_chord = extended[:, :, :, 3:-3]
        padded_span = extended[:, 3:-3, :, :]
        wake_rows = state[:, :, 1:4, :]
        mirrored = wake_rows
        for which_bit in range(lax.axis_size("wrap").bit_length() - 1):
            mirrored = partner(mirrored, "wrap", which_bit)
        slab_start = (lax.axis_size("wrap") - 1 - lax.axis_index("wrap")) * wake_rows.shape[1]
        partner_rows = jnp.take(mirrored, wake_partner - slab_start, axis=1)
        below = partner_rows[:, :, ::-1, :]
        above = jnp.broadcast_to(state[:, :, -1:, :], below.shape)
        padded_normal = jnp.concatenate([below, state, above], axis=2)
        total = (
            divergence(padded_chord, metric_chord, 1)
            + divergence(padded_normal, metric_normal, 2)
            + divergence(padded_span, metric_span, 3)
        )
        return total / volume[None]

    state1 = state0 + time_step * mask * evaluate(state0)
    return 0.5 * state0 + 0.5 * (state1 + time_step * mask * evaluate(state1))


def solution(mesh):
    placed = (
        P("wrap", None, "span"),
        P(None, "wrap", None, "span"),
        P("wrap", None, "span"),
        P(None, "wrap", None, "span"),
        P("wrap", None, "span"),
        P("wrap"),
        P("wrap", None, "span"),
    )
    return jax.shard_map(
        body, mesh=mesh, in_specs=placed, out_specs=P(None, "wrap", None, "span"), check_vma=False
    )
```

profile of v0, /device:TPU:0, one launch (start us, length us, event | category | flops | bytes accessed | tf_op | source)
XLA Modules:
  0.0 144.1 jit_solution(5702196340653204907)
XLA Ops:
  1.7 3.3 %collective-permute-start.5 = (f32[3,3,16,128]{3,1,2,0:T(4,128)}, f32[3,3,16,128]{3,1,2,0:T(4,128)S(1)}, u32[]{:S(2)}, u32[]{:S(2)}) collective-permute-start(f32[3,3,16,128]{3,1,2,0:T(4,128)} %copy.83), channel_id=1, source_target_pairs={{4,0},{8,4},{12,8},{16,12},{20,16},{24,20},{28,24},{0,28},{5,1},{9... | collective-permute-start | bytes 221192 | tf_op jit(solution)/shard_map/ppermute | solution.py:20
  10.0 2.1 %collective-permute-start.1 = (f32[5,3,16,128]{3,1,2,0:T(4,128)}, f32[5,3,16,128]{3,1,2,0:T(4,128)S(1)}, u32[]{:S(2)}, u32[]{:S(2)}) collective-permute-start(f32[5,3,16,128]{3,1,2,0:T(4,128)} %get-tuple-element.98), channel_id=1, source_target_pairs={{4,0},{8,4},{12,8},{16,12},{20,16},{24,20},{28,24},{0,28},{5,1},{9... | collective-permute-start | bytes 368648 | tf_op jit(solution)/shard_map/ppermute | solution.py:20
  14.5 1.6 %copy.69 = f32[16,16,128]{2,0,1:T(8,128)} copy(f32[16,16,128]{2,1,0:T(8,128)} %param.13) | data formatting | bytes 262144 | tf_op args[4]
  17.8 1.9 %copy.85 = f32[3,16,16,3]{3,1,2,0:T(8,128)} copy(f32[3,16,16,3]{3,2,1,0:T(8,128)} %get-tuple-element.68) | data formatting | bytes 18432
  23.1 3.7 %collective-permute-start.10 = (f32[3,16,16,3]{3,1,2,0:T(8,128)}, f32[3,16,16,3]{3,1,2,0:T(8,128)}, u32[]{:S(2)}, u32[]{:S(2)}) collective-permute-start(f32[3,16,16,3]{3,1,2,0:T(8,128)} %copy.87), channel_id=1, source_target_pairs={{1,0},{2,1},{3,2},{0,3},{5,4},{6,5},{7,6},{4,7},{9,8},{10,9},{11,1... | collective-permute-start | bytes 27656 | tf_op jit(solution)/shard_map/ppermute | solution.py:20
  29.3 3.8 %collective-permute-start.3 = (f32[5,22,16,3]{1,2,3,0:T(8,128)S(1)}, f32[5,22,16,3]{1,2,3,0:T(8,128)}, u32[]{:S(2)}, u32[]{:S(2)}) collective-permute-start(f32[5,22,16,3]{1,2,3,0:T(8,128)S(1)} %copy.57), channel_id=1, source_target_pairs={{1,0},{2,1},{3,2},{0,3},{5,4},{6,5},{7,6},{4,7},{9,8},{10,9},{11,1... | collective-permute-start | bytes 63368 | tf_op jit(solution)/shard_map/ppermute | solution.py:20
  33.8 2.1 %collective-permute-start.7 = (f32[5,16,3,128]{3,1,2,0:T(8,128)}, f32[5,16,3,128]{3,1,2,0:T(8,128)}, u32[]{:S(2)}, u32[]{:S(2)}) collective-permute-start(f32[5,16,3,128]{3,1,2,0:T(8,128)} %collective-permute-done.6), channel_id=1, source_target_pairs={{0,8},{4,12},{8,0},{12,4},{16,24},{20,28},{24,16},{28,20},{1,9},{5... | collective-permute-start | bytes 368648 | tf_op jit(solution)/shard_map/ppermute | solution.py:28
  35.9 13.8 %collective-permute-done.2 = f32[5,22,16,3]{1,2,3,0:T(8,128)S(1)} collective-permute-done((f32[5,22,16,3]{1,2,3,0:T(8,128)}, f32[5,22,16,3]{1,2,3,0:T(8,128)S(1)}, u32[]{:S(2)}, u32[]{:S(2)}) %collective-permute-start.2) | collective-permute-done | bytes 21152 | tf_op jit(solution)/shard_map/ppermute | solution.py:19
  54.0 1.7 %multiply_reduce_fusion.2 = (f32[16,16,134]{2,0,1:T(8,128)S(1)}, f32[16,16,134]{2,0,1:T(8,128)S(1)}, f32[16,16,134]{2,0,1:T(8,128)S(1)}, f32[3,16,16,134]{3,1,2,0:T(8,128)S(1)}, f32[3,16,16,134]{3,1,2,0:T(8,128)S(1)}) fusion(f32[16,16,134]{2,0,1:T(8,128)S(1)} %bitcast.209, f32[5,22,16,134]{3,1,2,0:T(8,128)S(1)} %pad_maximum_fusion, ...), kind=kLoop, calls=%fused_computation.64 | loop fusion | flops 926208 | bytes 2195468 | tf_op jit(solution)/shard_map/reduce_sum | solution.py:64
  60.1 6.8 %divide_add_fusion.1 = f32[5,16,16,129]{3,1,2,0:T(8,128)S(1)} fusion(f32[5,16,16,134]{3,1,2,0:T(8,128)S(1)} %get-tuple-element.47, f32[5,16,16,134]{3,1,2,0:T(8,128)S(1)} %get-tuple-element.46), kind=kLoop, calls=%fused_computation.13 | loop fusion | flops 21300480 | bytes 7265280 | tf_op jit(solution)/shard_map/add | solution.py:83
  68.0 5.0 %divide_add_fusion.3 = f32[5,17,16,128]{3,1,2,0:T(8,128)S(1)} fusion(f32[5,22,16,128]{3,1,2,0:T(8,128)S(1)} %get-tuple-element.51, f32[5,22,16,128]{3,1,2,0:T(8,128)S(1)} %get-tuple-element.50), kind=kLoop, calls=%fused_computation.41 | loop fusion | flops 22456320 | bytes 7659520 | tf_op jit(solution)/shard_map/add | solution.py:83
  73.0 1.7 %slice_subtract_fusion.1 = f32[4,16,16,129]{3,1,2,0:T(8,128)} fusion(f32[5,16,16,129]{3,1,2,0:T(8,128)S(1)} %divide_add_fusion.1, f32[1,16,16,134]{3,1,2,0:T(8,128)S(1)} %get-tuple-element.31, f32[3,16,16,134]{3,1,2,0:T(8,128)S(1)} %get-tuple-element.33, f32[16,16,129]{2,0,1:T(8,128)S(1)} %fusion.43), kind=kLoop, calls=%fused_computation.20 | loop fusion | flops 660480 | bytes 1737728 | tf_op jit(solution)/shard_map/sub | solution.py:100
  76.5 3.6 %collective-permute-done.8 = f32[5,16,3,128]{3,1,2,0:T(8,128)S(1)} collective-permute-done((f32[5,16,3,128]{3,1,2,0:T(8,128)}, f32[5,16,3,128]{3,1,2,0:T(8,128)S(1)}, u32[]{:S(2)}, u32[]{:S(2)}) %collective-permute-start.8) | collective-permute-done | bytes 122912 | tf_op jit(solution)/shard_map/ppermute | solution.py:28
  82.8 3.1 %divide_add_fusion.5 = f32[5,16,17,128]{3,1,2,0:T(8,128)S(1)} fusion(f32[5,16,22,128]{3,1,2,0:T(8,128)S(1)} %get-tuple-element.59, f32[5,16,22,128]{3,1,2,0:T(8,128)S(1)} %get-tuple-element.58), kind=kLoop, calls=%fused_computation.79 | loop fusion | flops 22456320 | bytes 7659520 | tf_op jit(solution)/shard_map/add | solution.py:83
  87.8 2.6 %collective-permute-start.12 = (f32[5,3,16,128]{3,1,2,0:T(4,128)S(1)}, f32[5,3,16,128]{3,1,2,0:T(4,128)S(1)}, u32[]{:S(2)}, u32[]{:S(2)}) collective-permute-start(f32[5,3,16,128]{3,1,2,0:T(4,128)S(1)} %get-tuple-element.96), channel_id=1, source_target_pairs={{4,0},{8,4},{12,8},{16,12},{20,16},{24,20},{28,24},{0,28},{5,1},{9... | collective-permute-start | bytes 368648 | tf_op jit(solution)/shard_map/ppermute | solution.py:20
  91.1 3.4 %collective-permute-done.11 = f32[5,3,16,128]{3,1,2,0:T(4,128)S(1)} collective-permute-done((f32[5,3,16,128]{3,1,2,0:T(4,128)S(1)}, f32[5,3,16,128]{3,1,2,0:T(4,128)S(1)}, u32[]{:S(2)}, u32[]{:S(2)}) %collective-permute-start.11) | collective-permute-done | bytes 122912 | tf_op jit(solution)/shard_map/ppermute | solution.py:19
  100.8 5.8 %collective-permute-done.13 = f32[5,22,16,3]{1,2,3,0:T(8,128)S(1)} collective-permute-done((f32[5,22,16,3]{1,2,3,0:T(8,128)}, f32[5,22,16,3]{1,2,3,0:T(8,128)S(1)}, u32[]{:S(2)}, u32[]{:S(2)}) %collective-permute-start.13) | collective-permute-done | bytes 21152 | tf_op jit(solution)/shard_map/ppermute | solution.py:19
  108.8 2.0 %pad_maximum_fusion.41 = (f32[5,1,16,134]{3,1,2,0:T(1,128)S(1)}, f32[5,1,16,134]{3,1,2,0:T(1,128)S(1)}) fusion(f32[5,22,16,3]{3,1,2,0:T(8,128)S(1)} %copy.73, f32[5,22,16,3]{3,1,2,0:T(8,128)S(1)} %copy.72, f32[5,3,16,128]{3,1,2,0:T(4,128)} %copy-done.14, f32[5,16,16,128]{3,1,2,0:T(8,128)S(1)} %fusion.24, f32[5,3,16,128]{3,1,2,0:T(4,128)} %copy-done.12), kind=kLoop, calls=%fused_computation.245 | loop fusion | flops 85760 | bytes 1029120 | tf_op jit(solution)/shard_map/slice | solution.py:123
  115.7 6.9 %divide_add_fusion = f32[5,16,16,129]{3,1,2,0:T(8,128)S(1)} fusion(f32[5,16,16,134]{3,1,2,0:T(8,128)S(1)} %get-tuple-element.45, f32[5,16,16,134]{3,1,2,0:T(8,128)S(1)} %get-tuple-element.44), kind=kLoop, calls=%fused_computation.10 | loop fusion | flops 21300480 | bytes 7265280 | tf_op jit(solution)/shard_map/add | solution.py:83
  123.6 5.0 %divide_add_fusion.2 = f32[5,17,16,128]{3,1,2,0:T(8,128)S(1)} fusion(f32[5,22,16,128]{3,1,2,0:T(8,128)S(1)} %get-tuple-element.49, f32[5,22,16,128]{3,1,2,0:T(8,128)S(1)} %get-tuple-element.48), kind=kLoop, calls=%fused_computation.38 | loop fusion | flops 22456320 | bytes 7659520 | tf_op jit(solution)/shard_map/add | solution.py:83
  128.6 1.7 %slice_subtract_fusion = f32[4,16,16,129]{3,1,2,0:T(8,128)} fusion(f32[5,16,16,129]{3,1,2,0:T(8,128)S(1)} %divide_add_fusion, f32[1,16,16,134]{3,1,2,0:T(8,128)S(1)} %get-tuple-element.28, f32[3,16,16,134]{3,1,2,0:T(8,128)S(1)} %get-tuple-element.30, f32[16,16,129]{2,0,1:T(8,128)S(1)} %copy-done.24), kind=kLoop, calls=%fused_computation.16 | loop fusion | flops 660480 | bytes 1737728 | tf_op jit(solution)/shard_map/sub | solution.py:100
  130.5 2.2 %collective-permute-start.17 = (f32[5,16,3,128]{3,1,2,0:T(8,128)}, f32[5,16,3,128]{3,1,2,0:T(8,128)S(1)}, u32[]{:S(2)}, u32[]{:S(2)}) collective-permute-start(f32[5,16,3,128]{3,1,2,0:T(8,128)} %collective-permute-done.16), channel_id=1, source_target_pairs={{0,16},{4,20},{8,24},{12,28},{16,0},{20,4},{24,8},{28,12},{1,17},{... | collective-permute-start | bytes 368648 | tf_op jit(solution)/shard_map/ppermute | solution.py:28
  132.7 3.1 %collective-permute-done.17 = f32[5,16,3,128]{3,1,2,0:T(8,128)S(1)} collective-permute-done((f32[5,16,3,128]{3,1,2,0:T(8,128)}, f32[5,16,3,128]{3,1,2,0:T(8,128)S(1)}, u32[]{:S(2)}, u32[]{:S(2)}) %collective-permute-start.17) | collective-permute-done | bytes 122912 | tf_op jit(solution)/shard_map/ppermute | solution.py:28
  138.3 3.1 %divide_add_fusion.4 = f32[5,16,17,128]{3,1,2,0:T(8,128)S(1)} fusion(f32[5,16,22,128]{3,1,2,0:T(8,128)S(1)} %get-tuple-element.57, f32[5,16,22,128]{3,1,2,0:T(8,128)S(1)} %get-tuple-element.56), kind=kLoop, calls=%fused_computation.78 | loop fusion | flops 22456320 | bytes 7659520 | tf_op jit(solution)/shard_map/add | solution.py:83
  (232 shorter events, 53.2 us)
Async XLA Ops:
  0.0 7.8 %copy-start.31 = (f32[3,16,16,128]{3,2,1,0:T(8,128)S(1)}, f32[3,16,16,128]{3,2,1,0:T(8,128)}, u32[]{:S(2)}) copy-start(f32[3,16,16,128]{3,2,1,0:T(8,128)} %param.10) | copy-start | bytes 1179652
  1.7 21.5 %collective-permute-start.5 = (f32[3,3,16,128]{3,1,2,0:T(4,128)}, f32[3,3,16,128]{3,1,2,0:T(4,128)S(1)}, u32[]{:S(2)}, u32[]{:S(2)}) collective-permute-start(f32[3,3,16,128]{3,1,2,0:T(4,128)} %copy.83), channel_id=1, source_target_pairs={{4,0},{8,4},{12,8},{16,12},{20,16},{24,20},{28,24},{0,28},{5,1},{9... | collective-permute-start | bytes 221192 | tf_op jit(solution)/shard_map/ppermute | solution.py:20
  5.7 27.5 %collective-permute-start.4 = (f32[3,3,16,128]{3,1,2,0:T(4,128)}, f32[3,3,16,128]{3,1,2,0:T(4,128)}, u32[]{:S(2)}, u32[]{:S(2)}) collective-permute-start(f32[3,3,16,128]{3,1,2,0:T(4,128)} %copy.81), channel_id=1, source_target_pairs={{0,4},{4,8},{8,12},{12,16},{16,20},{20,24},{24,28},{28,0},{1,5},{5... | collective-permute-start | bytes 221192 | tf_op jit(solution)/shard_map/ppermute | solution.py:19
  8.7 25.1 %collective-permute-start.6 = (f32[5,16,3,128]{3,1,2,0:T(8,128)}, f32[5,16,3,128]{3,1,2,0:T(8,128)}, u32[]{:S(2)}, u32[]{:S(2)}) collective-permute-start(f32[5,16,3,128]{3,1,2,0:T(8,128)} %slice.705), channel_id=1, source_target_pairs={{0,4},{4,0},{8,12},{12,8},{16,20},{20,16},{24,28},{28,24},{1,5},{5... | collective-permute-start | bytes 368648 | tf_op jit(solution)/shard_map/ppermute | solution.py:28
  9.5 17.3 %collective-permute-start = (f32[5,3,16,128]{3,1,2,0:T(4,128)}, f32[5,3,16,128]{3,1,2,0:T(4,128)S(1)}, u32[]{:S(2)}, u32[]{:S(2)}) collective-permute-start(f32[5,3,16,128]{3,1,2,0:T(4,128)} %get-tuple-element.97), channel_id=1, source_target_pairs={{0,4},{4,8},{8,12},{12,16},{16,20},{20,24},{24,28},{28,0},{1,5},{5... | collective-permute-start | bytes 368648 | tf_op jit(solution)/shard_map/ppermute | solution.py:19
  10.0 16.9 %collective-permute-start.1 = (f32[5,3,16,128]{3,1,2,0:T(4,128)}, f32[5,3,16,128]{3,1,2,0:T(4,128)S(1)}, u32[]{:S(2)}, u32[]{:S(2)}) collective-permute-start(f32[5,3,16,128]{3,1,2,0:T(4,128)} %get-tuple-element.98), channel_id=1, source_target_pairs={{4,0},{8,4},{12,8},{16,12},{20,16},{24,20},{28,24},{0,28},{5,1},{9... | collective-permute-start | bytes 368648 | tf_op jit(solution)/shard_map/ppermute | solution.py:20
  21.5 60.9 %copy-start.2 = (f32[3,16,16,128]{3,1,2,0:T(8,128)}, f32[3,16,16,128]{3,1,2,0:T(8,128)S(1)}, u32[]{:S(2)}) copy-start(f32[3,16,16,128]{3,1,2,0:T(8,128)S(1)} %copy_add_fusion) | copy-start | bytes 1179652
  23.1 30.1 %collective-permute-start.10 = (f32[3,16,16,3]{3,1,2,0:T(8,128)}, f32[3,16,16,3]{3,1,2,0:T(8,128)}, u32[]{:S(2)}, u32[]{:S(2)}) collective-permute-start(f32[3,16,16,3]{3,1,2,0:T(8,128)} %copy.87), channel_id=1, source_target_pairs={{1,0},{2,1},{3,2},{0,3},{5,4},{6,5},{7,6},{4,7},{9,8},{10,9},{11,1... | collective-permute-start | bytes 27656 | tf_op jit(solution)/shard_map/ppermute | solution.py:20
  26.8 40.3 %copy-start.19 = (f32[3,3,16,128]{3,1,2,0:T(4,128)}, f32[3,3,16,128]{3,1,2,0:T(4,128)S(1)}, u32[]{:S(2)}) copy-start(f32[3,3,16,128]{3,1,2,0:T(4,128)S(1)} %broadcast_select_fusion) | copy-start | bytes 221188
  26.8 26.2 %copy-start.10 = (f32[5,3,16,128]{3,1,2,0:T(4,128)}, f32[5,3,16,128]{3,1,2,0:T(4,128)S(1)}, u32[]{:S(2)}) copy-start(f32[5,3,16,128]{3,1,2,0:T(4,128)S(1)} %collective-permute-done) | copy-start | bytes 368644
  26.8 26.4 %collective-permute-start.9 = (f32[3,16,16,3]{3,1,2,0:T(8,128)}, f32[3,16,16,3]{3,1,2,0:T(8,128)}, u32[]{:S(2)}, u32[]{:S(2)}) collective-permute-start(f32[3,16,16,3]{3,1,2,0:T(8,128)} %copy.85), channel_id=1, source_target_pairs={{0,1},{1,2},{2,3},{3,0},{4,5},{5,6},{6,7},{7,4},{8,9},{9,10},{10,1... | collective-permute-start | bytes 27656 | tf_op jit(solution)/shard_map/ppermute | solution.py:19
  29.3 21.0 %collective-permute-start.3 = (f32[5,22,16,3]{1,2,3,0:T(8,128)S(1)}, f32[5,22,16,3]{1,2,3,0:T(8,128)}, u32[]{:S(2)}, u32[]{:S(2)}) collective-permute-start(f32[5,22,16,3]{1,2,3,0:T(8,128)S(1)} %copy.57), channel_id=1, source_target_pairs={{1,0},{2,1},{3,2},{0,3},{5,4},{6,5},{7,6},{4,7},{9,8},{10,9},{11,1... | collective-permute-start | bytes 63368 | tf_op jit(solution)/shard_map/ppermute | solution.py:20
  33.1 16.6 %collective-permute-start.2 = (f32[5,22,16,3]{1,2,3,0:T(8,128)}, f32[5,22,16,3]{1,2,3,0:T(8,128)S(1)}, u32[]{:S(2)}, u32[]{:S(2)}) collective-permute-start(f32[5,22,16,3]{1,2,3,0:T(8,128)} %copy.56), channel_id=1, source_target_pairs={{0,1},{1,2},{2,3},{3,0},{4,5},{5,6},{6,7},{7,4},{8,9},{9,10},{10,1... | collective-permute-start | bytes 63368 | tf_op jit(solution)/shard_map/ppermute | solution.py:19
  33.8 41.1 %collective-permute-start.7 = (f32[5,16,3,128]{3,1,2,0:T(8,128)}, f32[5,16,3,128]{3,1,2,0:T(8,128)}, u32[]{:S(2)}, u32[]{:S(2)}) collective-permute-start(f32[5,16,3,128]{3,1,2,0:T(8,128)} %collective-permute-done.6), channel_id=1, source_target_pairs={{0,8},{4,12},{8,0},{12,4},{16,24},{20,28},{24,16},{28,20},{1,9},{5... | collective-permute-start | bytes 368648 | tf_op jit(solution)/shard_map/ppermute | solution.py:28
  55.9 17.0 %copy-start.23 = (f32[16,16,129]{2,0,1:T(8,128)}, f32[16,16,129]{2,0,1:T(8,128)S(1)}, u32[]{:S(2)}) copy-start(f32[16,16,129]{2,0,1:T(8,128)S(1)} %fusion.43) | copy-start | bytes 396292
  60.0 14.7 %copy-start.29 = (f32[17,16,128]{2,0,1:T(8,128)}, f32[17,16,128]{2,0,1:T(8,128)S(1)}, u32[]{:S(2)}) copy-start(f32[17,16,128]{2,0,1:T(8,128)S(1)} %fusion.53) | copy-start | bytes 417796
  74.9 5.2 %collective-permute-start.8 = (f32[5,16,3,128]{3,1,2,0:T(8,128)}, f32[5,16,3,128]{3,1,2,0:T(8,128)S(1)}, u32[]{:S(2)}, u32[]{:S(2)}) collective-permute-start(f32[5,16,3,128]{3,1,2,0:T(8,128)} %collective-permute-done.7), channel_id=1, source_target_pairs={{0,16},{4,20},{8,24},{12,28},{16,0},{20,4},{24,8},{28,12},{1,17},{... | collective-permute-start | bytes 368648 | tf_op jit(solution)/shard_map/ppermute | solution.py:28
  87.7 6.7 %collective-permute-start.11 = (f32[5,3,16,128]{3,1,2,0:T(4,128)S(1)}, f32[5,3,16,128]{3,1,2,0:T(4,128)S(1)}, u32[]{:S(2)}, u32[]{:S(2)}) collective-permute-start(f32[5,3,16,128]{3,1,2,0:T(4,128)S(1)} %get-tuple-element.95), channel_id=1, source_target_pairs={{0,4},{4,8},{8,12},{12,16},{16,20},{20,24},{24,28},{28,0},{1,5},{5... | collective-permute-start | bytes 368648 | tf_op jit(solution)/shard_map/ppermute | solution.py:19
  87.8 6.7 %collective-permute-start.12 = (f32[5,3,16,128]{3,1,2,0:T(4,128)S(1)}, f32[5,3,16,128]{3,1,2,0:T(4,128)S(1)}, u32[]{:S(2)}, u32[]{:S(2)}) collective-permute-start(f32[5,3,16,128]{3,1,2,0:T(4,128)S(1)} %get-tuple-element.96), channel_id=1, source_target_pairs={{4,0},{8,4},{12,8},{16,12},{20,16},{24,20},{28,24},{0,28},{5,1},{9... | collective-permute-start | bytes 368648 | tf_op jit(solution)/shard_map/ppermute | solution.py:20
  91.1 9.7 %collective-permute-start.15 = (f32[5,16,3,128]{3,1,2,0:T(8,128)}, f32[5,16,3,128]{3,1,2,0:T(8,128)}, u32[]{:S(2)}, u32[]{:S(2)}) collective-permute-start(f32[5,16,3,128]{3,1,2,0:T(8,128)} %slice.772), channel_id=1, source_target_pairs={{0,4},{4,0},{8,12},{12,8},{16,20},{20,16},{24,28},{28,24},{1,5},{5... | collective-permute-start | bytes 368648 | tf_op jit(solution)/shard_map/ppermute | solution.py:28
  98.1 9.1 %collective-permute-start.14 = (f32[5,22,16,3]{1,2,3,0:T(8,128)S(1)}, f32[5,22,16,3]{1,2,3,0:T(8,128)}, u32[]{:S(2)}, u32[]{:S(2)}) collective-permute-start(f32[5,22,16,3]{1,2,3,0:T(8,128)S(1)} %copy.71), channel_id=1, source_target_pairs={{1,0},{2,1},{3,2},{0,3},{5,4},{6,5},{7,6},{4,7},{9,8},{10,9},{11,1... | collective-permute-start | bytes 63368 | tf_op jit(solution)/shard_map/ppermute | solution.py:20
  99.7 6.9 %collective-permute-start.13 = (f32[5,22,16,3]{1,2,3,0:T(8,128)}, f32[5,22,16,3]{1,2,3,0:T(8,128)S(1)}, u32[]{:S(2)}, u32[]{:S(2)}) collective-permute-start(f32[5,22,16,3]{1,2,3,0:T(8,128)} %copy.70), channel_id=1, source_target_pairs={{0,1},{1,2},{2,3},{3,0},{4,5},{5,6},{6,7},{7,4},{8,9},{9,10},{10,1... | collective-permute-start | bytes 63368 | tf_op jit(solution)/shard_map/ppermute | solution.py:19
  100.8 29.7 %collective-permute-start.16 = (f32[5,16,3,128]{3,1,2,0:T(8,128)}, f32[5,16,3,128]{3,1,2,0:T(8,128)}, u32[]{:S(2)}, u32[]{:S(2)}) collective-permute-start(f32[5,16,3,128]{3,1,2,0:T(8,128)} %collective-permute-done.15), channel_id=1, source_target_pairs={{0,8},{4,12},{8,0},{12,4},{16,24},{20,28},{24,16},{28,20},{1,9},{5... | collective-permute-start | bytes 368648 | tf_op jit(solution)/shard_map/ppermute | solution.py:28
  130.5 5.3 %collective-permute-start.17 = (f32[5,16,3,128]{3,1,2,0:T(8,128)}, f32[5,16,3,128]{3,1,2,0:T(8,128)S(1)}, u32[]{:S(2)}, u32[]{:S(2)}) collective-permute-start(f32[5,16,3,128]{3,1,2,0:T(8,128)} %collective-permute-done.16), channel_id=1, source_target_pairs={{0,16},{4,20},{8,24},{12,28},{16,0},{20,4},{24,8},{28,12},{1,17},{... | collective-permute-start | bytes 368648 | tf_op jit(solution)/shard_map/ppermute | solution.py:28
  (41 other events, 95.8 us)
where the time goes:
time: 145 us; the launch traced here: 144 us
  other arithmetic  55 us (38%)
  local copies, waits for them, and re-layouts  34.2 us (24%)
  waiting for transfers between devices  29.7 us (20%)
  starting transfers between devices  24.1 us (17%)
    add x6, other arithmetic, divergence(): inviscid + reconstruct(window(split_minus, 5, faces, array_dim), window(s...  29.9 us
    ppermute x6, waiting for transfers between devices, padded(): before = lax.ppermute(last, axis, up)  23.1 us
    ppermute x6, starting transfers between devices, padded(): after = lax.ppermute(initial, axis, down)  17.2 us
    unnamed x104, local copies, waits for them, and re-layouts  15.5 us
    ppermute x6, waiting for transfers between devices, partner(): return lax.ppermute(value, axis, pairs)  6.61 us
    slice x8, local copies, waits for them, and re-layouts, padded(): last = lax.slice_in_dim(shard, length - width, length, axis=dim)  5.99 us
    ppermute x6, starting transfers between devices, partner(): return lax.ppermute(value, axis, pairs)  5.86 us
    sub x6, other arithmetic, divergence(): viscous - inviscid[1:5]  3.88 us
  transfers between devices with their start and end apart: 18, of which 5 were waited for; matrix products, arithmetic and copies ran while one was open for 47% of the time, Pallas kernels for 0%

commit v1 on v0

v1 whole, which is shorter than its diff:
```python
import functools

import jax
import jax.numpy as jnp
from jax import lax
from jax.experimental import pallas as pl
from jax.experimental.pallas import tpu as pltpu
from jax.sharding import PartitionSpec as P

epsilon = 1e-06
viscosity = 0.8
conduction = 1.0
time_step = 0.05
H = 3
F32 = jnp.float32


def point_fluxes(state, row):
    rho, m0, m1, m2, energy = state
    x0, x1, x2 = row
    inverse = 1.0 / rho
    u0, u1, u2 = m0 * inverse, m1 * inverse, m2 * inverse
    speed_sq = u0 * u0 + u1 * u1 + u2 * u2
    pressure = 0.4 * (energy - 0.5 * rho * speed_sq)
    ratio = pressure * inverse
    contra = x0 * u0 + x1 * u1 + x2 * u2
    metric_sq = x0 * x0 + x1 * x1 + x2 * x2
    sound_sq = 1.4 * ratio * metric_sq
    speed = jnp.abs(contra) + sound_sq * lax.rsqrt(jnp.maximum(sound_sq, 1e-30))
    fluxes = (
        rho * contra,
        m0 * contra + x0 * pressure,
        m1 * contra + x1 * pressure,
        m2 * contra + x2 * pressure,
        (energy + pressure) * contra,
    )
    waves = [speed * one for one in state]
    plus = [a + b for a, b in zip(fluxes, waves)]
    minus = [a - b for a, b in zip(fluxes, waves)]
    diffused = (u0, u1, u2, 0.5 * speed_sq + conduction * ratio)
    return plus, minus, diffused, metric_sq


class Split:
    def __init__(self, load):
        self.load, self.memo = load, {}

    def get(self, name, n):
        if (name, n) not in self.memo:
            self.memo[name, n] = getattr(self, "make_" + name)(n)
        return self.memo[name, n]

    def make_v(self, n):
        return self.load(n)

    def make_d(self, n):
        return self.get("v", n + 1) - self.get("v", n)

    def make_e(self, n):
        return self.get("d", n) - self.get("d", n - 1)

    def make_t(self, n):
        return self.get("e", n + 1) - self.get("e", n)

    def make_t2(self, n):
        return self.get("t", n) + self.get("t", n)

    def make_smooth(self, n):
        high, low, bend = self.get("d", n), self.get("d", n - 1), self.get("e", n)
        twice = bend + bend
        a, b = high * twice, low * twice
        centre = (a - b) * (2.0 / 3.0) + (high * low + 16.0 * epsilon / 3.0)
        return centre + a, centre, centre - b

    def correction(self, outer, middle, inner, near, far):
        left = middle * pl.reciprocal(outer, approx=True)
        right = middle * pl.reciprocal(inner, approx=True)
        weight_left = left * left * (1.0 / 3.0)
        weight_right = right * right
        total = (weight_left + weight_right) + 2.0
        return (weight_left * near + weight_right * far) * pl.reciprocal(total, approx=True)


def sweep(load_plus, load_minus, load_diffused, load_metric, store, first, last):
    plus, minus = Split(load_plus), Split(load_minus)
    central, diffused, metric = {}, {}, {}

    def flux_centre(n):
        if n not in central:
            both = plus.get("v", n) + minus.get("v", n)
            central[n] = 6.0 * both - (plus.get("e", n) + minus.get("e", n))
        return central[n]

    def cached(table, load, n):
        if n not in table:
            table[n] = load(n)
        return table[n]

    before = None
    for n in range(first, last + 1):
        up = plus.correction(
            plus.get("smooth", n - 1)[0],
            plus.get("smooth", n)[1],
            plus.get("smooth", n + 1)[2],
            plus.get("t2", n - 1),
            plus.get("t", n),
        )
        down = minus.correction(
            minus.get("smooth", n + 2)[2],
            minus.get("smooth", n + 1)[1],
            minus.get("smooth", n)[0],
            minus.get("t2", n + 1),
            minus.get("t", n),
        )
        correction = down - up
        flux = flux_centre(n) + flux_centre(n + 1) + (plus.get("t", n) - minus.get("t", n))
        flux = flux + (correction + correction)
        face_metric = cached(metric, load_metric, n) + cached(metric, load_metric, n + 1)
        jump = cached(diffused, load_diffused, n + 1) - cached(diffused, load_diffused, n)
        net = face_metric * jump - flux
        if before is not None:
            store(n, net - before)
        before = net


class Lines:
    def __init__(self, plus, minus, diffused, metric, width):
        self.refs, self.width = (plus, minus, diffused, metric), width

    def rows(self, n, count):
        return pl.ds(pl.multiple_of((n + H) * self.width, 8), count)

    def put(self, n, count, state, row):
        plus_ref, minus_ref, diffused_ref, metric_ref = self.refs
        plus, minus, diffused, metric_sq = point_fluxes(state, row)
        rows = self.rows(n, count)
        for f in range(5):
            plus_ref[f, rows, :] = plus[f]
            minus_ref[f, rows, :] = minus[f]
        for m in range(4):
            diffused_ref[1 + m, rows, :] = diffused[m]
        metric_ref[rows, :] = metric_sq * (24.0 * viscosity * 0.5)

    def copy(self, n, source):
        plus_ref, minus_ref, diffused_ref, metric_ref = self.refs
        to, origin = self.rows(n, self.width), self.rows(source, self.width)
        for ref in (plus_ref, minus_ref, diffused_ref):
            ref[:, to, :] = ref[:, origin, :]
        metric_ref[to, :] = metric_ref[origin, :]

    def zero_diffused(self):
        self.refs[2][0] = jnp.zeros(self.refs[2].shape[1:], F32)

    def sweep(self, f, tile, store, first, last):
        def loader(ref, lead):
            return lambda n: ref[lead + (pl.ds(pl.multiple_of((n + H) * self.width + tile * 8, 8), 8), slice(None))]

        plus_ref, minus_ref, diffused_ref, metric_ref = self.refs
        sweep(
            loader(plus_ref, (f,)),
            loader(minus_ref, (f,)),
            loader(diffused_ref, (f,)),
            loader(metric_ref, ()),
            store,
            first,
            last,
        )


def to_span(value, put, height):
    for half in range(2):
        turned = value[half * 128 : (half + 1) * 128].T
        for q in range(4):
            put(q * 2 + half, turned[q * height : (q + 1) * height])


def send_parts(state_ref, span_ref, fields, outs, dims):
    rows_i, height = dims
    low_ref, high_ref, wake_ref, span_low_ref, span_high_ref = outs
    total = rows_i * rows_i
    for f in range(5):
        low_ref[f] = state_ref[f, 0 : H * rows_i, :]
        high_ref[f] = state_ref[f, total - H * rows_i : total, :]
        for r in range(H):
            wake_ref[pl.ds(f * H + r, rows_i, stride=16), :] = state_ref[f, pl.ds(r + 1, rows_i, stride=rows_i), :]
    for f in range(fields):
        for r in range(H):
            span_low_ref[f, 2 * r : 2 * r + 2, :] = span_ref[f, r * 8 : r * 8 + 2, :]
            top = (height - H + r) * 8
            span_high_ref[f, 2 * r : 2 * r + 2, :] = span_ref[f, top + 6 : top + 8, :]


def prepare_kernel(dims, rho_ref, vel_ref, pre_ref, met_ref, state_ref, span_ref, *outs):
    rows_i, height = dims
    total = rows_i * rows_i
    rho, pressure = rho_ref[...], pre_ref[...]
    u = [vel_ref[m] for m in range(3)]
    speed_sq = u[0] * u[0] + u[1] * u[1] + u[2] * u[2]
    state_ref[0] = rho
    for m in range(3):
        state_ref[1 + m] = rho * u[m]
    state_ref[4] = pressure * (1.0 / 0.4) + 0.5 * rho * speed_sq
    low_ref, high_ref = outs[:2]
    for m in range(3):
        low_ref[5 + m] = met_ref[m, 0 : H * rows_i, :]
        high_ref[5 + m] = met_ref[m, total - H * rows_i : total, :]
    for f in range(8):
        value = state_ref[f] if f < 5 else met_ref[6 + f - 5]

        def put(start, block, f=f):
            span_ref[f, pl.ds(start, height, stride=8), :] = block

        to_span(value, put, height)
    send_parts(state_ref, span_ref, 8, outs, dims)


def unit(which, m, value):
    return value + 1.0 if which == m else value


def stage_kernel(dims, final, *refs):
    rows_i, height = dims
    total = rows_i * rows_i
    size_in = 13
    (state_ref, span_ref, span_met_ref, met_ref, vol_ref, blank_ref, partner_ref,
     low_ref, high_ref, met_low_ref, met_high_ref, wake_ref, span_low_ref, span_high_ref) = refs[:14]
    refs = refs[14:]
    if final:
        start_ref, out_ref = refs[:2]
        refs = refs[2:]
    else:
        out_ref, out_span_ref = refs[:2]
        outs = refs[2:7]
        refs = refs[7:]
    acc_ref, acc_span_ref, plus_ref, minus_ref, diffused_ref, metric_ref, ghost_ref, pad_ref, pad_met_ref = refs

    position, count = lax.axis_index("wrap"), lax.axis_size("wrap")
    is_first, is_last = position == 0, position == count - 1

    lines = Lines(plus_ref, minus_ref, diffused_ref, metric_ref, 8)
    lines.zero_diffused()
    def interior_span(step, carry):
        rows = pl.ds(pl.multiple_of(step * 16, 16), 16)
        lines.put(2 * step, 16, [span_ref[f, rows, :] for f in range(5)],
                  [unit(2, m, span_met_ref[5 + m, rows, :]) for m in range(3)])
        return carry

    lax.fori_loop(0, height // 2, interior_span, 0)
    sublane = lax.broadcasted_iota(jnp.int32, (8, 128), 0)
    for r in range(H):
        for f in range(8):
            pad_ref[f, r * 8 : r * 8 + 2, :] = (span_low_ref[f, 2 * r : 2 * r + 2, :])
            pad_ref[f, (H + r) * 8 + 6 : (H + r) * 8 + 8, :] = span_high_ref[f, 2 * r : 2 * r + 2, :]
    for r in range(H):
        def joined(low):
            values = []
            for f in range(8):
                ref = span_ref if f < 5 else span_met_ref
                if low:
                    own = pltpu.roll(ref[f, (height - H + r) * 8 : (height - H + r) * 8 + 8, :], 2, 0)
                    values.append(jnp.where(sublane < 2, pad_ref[f, r * 8 : r * 8 + 8, :], own))
                else:
                    own = pltpu.roll(ref[f, r * 8 : r * 8 + 8, :], 6, 0)
                    values.append(jnp.where(sublane >= 6, pad_ref[f, (H + r) * 8 : (H + r) * 8 + 8, :], own))
            return values[:5], [unit(2, m, values[5 + m]) for m in range(3)]

        lines.put(r - H, 8, *joined(True))
        lines.put(height + r, 8, *joined(False))

    def span_sweep(f, carry):
        def store(n, value):
            acc_span_ref[f, n * 8 : n * 8 + 8, :] = value

        lines.sweep(f, 0, store, -1, height - 1)
        return carry

    lax.fori_loop(0, 5, span_sweep, 0)
    for f in range(5):
        for half in range(2):
            parts = [acc_span_ref[f, pl.ds(q * 2 + half, height, stride=8), :] for q in range(4)]
            acc_ref[f, half * 128 : (half + 1) * 128, :] = jnp.concatenate(parts, axis=0).T

    lines = Lines(plus_ref, minus_ref, diffused_ref, metric_ref, rows_i)

    def interior_chord(n, carry):
        rows = pl.ds(pl.multiple_of(n * rows_i, 16), rows_i)
        lines.put(n, rows_i, [state_ref[f, rows, :] for f in range(5)],
                  [unit(0, m, met_ref[m, rows, :]) for m in range(3)])
        return carry

    lax.fori_loop(0, rows_i, interior_chord, 0)
    for r in range(H):
        rows = slice(r * rows_i, (r + 1) * rows_i)
        edge = slice(0, rows_i)
        lines.put(
            r - H, rows_i,
            [jnp.where(is_first, state_ref[f, edge, :], low_ref[f, rows, :]) for f in range(5)],
            [unit(0, m, jnp.where(is_first, met_ref[m, edge, :], met_low_ref[5 + m, rows, :])) for m in range(3)],
        )
        edge = slice(total - rows_i, total)
        lines.put(
            rows_i + r, rows_i,
            [jnp.where(is_last, state_ref[f, edge, :], high_ref[f, rows, :]) for f in range(5)],
            [unit(0, m, jnp.where(is_last, met_ref[m, edge, :], met_high_ref[5 + m, rows, :])) for m in range(3)],
        )

    def chord_sweep(step, carry):
        f, tile = step // 2, step % 2

        def store(n, value):
            rows = pl.ds(pl.multiple_of(n * rows_i + tile * 8, 8), 8)
            acc_ref[f, rows, :] = acc_ref[f, rows, :] + value

        lines.sweep(f, tile, store, -1, rows_i - 1)
        return carry

    lax.fori_loop(0, 10, chord_sweep, 0)

    def interior_normal(n, carry):
        rows = pl.ds(n, rows_i, stride=rows_i)
        lines.put(n, rows_i, [state_ref[f, rows, :] for f in range(5)],
                  [unit(1, m, met_ref[3 + m, rows, :]) for m in range(3)])
        return carry

    lax.fori_loop(0, rows_i, interior_normal, 0)
    base = (count - 1 - position) * rows_i
    for i in range(rows_i):
        ghost_ref[i * 16 : i * 16 + 16, :] = wake_ref[pl.ds(pl.multiple_of((partner_ref[i] - base) * 16, 16), 16), :]
    wall = pl.ds(0, rows_i, stride=rows_i)
    for r in range(H):
        lines.put(-1 - r, rows_i, [ghost_ref[pl.ds(f * H + r, rows_i, stride=16), :] for f in range(5)],
                  [unit(1, m, met_ref[3 + m, wall, :]) for m in range(3)])
        lines.copy(rows_i + r, rows_i - 1)

    def normal_sweep(step, carry):
        f, tile = step // 2, step % 2

        def store(n, value):
            rows = pl.ds(tile * 8 * rows_i + n, 8, stride=rows_i)
            acc_ref[f, rows, :] = acc_ref[f, rows, :] + value

        lines.sweep(f, tile, store, -1, rows_i - 1)
        return carry

    lax.fori_loop(0, 10, normal_sweep, 0)

    scale = (time_step / 24.0) * blank_ref[...].astype(F32) / vol_ref[...]
    for f in range(5):
        moved = state_ref[f] + scale * acc_ref[f]
        out_ref[f] = 0.5 * start_ref[f] + 0.5 * moved if final else moved
    if not final:
        for f in range(5):
            def put(start, block, f=f):
                out_span_ref[f, pl.ds(start, height, stride=8), :] = block

            to_span(out_ref[f], put, height)
        send_parts(out_ref, out_span_ref, 5, outs, dims)


def shape(*sizes):
    return jax.ShapeDtypeStruct(sizes, F32)


def body(density, velocity, pressure, metrics, volume, wake_partner, iblank):
    rows_i, rows_j, lanes = density.shape
    total, height = rows_i * rows_j, lanes // 4
    dims = (rows_i, height)
    metrics = metrics.reshape(9, total, lanes)
    volume, blank = volume.reshape(total, lanes), iblank.reshape(total, lanes)
    whole = pl.BlockSpec(memory_space=pltpu.VMEM)
    params = pltpu.CompilerParams(vmem_limit_bytes=40 * 2**20)

    def parts(fields):
        edge = H * rows_j
        return [shape(fields, edge, lanes), shape(fields, edge, lanes), shape(rows_i * 16, lanes),
                shape(fields, 8, lanes), shape(fields, 8, lanes)]

    def exchange(sent):
        low, high, wake, span_low, span_high = sent
        n, s = lax.axis_size("wrap"), lax.axis_size("span")
        up = [(i, i + 1) for i in range(n - 1)]
        down = [(i + 1, i) for i in range(n - 1)]
        mirror = [(i, n - 1 - i) for i in range(n)]
        ring_up = [(i, (i + 1) % s) for i in range(s)]
        ring_down = [((i + 1) % s, i) for i in range(s)]
        return (lax.ppermute(high, "wrap", up), lax.ppermute(low, "wrap", down), lax.ppermute(wake, "wrap", mirror),
                lax.ppermute(span_high, "span", ring_up), lax.ppermute(span_low, "span", ring_down))

    state, span, *sent = pl.pallas_call(
        functools.partial(prepare_kernel, dims),
        out_shape=[shape(5, total, lanes), shape(8, total, lanes)] + parts(8),
        in_specs=[whole] * 4,
        out_specs=[whole] * 7,
        compiler_params=params,
        name="prepare",
    )(density.reshape(total, lanes), velocity.reshape(3, total, lanes), pressure.reshape(total, lanes), metrics)
    below, above, wake, span_below, span_above = exchange(sent)

    points = (rows_i + 2 * H) * rows_i
    scratch = [pltpu.VMEM((5, total, lanes), F32), pltpu.VMEM((5, total, lanes), F32)]
    scratch += [pltpu.VMEM((5, points, lanes), F32)] * 3 + [pltpu.VMEM((points, lanes), F32)]
    scratch += [pltpu.VMEM((rows_i * 16, lanes), F32), pltpu.VMEM((8, 6 * 8, lanes), F32), pltpu.VMEM((8, 128), F32)]
    smem = pl.BlockSpec(memory_space=pltpu.SMEM)
    in_specs = [whole] * 6 + [smem] + [whole] * 7

    moved, moved_span, *sent = pl.pallas_call(
        functools.partial(stage_kernel, dims, False),
        out_shape=[shape(5, total, lanes), shape(5, total, lanes)] + parts(5),
        in_specs=in_specs,
        out_specs=[whole] * 7,
        scratch_shapes=scratch,
        compiler_params=params,
        name="first_section",
    )(state, span, span, metrics, volume, blank, wake_partner, below, above, below, above, wake, span_below, span_above)
    below2, above2, wake, span_below2, span_above2 = exchange(sent)
    grow = lambda new, old: jnp.concatenate([new, old[5:]], axis=0)
    (result,) = pl.pallas_call(
        functools.partial(stage_kernel, dims, True),
        out_shape=[shape(5, total, lanes)],
        in_specs=in_specs + [whole],
        out_specs=[whole],
        scratch_shapes=scratch,
        compiler_params=params,
        name="second_section",
    )(moved, moved_span, span, metrics, volume, blank, wake_partner, below2, above2, below, above, wake,
      grow(span_below2, span_below), grow(span_above2, span_above), state)
    return result.reshape(5, rows_i, rows_j, lanes)


def solution(mesh):
    placed = (
        P("wrap", None, "span"),
        P(None, "wrap", None, "span"),
        P("wrap", None, "span"),
        P(None, "wrap", None, "span"),
        P("wrap", None, "span"),
        P("wrap"),
        P("wrap", None, "span"),
    )
    return jax.shard_map(
        body, mesh=mesh, in_specs=placed, out_specs=P(None, "wrap", None, "span"), check_vma=False
    )
```

time: 145 us -> 53.7 us (0.37)
  the two profiles are of different devices: /device:TPU:0 before, /device:TPU:3 now
where the time goes in v1:
time: 53.7 us; the launch traced here: 53.4 us
  starting transfers between devices  22.7 us (42%)
  Pallas kernels  19.2 us (36%)
  waiting for transfers between devices  7.29 us (14%)
  local copies, waits for them, and re-layouts  4.11 us (8%)
    pallas_call x1, Pallas kernels, body(): pl.pallas_call(functools.partial(stage_kernel, dims, True), out_shape=[sh...  9.66 us
    pallas_call x1, Pallas kernels, body(): pl.pallas_call(functools.partial(stage_kernel, dims, False), out_shape=[s...  9.07 us
    ppermute x2, starting transfers between devices, exchange(): lax.ppermute(high, 'wrap', up)  6.68 us
    ppermute x2, starting transfers between devices, exchange(): lax.ppermute(wake, 'wrap', mirror)  5.4 us
    ppermute x2, starting transfers between devices, exchange(): lax.ppermute(span_low, 'span', ring_down)  4.14 us
    unnamed x16, local copies, waits for them, and re-layouts  4.1 us
    ppermute x2, starting transfers between devices, exchange(): lax.ppermute(low, 'wrap', down)  3.84 us
    ppermute x2, waiting for transfers between devices, exchange(): lax.ppermute(low, 'wrap', down)  3.13 us
  transfers between devices with their start and end apart: 10, of which 5 were waited for; matrix products, arithmetic and copies ran while one was open for 0% of the time, Pallas kernels for 0%

profile of v1, /device:TPU:3, one launch (start us, length us, event | category | flops | bytes accessed | tf_op | source)
XLA Modules:
  0.0 53.4 jit_solution(1191776093979955074)
XLA Ops:
  0.0 1.3 %copy-done = f32[9,16,16,128]{3,2,1,0:T(8,128)S(1)} copy-done((f32[9,16,16,128]{3,2,1,0:T(8,128)S(1)}, f32[9,16,16,128]{3,2,1,0:T(8,128)}, u32[]{:S(2)}) %copy-start) | copy-done | bytes 1179672
  1.3 1.0 %copy-done.4 = f32[3,16,16,128]{3,2,1,0:T(8,128)S(1)} copy-done((f32[3,16,16,128]{3,2,1,0:T(8,128)S(1)}, f32[3,16,16,128]{3,2,1,0:T(8,128)}, u32[]{:S(2)}) %copy-start.4) | copy-done | bytes 393240
  2.3 0.9 %copy-done.5 = f32[16,16,128]{2,1,0:T(8,128)S(1)} copy-done((f32[16,16,128]{2,1,0:T(8,128)S(1)}, f32[16,16,128]{2,1,0:T(8,128)}, u32[]{:S(2)}) %copy-start.5) | copy-done | bytes 131096
  3.2 0.9 %copy-done.6 = f32[16,16,128]{2,1,0:T(8,128)S(1)} copy-done((f32[16,16,128]{2,1,0:T(8,128)S(1)}, f32[16,16,128]{2,1,0:T(8,128)}, u32[]{:S(2)}) %copy-start.6) | copy-done | bytes 131096
  4.1 0.4 prepare.1
  4.5 3.7 %collective-permute-start = (f32[8,48,128]{2,1,0:T(8,128)S(1)}, f32[8,48,128]{2,1,0:T(8,128)S(1)}, u32[]{:S(2)}, u32[]{:S(2)}) collective-permute-start(f32[8,48,128]{2,1,0:T(8,128)S(1)} %get-tuple-element.21), channel_id=1, source_target_pairs={{0,4},{4,8},{8,12},{12,16},{16,20},{20,24},{24,28},{1,5},{5,9},{9,... | collective-permute-start | bytes 589832 | tf_op jit(solution)/shard_map/ppermute | solution.py:386
  8.2 1.9 %collective-permute-start.1 = (f32[8,48,128]{2,1,0:T(8,128)S(1)}, f32[8,48,128]{2,1,0:T(8,128)S(1)}, u32[]{:S(2)}, u32[]{:S(2)}) collective-permute-start(f32[8,48,128]{2,1,0:T(8,128)S(1)} %get-tuple-element.22), channel_id=1, source_target_pairs={{4,0},{8,4},{12,8},{16,12},{20,16},{24,20},{28,24},{5,1},{9,5},{13... | collective-permute-start | bytes 589832 | tf_op jit(solution)/shard_map/ppermute | solution.py:386
  10.2 2.7 %collective-permute-start.2 = (f32[256,128]{1,0:T(8,128)S(1)}, f32[256,128]{1,0:T(8,128)S(1)}, u32[]{:S(2)}, u32[]{:S(2)}) collective-permute-start(f32[256,128]{1,0:T(8,128)S(1)} %get-tuple-element.23), channel_id=1, source_target_pairs={{0,28},{4,24},{8,20},{12,16},{16,12},{20,8},{24,4},{28,0},{1,29},{... | collective-permute-start | bytes 393224 | tf_op jit(solution)/shard_map/ppermute | solution.py:386
  12.8 1.3 %collective-permute-start.3 = (f32[8,8,128]{2,1,0:T(8,128)S(1)}, f32[8,8,128]{2,1,0:T(8,128)S(1)}, u32[]{:S(2)}, u32[]{:S(2)}) collective-permute-start(f32[8,8,128]{2,1,0:T(8,128)S(1)} %get-tuple-element.24), channel_id=1, source_target_pairs={{0,1},{1,2},{2,3},{3,0},{4,5},{5,6},{6,7},{7,4},{8,9},{9,10},{10,1... | collective-permute-start | bytes 98312 | tf_op jit(solution)/shard_map/ppermute | solution.py:387
  14.1 2.0 %collective-permute-start.4 = (f32[8,8,128]{2,1,0:T(8,128)S(1)}, f32[8,8,128]{2,1,0:T(8,128)S(1)}, u32[]{:S(2)}, u32[]{:S(2)}) collective-permute-start(f32[8,8,128]{2,1,0:T(8,128)S(1)} %get-tuple-element.25), channel_id=1, source_target_pairs={{1,0},{2,1},{3,2},{0,3},{5,4},{6,5},{7,6},{4,7},{9,8},{10,9},{11,1... | collective-permute-start | bytes 98312 | tf_op jit(solution)/shard_map/ppermute | solution.py:387
  16.2 1.3 %collective-permute-done.3.refs_12_ = f32[8,8,128]{2,1,0:T(8,128)S(1)} collective-permute-done((f32[8,8,128]{2,1,0:T(8,128)S(1)}, f32[8,8,128]{2,1,0:T(8,128)S(1)}, u32[]{:S(2)}, u32[]{:S(2)}) %collective-permute-start.3) | collective-permute-done | bytes 32800 | tf_op jit(solution)/shard_map/ppermute | solution.py:387
  17.5 0.2 collective-permute-done.4.refs_13_
  17.7 1.2 %collective-permute-done.2.refs_11_ = f32[256,128]{1,0:T(8,128)S(1)} collective-permute-done((f32[256,128]{1,0:T(8,128)S(1)}, f32[256,128]{1,0:T(8,128)S(1)}, u32[]{:S(2)}, u32[]{:S(2)}) %collective-permute-start.2) | collective-permute-done | bytes 131104 | tf_op jit(solution)/shard_map/ppermute | solution.py:386
  18.9 0.0 collective-permute-done.refs_7_.refs_9_
  18.9 0.0 collective-permute-done.1.refs_8_.refs_10_
  19.0 9.1 %first_section.1 = (f32[5,256,128]{2,1,0:T(8,128)S(1)}, f32[5,256,128]{2,1,0:T(8,128)S(1)}, f32[5,48,128]{2,1,0:T(8,128)S(1)}, f32[5,48,128]{2,1,0:T(8,128)S(1)}...) custom-call(f32[5,256,128]{2,1,0:T(8,128)S(1)} %get-tuple-element.19.refs_0_.refs_14_, ...), custom_call_target="tpu_custom_call" | custom-call | tf_op jit(solution)/shard_map/first_section/pallas_call | solution.py:406
  28.0 1.3 %collective-permute-start.8 = (f32[5,8,128]{2,1,0:T(8,128)S(1)}, f32[5,8,128]{2,1,0:T(8,128)S(1)}, u32[]{:S(2)}, u32[]{:S(2)}) collective-permute-start(f32[5,8,128]{2,1,0:T(8,128)S(1)} %get-tuple-element.31), channel_id=1, source_target_pairs={{0,1},{1,2},{2,3},{3,0},{4,5},{5,6},{6,7},{7,4},{8,9},{9,10},{10,1... | collective-permute-start | bytes 61448 | tf_op jit(solution)/shard_map/ppermute | solution.py:387
  29.4 2.1 %collective-permute-start.9 = (f32[5,8,128]{2,1,0:T(8,128)S(1)}, f32[5,8,128]{2,1,0:T(8,128)S(1)}, u32[]{:S(2)}, u32[]{:S(2)}) collective-permute-start(f32[5,8,128]{2,1,0:T(8,128)S(1)} %get-tuple-element.32), channel_id=1, source_target_pairs={{1,0},{2,1},{3,2},{0,3},{5,4},{6,5},{7,6},{4,7},{9,8},{10,9},{11,1... | collective-permute-start | bytes 61448 | tf_op jit(solution)/shard_map/ppermute | solution.py:387
  31.5 3.0 %collective-permute-start.5 = (f32[5,48,128]{2,1,0:T(8,128)S(1)}, f32[5,48,128]{2,1,0:T(8,128)S(1)}, u32[]{:S(2)}, u32[]{:S(2)}) collective-permute-start(f32[5,48,128]{2,1,0:T(8,128)S(1)} %get-tuple-element.28), channel_id=1, source_target_pairs={{0,4},{4,8},{8,12},{12,16},{16,20},{20,24},{24,28},{1,5},{5,9},{9,... | collective-permute-start | bytes 368648 | tf_op jit(solution)/shard_map/ppermute | solution.py:386
  34.5 1.9 %collective-permute-start.6 = (f32[5,48,128]{2,1,0:T(8,128)S(1)}, f32[5,48,128]{2,1,0:T(8,128)S(1)}, u32[]{:S(2)}, u32[]{:S(2)}) collective-permute-start(f32[5,48,128]{2,1,0:T(8,128)S(1)} %get-tuple-element.29), channel_id=1, source_target_pairs={{4,0},{8,4},{12,8},{16,12},{20,16},{24,20},{28,24},{5,1},{9,5},{13... | collective-permute-start | bytes 368648 | tf_op jit(solution)/shard_map/ppermute | solution.py:386
  36.4 2.7 %collective-permute-start.7 = (f32[256,128]{1,0:T(8,128)S(1)}, f32[256,128]{1,0:T(8,128)S(1)}, u32[]{:S(2)}, u32[]{:S(2)}) collective-permute-start(f32[256,128]{1,0:T(8,128)S(1)} %get-tuple-element.30), channel_id=1, source_target_pairs={{0,28},{4,24},{8,20},{12,16},{16,12},{20,8},{24,4},{28,0},{1,29},{... | collective-permute-start | bytes 393224 | tf_op jit(solution)/shard_map/ppermute | solution.py:386
  39.2 3.1 %collective-permute-done.6.refs_8_ = f32[5,48,128]{2,1,0:T(8,128)S(1)} collective-permute-done((f32[5,48,128]{2,1,0:T(8,128)S(1)}, f32[5,48,128]{2,1,0:T(8,128)S(1)}, u32[]{:S(2)}, u32[]{:S(2)}) %collective-permute-start.6) | collective-permute-done | bytes 122912 | tf_op jit(solution)/shard_map/ppermute | solution.py:386
  42.3 1.4 %collective-permute-done.7.refs_11_ = f32[256,128]{1,0:T(8,128)S(1)} collective-permute-done((f32[256,128]{1,0:T(8,128)S(1)}, f32[256,128]{1,0:T(8,128)S(1)}, u32[]{:S(2)}, u32[]{:S(2)}) %collective-permute-start.7) | collective-permute-done | bytes 131104 | tf_op jit(solution)/shard_map/ppermute | solution.py:386
  43.7 9.7 %second_section.1 = f32[5,256,128]{2,1,0:T(8,128)} custom-call(f32[5,256,128]{2,1,0:T(8,128)S(1)} %get-tuple-element.26.refs_0_, f32[5,256,128]{2,1,0:T(8,128)S(1)} %get-tuple-element.27.refs_1_, f32[8,256,128]{2,1,0:T(8,128)S(1)} %get-tuple-element.20.refs_1_.refs_2_, f32[9,256,128]{2,1,0:T(8,128)S(1)} %bitcast.9, f32[256,128]{1,0:T(8,128)S(1)} %bitcast.11, ...), custom_call_target="tpu_custom_call" | custom-call | tf_op jit(solution)/shard_map/second_section/pallas_call | solution.py:417
  (19 shorter events, 0.0 us)
Async XLA Ops:
  0.0 18.9 %copy-start.7 = (s32[16]{0:T(128)S(1)}, s32[16]{0:T(128)}, u32[]{:S(2)}) copy-start(s32[16]{0:T(128)} %refs_6_.3) | copy-start | bytes 196
  0.0 1.3 %copy-start = (f32[9,16,16,128]{3,2,1,0:T(8,128)S(1)}, f32[9,16,16,128]{3,2,1,0:T(8,128)}, u32[]{:S(2)}) copy-start(f32[9,16,16,128]{3,2,1,0:T(8,128)} %param.10) | copy-start | bytes 3538948
  1.3 1.0 %copy-start.4 = (f32[3,16,16,128]{3,2,1,0:T(8,128)S(1)}, f32[3,16,16,128]{3,2,1,0:T(8,128)}, u32[]{:S(2)}) copy-start(f32[3,16,16,128]{3,2,1,0:T(8,128)} %param.8) | copy-start | bytes 1179652
  2.3 0.9 %copy-start.5 = (f32[16,16,128]{2,1,0:T(8,128)S(1)}, f32[16,16,128]{2,1,0:T(8,128)}, u32[]{:S(2)}) copy-start(f32[16,16,128]{2,1,0:T(8,128)} %param.7) | copy-start | bytes 393220
  3.2 0.9 %copy-start.6 = (f32[16,16,128]{2,1,0:T(8,128)S(1)}, f32[16,16,128]{2,1,0:T(8,128)}, u32[]{:S(2)}) copy-start(f32[16,16,128]{2,1,0:T(8,128)} %param.9) | copy-start | bytes 393220
  4.1 14.8 %copy-start.1 = (f32[9,16,16,128]{3,2,1,0:T(8,128)S(1)}, f32[9,16,16,128]{3,2,1,0:T(8,128)}, u32[]{:S(2)}) copy-start(f32[9,16,16,128]{3,2,1,0:T(8,128)} %param.10) | copy-start | bytes 3538948
  4.1 14.8 %copy-start.2 = (f32[16,16,128]{2,1,0:T(8,128)S(1)}, f32[16,16,128]{2,1,0:T(8,128)}, u32[]{:S(2)}) copy-start(f32[16,16,128]{2,1,0:T(8,128)} %param.11) | copy-start | bytes 393220
  4.1 14.9 %copy-start.3 = (s32[16,16,128]{2,1,0:T(8,128)S(1)}, s32[16,16,128]{2,1,0:T(8,128)}, u32[]{:S(2)}) copy-start(s32[16,16,128]{2,1,0:T(8,128)} %param.13) | copy-start | bytes 393220
  4.5 14.4 %collective-permute-start = (f32[8,48,128]{2,1,0:T(8,128)S(1)}, f32[8,48,128]{2,1,0:T(8,128)S(1)}, u32[]{:S(2)}, u32[]{:S(2)}) collective-permute-start(f32[8,48,128]{2,1,0:T(8,128)S(1)} %get-tuple-element.21), channel_id=1, source_target_pairs={{0,4},{4,8},{8,12},{12,16},{16,20},{20,24},{24,28},{1,5},{5,9},{9,... | collective-permute-start | bytes 589832 | tf_op jit(solution)/shard_map/ppermute | solution.py:386
  8.2 10.7 %collective-permute-start.1 = (f32[8,48,128]{2,1,0:T(8,128)S(1)}, f32[8,48,128]{2,1,0:T(8,128)S(1)}, u32[]{:S(2)}, u32[]{:S(2)}) collective-permute-start(f32[8,48,128]{2,1,0:T(8,128)S(1)} %get-tuple-element.22), channel_id=1, source_target_pairs={{4,0},{8,4},{12,8},{16,12},{20,16},{24,20},{28,24},{5,1},{9,5},{13... | collective-permute-start | bytes 589832 | tf_op jit(solution)/shard_map/ppermute | solution.py:386
  10.2 8.8 %collective-permute-start.2 = (f32[256,128]{1,0:T(8,128)S(1)}, f32[256,128]{1,0:T(8,128)S(1)}, u32[]{:S(2)}, u32[]{:S(2)}) collective-permute-start(f32[256,128]{1,0:T(8,128)S(1)} %get-tuple-element.23), channel_id=1, source_target_pairs={{0,28},{4,24},{8,20},{12,16},{16,12},{20,8},{24,4},{28,0},{1,29},{... | collective-permute-start | bytes 393224 | tf_op jit(solution)/shard_map/ppermute | solution.py:386
  12.8 4.7 %collective-permute-start.3 = (f32[8,8,128]{2,1,0:T(8,128)S(1)}, f32[8,8,128]{2,1,0:T(8,128)S(1)}, u32[]{:S(2)}, u32[]{:S(2)}) collective-permute-start(f32[8,8,128]{2,1,0:T(8,128)S(1)} %get-tuple-element.24), channel_id=1, source_target_pairs={{0,1},{1,2},{2,3},{3,0},{4,5},{5,6},{6,7},{7,4},{8,9},{9,10},{10,1... | collective-permute-start | bytes 98312 | tf_op jit(solution)/shard_map/ppermute | solution.py:387
  14.1 3.5 %collective-permute-start.4 = (f32[8,8,128]{2,1,0:T(8,128)S(1)}, f32[8,8,128]{2,1,0:T(8,128)S(1)}, u32[]{:S(2)}, u32[]{:S(2)}) collective-permute-start(f32[8,8,128]{2,1,0:T(8,128)S(1)} %get-tuple-element.25), channel_id=1, source_target_pairs={{1,0},{2,1},{3,2},{0,3},{5,4},{6,5},{7,6},{4,7},{9,8},{10,9},{11,1... | collective-permute-start | bytes 98312 | tf_op jit(solution)/shard_map/ppermute | solution.py:387
  28.0 11.1 %collective-permute-start.8 = (f32[5,8,128]{2,1,0:T(8,128)S(1)}, f32[5,8,128]{2,1,0:T(8,128)S(1)}, u32[]{:S(2)}, u32[]{:S(2)}) collective-permute-start(f32[5,8,128]{2,1,0:T(8,128)S(1)} %get-tuple-element.31), channel_id=1, source_target_pairs={{0,1},{1,2},{2,3},{3,0},{4,5},{5,6},{6,7},{7,4},{8,9},{9,10},{10,1... | collective-permute-start | bytes 61448 | tf_op jit(solution)/shard_map/ppermute | solution.py:387
  29.4 9.8 %collective-permute-start.9 = (f32[5,8,128]{2,1,0:T(8,128)S(1)}, f32[5,8,128]{2,1,0:T(8,128)S(1)}, u32[]{:S(2)}, u32[]{:S(2)}) collective-permute-start(f32[5,8,128]{2,1,0:T(8,128)S(1)} %get-tuple-element.32), channel_id=1, source_target_pairs={{1,0},{2,1},{3,2},{0,3},{5,4},{6,5},{7,6},{4,7},{9,8},{10,9},{11,1... | collective-permute-start | bytes 61448 | tf_op jit(solution)/shard_map/ppermute | solution.py:387
  31.5 7.7 %collective-permute-start.5 = (f32[5,48,128]{2,1,0:T(8,128)S(1)}, f32[5,48,128]{2,1,0:T(8,128)S(1)}, u32[]{:S(2)}, u32[]{:S(2)}) collective-permute-start(f32[5,48,128]{2,1,0:T(8,128)S(1)} %get-tuple-element.28), channel_id=1, source_target_pairs={{0,4},{4,8},{8,12},{12,16},{16,20},{20,24},{24,28},{1,5},{5,9},{9,... | collective-permute-start | bytes 368648 | tf_op jit(solution)/shard_map/ppermute | solution.py:386
  34.5 7.8 %collective-permute-start.6 = (f32[5,48,128]{2,1,0:T(8,128)S(1)}, f32[5,48,128]{2,1,0:T(8,128)S(1)}, u32[]{:S(2)}, u32[]{:S(2)}) collective-permute-start(f32[5,48,128]{2,1,0:T(8,128)S(1)} %get-tuple-element.29), channel_id=1, source_target_pairs={{4,0},{8,4},{12,8},{16,12},{20,16},{24,20},{28,24},{5,1},{9,5},{13... | collective-permute-start | bytes 368648 | tf_op jit(solution)/shard_map/ppermute | solution.py:386
  36.4 7.3 %collective-permute-start.7 = (f32[256,128]{1,0:T(8,128)S(1)}, f32[256,128]{1,0:T(8,128)S(1)}, u32[]{:S(2)}, u32[]{:S(2)}) collective-permute-start(f32[256,128]{1,0:T(8,128)S(1)} %get-tuple-element.30), channel_id=1, source_target_pairs={{0,28},{4,24},{8,20},{12,16},{16,12},{20,8},{24,4},{28,0},{1,29},{... | collective-permute-start | bytes 393224 | tf_op jit(solution)/shard_map/ppermute | solution.py:386

commit v2 on v1

v2 whole, which is shorter than its diff:
```python
import functools

import jax
import jax.numpy as jnp
from jax import lax
from jax.experimental import pallas as pl
from jax.experimental.pallas import tpu as pltpu
from jax.sharding import PartitionSpec as P

epsilon = 1e-06
viscosity = 0.8
conduction = 1.0
time_step = 0.05
H = 3
F32 = jnp.float32


def primitives(state):
    rho, m0, m1, m2, energy = state
    inverse = 1.0 / rho
    velocity = (m0 * inverse, m1 * inverse, m2 * inverse)
    speed_sq = velocity[0] * velocity[0] + velocity[1] * velocity[1] + velocity[2] * velocity[2]
    pressure = 0.4 * (energy - 0.5 * rho * speed_sq)
    ratio = pressure * inverse
    heat = 0.5 * speed_sq + conduction * ratio
    return velocity, pressure, energy + pressure, 1.4 * ratio, heat


def point_fluxes(state, prims, row):
    rho, m0, m1, m2, _ = state
    (u0, u1, u2), pressure, enthalpy, sound_sq, _ = prims
    x0, x1, x2 = row
    contra = x0 * u0 + x1 * u1 + x2 * u2
    metric_sq = x0 * x0 + x1 * x1 + x2 * x2
    square = sound_sq * metric_sq
    speed = jnp.abs(contra) + square * lax.rsqrt(jnp.maximum(square, 1e-30))
    fluxes = (
        rho * contra,
        m0 * contra + x0 * pressure,
        m1 * contra + x1 * pressure,
        m2 * contra + x2 * pressure,
        enthalpy * contra,
    )
    waves = [speed * one for one in state]
    plus = [a + b for a, b in zip(fluxes, waves)]
    minus = [a - b for a, b in zip(fluxes, waves)]
    return plus, minus, metric_sq * (24.0 * viscosity * 0.5)


class Split:
    def __init__(self, load):
        self.load, self.memo = load, {}

    def get(self, name, n):
        if (name, n) not in self.memo:
            self.memo[name, n] = getattr(self, "make_" + name)(n)
        return self.memo[name, n]

    def make_v(self, n):
        return self.load(n)

    def make_d(self, n):
        return self.get("v", n + 1) - self.get("v", n)

    def make_e(self, n):
        return self.get("d", n) - self.get("d", n - 1)

    def make_t(self, n):
        return self.get("e", n + 1) - self.get("e", n)

    def make_t2(self, n):
        return self.get("t", n) + self.get("t", n)

    def make_smooth(self, n):
        high, low, bend = self.get("d", n), self.get("d", n - 1), self.get("e", n)
        twice = bend + bend
        a, b = high * twice, low * twice
        centre = (a - b) * (2.0 / 3.0) + (high * low + 16.0 * epsilon / 3.0)
        return centre + a, centre, centre - b

    def correction(self, outer, middle, inner, near, far):
        left = middle * pl.reciprocal(outer, approx=True)
        right = middle * pl.reciprocal(inner, approx=True)
        weight_left = left * left * (1.0 / 3.0)
        weight_right = right * right
        total = (weight_left + weight_right) + 2.0
        return (weight_left * near + weight_right * far) * pl.reciprocal(total, approx=True)


def sweep(load_plus, load_minus, load_diffused, load_metric, store, first, last, open_low=False, open_high=False):
    plus, minus = Split(load_plus), Split(load_minus)
    central, diffused, metric = {}, {}, {}

    def flux_centre(n):
        if n not in central:
            both = plus.get("v", n) + minus.get("v", n)
            central[n] = 6.0 * both - (plus.get("e", n) + minus.get("e", n))
        return central[n]

    def cached(table, load, n):
        if n not in table:
            table[n] = load(n)
        return table[n]

    before = None
    for n in range(first, last + 1):
        up = plus.correction(
            plus.get("smooth", n - 1)[0],
            plus.get("smooth", n)[1],
            plus.get("smooth", n + 1)[2],
            plus.get("t2", n - 1),
            plus.get("t", n),
        )
        down = minus.correction(
            minus.get("smooth", n + 2)[2],
            minus.get("smooth", n + 1)[1],
            minus.get("smooth", n)[0],
            minus.get("t2", n + 1),
            minus.get("t", n),
        )
        correction = down - up
        flux = flux_centre(n) + flux_centre(n + 1) + (plus.get("t", n) - minus.get("t", n))
        flux = flux + (correction + correction)
        face_metric = cached(metric, load_metric, n) + cached(metric, load_metric, n + 1)
        jump = cached(diffused, load_diffused, n + 1) - cached(diffused, load_diffused, n)
        net = face_metric * jump - flux
        if before is not None:
            store(n, net - before)
        elif open_low:
            store(n, net)
        before = net
    if open_high:
        store(last + 1, -before)


def put(refs, rows, plus, minus, metric=None):
    plus_ref, minus_ref, metric_ref = refs
    for f in range(5):
        plus_ref[f, rows, :] = plus[f]
        minus_ref[f, rows, :] = minus[f]
    if metric is not None:
        metric_ref[rows, :] = metric


def put_diffused(ref, rows, prims):
    for m in range(3):
        ref[1 + m, rows, :] = prims[0][m]
    ref[4, rows, :] = prims[4]


def aligned(start, count):
    return pl.ds(pl.multiple_of(start, 8), count)


def unit(which, m, value):
    return value + 1.0 if which == m else value


def to_span(value, store, height):
    for half in range(2):
        turned = value[half * 128 : (half + 1) * 128].T
        for q in range(4):
            store(q * 2 + half, turned[q * height : (q + 1) * height])


def send_parts(state_ref, span_ref, fields, outs, dims):
    rows_i, height = dims
    total = rows_i * rows_i
    core_ref, chip_ref, wake_ref, span_low_ref, span_high_ref = outs
    even = lax.rem(lax.axis_index("wrap"), 2) == 0
    edge = H * rows_i
    to_core, to_chip = jnp.where(even, total - edge, 0), jnp.where(even, 0, total - edge)
    for f in range(5):
        core_ref[f] = state_ref[f, aligned(to_core, edge), :]
        chip_ref[f] = state_ref[f, aligned(to_chip, edge), :]
        for r in range(H):
            wake_ref[pl.ds(f * H + r, rows_i, stride=16), :] = state_ref[f, pl.ds(r + 1, rows_i, stride=rows_i), :]
    for f in range(fields):
        for r in range(H):
            span_low_ref[f, 2 * r : 2 * r + 2, :] = span_ref[f, r * 8 : r * 8 + 2, :]
            top = (height - H + r) * 8
            span_high_ref[f, 2 * r : 2 * r + 2, :] = span_ref[f, top + 6 : top + 8, :]


def prepare_kernel(dims, rho_hbm, vel_hbm, pre_hbm, met_hbm, state_ref, span_ref, met_ref, *refs):
    outs, (rho_ref, vel_ref, pre_ref, sems) = refs[:5], refs[5:]
    rows_i, height = dims
    total = rows_i * rows_i
    pairs = [(rho_hbm, rho_ref), (vel_hbm, vel_ref), (pre_hbm, pre_ref)]
    pairs += [(met_hbm.at[pl.ds(3 * d, 3)], met_ref.at[pl.ds(3 * d, 3)]) for d in (2, 0, 1)]
    copies = [pltpu.make_async_copy(a, b, sems.at[n]) for n, (a, b) in enumerate(pairs)]
    for copy in copies:
        copy.start()
    for copy in copies[:3]:
        copy.wait()
    rho, pressure = rho_ref[...], pre_ref[...]
    u = [vel_ref[m] for m in range(3)]
    speed_sq = u[0] * u[0] + u[1] * u[1] + u[2] * u[2]
    state_ref[0] = rho
    for m in range(3):
        state_ref[1 + m] = rho * u[m]
    state_ref[4] = pressure * (1.0 / 0.4) + 0.5 * rho * speed_sq
    core_ref, chip_ref = outs[:2]
    for f in range(8):
        if f == 5:
            copies[3].wait()
        value = state_ref[f] if f < 5 else met_ref[6 + f - 5]

        def store(start, block, f=f):
            span_ref[f, pl.ds(start, height, stride=8), :] = block

        to_span(value, store, height)
    send_parts(state_ref, span_ref, 8, outs, dims)
    copies[4].wait()
    even = lax.rem(lax.axis_index("wrap"), 2) == 0
    edge = H * rows_i
    to_core, to_chip = jnp.where(even, total - edge, 0), jnp.where(even, 0, total - edge)
    for m in range(3):
        core_ref[5 + m] = met_ref[m, aligned(to_core, edge), :]
        chip_ref[5 + m] = met_ref[m, aligned(to_chip, edge), :]
    copies[5].wait()


def early_kernel(dims, state_ref, span_ref, span_met_ref, met_ref, acc_ref, plus_i, minus_i, metric_i, plus_j, minus_j,
                 metric_j, diffused_ref, plus_k, minus_k, metric_k, diffused_k):
    rows_i, height = dims
    diffused_ref[0] = jnp.zeros(diffused_ref.shape[1:], F32)
    diffused_k[0] = jnp.zeros(diffused_k.shape[1:], F32)

    def planes(n, carry):
        rows = aligned(n * rows_i, rows_i)
        state = [state_ref[f, rows, :] for f in range(5)]
        prims = primitives(state)
        put_diffused(diffused_ref, rows, prims)
        put((plus_i, minus_i, metric_i), rows,
            *point_fluxes(state, prims, [unit(0, m, met_ref[m, rows, :]) for m in range(3)]))
        put((plus_j, minus_j, metric_j), rows,
            *point_fluxes(state, prims, [unit(1, m, met_ref[3 + m, rows, :]) for m in range(3)]))
        return carry

    lax.fori_loop(0, rows_i, planes, 0, unroll=2)

    def spans(n, carry):
        rows = aligned(n * 16, 16)
        state = [span_ref[f, rows, :] for f in range(5)]
        prims = primitives(state)
        put_diffused(diffused_k, rows, prims)
        put((plus_k, minus_k, metric_k), rows,
            *point_fluxes(state, prims, [unit(2, m, span_met_ref[5 + m, rows, :]) for m in range(3)]))
        return carry

    lax.fori_loop(0, height // 2, spans, 0, unroll=2)

    def normal(step, carry):
        f, tile = step // 2, step % 2

        def rows(n):
            return pl.ds(tile * 8 * rows_i + min(n, rows_i - 1), 8, stride=rows_i)

        def store(n, value):
            acc_ref[f, rows(n), :] = value

        for n in range(2):
            store(n, jnp.zeros((8, 128), F32))
        sweep(lambda n: plus_j[f, rows(n), :], lambda n: minus_j[f, rows(n), :], lambda n: diffused_ref[f, rows(n), :],
              lambda n: metric_j[rows(n), :], store, 2, rows_i - 1, open_low=True)
        return carry

    lax.fori_loop(0, 10, normal, 0)


def span_kernel(dims, span_ref, span_met_ref, span_low_ref, span_high_ref, met_low_ref, met_high_ref,
                plus_k, minus_k, metric_k, diffused_k, out_ref,
                acc_ref, halo_plus, halo_minus, halo_metric, halo_diffused, pad_ref):
    rows_i, height = dims
    sublane = lax.broadcasted_iota(jnp.int32, (8, 128), 0)
    halo_diffused[0] = jnp.zeros(halo_diffused.shape[1:], F32)
    for r in range(H):
        for f in range(8):
            low, high = (span_low_ref, span_high_ref) if f < 5 else (met_low_ref, met_high_ref)
            pad_ref[f, r * 8 : r * 8 + 2, :] = low[f, 2 * r : 2 * r + 2, :]
            pad_ref[f, (H + r) * 8 + 6 : (H + r) * 8 + 8, :] = high[f, 2 * r : 2 * r + 2, :]
    for r in range(2 * H):
        rows = slice(r * 8, r * 8 + 8)
        values = []
        for f in range(8):
            ref = span_ref if f < 5 else span_met_ref
            if r < H:
                own = pltpu.roll(ref[f, (height - H + r) * 8 : (height - H + r) * 8 + 8, :], 2, 0)
                values.append(jnp.where(sublane < 2, pad_ref[f, rows, :], own))
            else:
                own = pltpu.roll(ref[f, (r - H) * 8 : (r - H) * 8 + 8, :], 6, 0)
                values.append(jnp.where(sublane >= 6, pad_ref[f, rows, :], own))
        prims = primitives(values[:5])
        put_diffused(halo_diffused, rows, prims)
        put((halo_plus, halo_minus, halo_metric), rows,
            *point_fluxes(values[:5], prims, [unit(2, m, values[5 + m]) for m in range(3)]))

    def sweep_span(f, carry):
        def loader(ref, halo, lead):
            def load(n):
                if 0 <= n < height:
                    return ref[lead + (slice(n * 8, n * 8 + 8),)]
                r = n + H if n < 0 else n - height + H
                return halo[lead + (slice(r * 8, r * 8 + 8),)]

            return load

        def store(n, value):
            acc_ref[f, n * 8 : n * 8 + 8, :] = value

        sweep(loader(plus_k, halo_plus, (f,)), loader(minus_k, halo_minus, (f,)), loader(diffused_k, halo_diffused, (f,)),
              loader(metric_k, halo_metric, ()), store, -1, height - 1)
        return carry

    lax.fori_loop(0, 5, sweep_span, 0)
    for f in range(5):
        for half in range(2):
            parts = [acc_ref[f, pl.ds(q * 2 + half, height, stride=8), :] for q in range(4)]
            out_ref[f, half * 128 : (half + 1) * 128, :] = jnp.concatenate(parts, axis=0).T


def late_kernel(dims, final, *refs):
    rows_i, height = dims
    total = rows_i * rows_i
    (state_ref, met_ref, vol_ref, blank_ref, partner_ref, core_ref, chip_ref, met_core_ref, met_chip_ref, wake_ref,
     normal_ref, span_acc_ref, plus_i, minus_i, metric_i, plus_j, minus_j, metric_j, diffused_ref) = refs[:19]
    refs = refs[19:]
    if final:
        start_ref, out_ref = refs[:2]
        refs = refs[2:]
    else:
        out_ref, out_span_ref = refs[:2]
        outs, refs = refs[2:7], refs[7:]
    acc_ref, halo_plus, halo_minus, halo_metric, halo_diffused, ghost_ref = refs
    position, count = lax.axis_index("wrap"), lax.axis_size("wrap")
    even = lax.rem(position, 2) == 0
    at_end = (position == 0) | (position == count - 1)
    halo_diffused[0] = jnp.zeros(halo_diffused.shape[1:], F32)

    core_rows, chip_rows = jnp.where(even, H, 0), jnp.where(even, 0, H)
    own = jnp.where(even, 0, total - rows_i)
    for r in range(H):
        rows = slice(r * rows_i, (r + 1) * rows_i)
        state = [core_ref[f, rows, :] for f in range(5)]
        prims = primitives(state)
        to = aligned((core_rows + r) * rows_i, rows_i)
        put_diffused(halo_diffused, to, prims)
        put((halo_plus, halo_minus, halo_metric), to,
            *point_fluxes(state, prims, [unit(0, m, met_core_ref[5 + m, rows, :]) for m in range(3)]))
        edge = aligned(own, rows_i)
        state = [jnp.where(at_end, state_ref[f, edge, :], chip_ref[f, rows, :]) for f in range(5)]
        row = [jnp.where(at_end, met_ref[m, edge, :], met_chip_ref[5 + m, rows, :]) for m in range(3)]
        prims = primitives(state)
        to = aligned((chip_rows + r) * rows_i, rows_i)
        put_diffused(halo_diffused, to, prims)
        put((halo_plus, halo_minus, halo_metric), to,
            *point_fluxes(state, prims, [unit(0, m, row[m]) for m in range(3)]))

    def chord(step, carry):
        f, tile = step // 2, step % 2

        def loader(ref, halo, lead):
            def load(n):
                if 0 <= n < rows_i:
                    return ref[lead + (aligned(n * rows_i + tile * 8, 8),)]
                r = n + H if n < 0 else n - rows_i + H
                return halo[lead + (aligned(r * rows_i + tile * 8, 8),)]

            return load

        def store(n, value):
            rows = aligned(n * rows_i + tile * 8, 8)
            acc_ref[f, rows, :] = value + (normal_ref[f, rows, :] + span_acc_ref[f, rows, :])

        sweep(loader(plus_i, halo_plus, (f,)), loader(minus_i, halo_minus, (f,)), loader(diffused_ref, halo_diffused, (f,)),
              loader(metric_i, halo_metric, ()), store, -1, rows_i - 1)
        return carry

    lax.fori_loop(0, 10, chord, 0)

    base = (count - 1 - position) * rows_i
    for i in range(rows_i):
        ghost_ref[i * 16 : i * 16 + 16, :] = wake_ref[aligned((partner_ref[i] - base) * 16, 16), :]
    wall = pl.ds(0, rows_i, stride=rows_i)
    for r in range(H):
        state = [ghost_ref[pl.ds(f * H + r, rows_i, stride=16), :] for f in range(5)]
        prims = primitives(state)
        to = slice(r * rows_i, (r + 1) * rows_i)
        put_diffused(halo_diffused, to, prims)
        put((halo_plus, halo_minus, halo_metric), to,
            *point_fluxes(state, prims, [unit(1, m, met_ref[3 + m, wall, :]) for m in range(3)]))

    def normal(step, carry):
        f, tile = step // 2, step % 2

        def rows(n):
            return pl.ds(tile * 8 * rows_i + n, 8, stride=rows_i)

        def loader(ref, halo, lead):
            def load(n):
                if n >= 0:
                    return ref[lead + (rows(n),)]
                return halo[lead + (aligned((-1 - n) * rows_i + tile * 8, 8),)]

            return load

        def store(n, value):
            acc_ref[f, rows(n), :] = acc_ref[f, rows(n), :] + value

        sweep(loader(plus_j, halo_plus, (f,)), loader(minus_j, halo_minus, (f,)), loader(diffused_ref, halo_diffused, (f,)),
              lambda n: metric_j[rows(max(n, 0)), :], store, -1, 1, open_high=True)
        return carry

    lax.fori_loop(0, 10, normal, 0)

    scale = (time_step / 24.0) * blank_ref[...].astype(F32) / vol_ref[...]
    for f in range(5):
        moved = state_ref[f] + scale * acc_ref[f]
        out_ref[f] = 0.5 * start_ref[f] + 0.5 * moved if final else moved
    if not final:
        for f in range(5):
            def store(start, block, f=f):
                out_span_ref[f, pl.ds(start, height, stride=8), :] = block

            to_span(out_ref[f], store, height)
        send_parts(out_ref, out_span_ref, 5, outs, dims)


def shape(*sizes):
    return jax.ShapeDtypeStruct(sizes, F32)


def exchange(sent):
    core, chip, wake, span_low, span_high = sent
    n, s = lax.axis_size("wrap"), lax.axis_size("span")
    cores = [(i, i ^ 1) for i in range(n)]
    chips = [pair for i in range(1, n - 1, 2) for pair in ((i, i + 1), (i + 1, i))]
    mirror = [(i, n - 1 - i) for i in range(n)]
    ring_up = [(i, (i + 1) % s) for i in range(s)]
    ring_down = [((i + 1) % s, i) for i in range(s)]
    return (lax.ppermute(core, "wrap", cores), lax.ppermute(chip, "wrap", chips), lax.ppermute(wake, "wrap", mirror),
            lax.ppermute(span_high, "span", ring_up), lax.ppermute(span_low, "span", ring_down))


def body(density, velocity, pressure, metrics, volume, wake_partner, iblank):
    rows_i, rows_j, lanes = density.shape
    total, height = rows_i * rows_j, lanes // 4
    dims = (rows_i, height)
    volume, blank = volume.reshape(total, lanes), iblank.reshape(total, lanes)
    whole = pl.BlockSpec(memory_space=pltpu.VMEM)
    far = pl.BlockSpec(memory_space=pltpu.HBM)
    smem = pl.BlockSpec(memory_space=pltpu.SMEM)
    params = pltpu.CompilerParams(vmem_limit_bytes=16 * 2**20)

    def call(kernel, name, ins, outs, scratch, specs=None, cost=0):
        return pl.pallas_call(
            kernel,
            out_shape=outs,
            in_specs=specs or [whole] * len(ins),
            out_specs=[whole] * len(outs),
            scratch_shapes=scratch,
            compiler_params=params,
            cost_estimate=pl.CostEstimate(flops=cost, bytes_accessed=cost // 4, transcendentals=0),
            name=name,
        )(*ins)

    def parts(fields):
        edge = H * rows_j
        return [shape(fields, edge, lanes), shape(fields, edge, lanes), shape(rows_i * 16, lanes),
                shape(fields, 8, lanes), shape(fields, 8, lanes)]

    field, span_rows, halo = shape(5, total, lanes), height * 8, 2 * H * rows_i
    state, span, met, *sent = call(
        functools.partial(prepare_kernel, dims), "prepare",
        (density.reshape(total, lanes), velocity.reshape(3, total, lanes), pressure.reshape(total, lanes),
         metrics.reshape(9, total, lanes)),
        [field, shape(8, total, lanes), shape(9, total, lanes)] + parts(8),
        [pltpu.VMEM((total, lanes), F32), pltpu.VMEM((3, total, lanes), F32), pltpu.VMEM((total, lanes), F32),
         pltpu.SemaphoreType.DMA((6,))],
        [far] * 4,
    )
    span_met = span

    def halo_scratch(rows):
        return [pltpu.VMEM((5, rows, lanes), F32), pltpu.VMEM((5, rows, lanes), F32), pltpu.VMEM((rows, lanes), F32),
                pltpu.VMEM((5, rows, lanes), F32)]

    metric_halo = None
    start = state
    for final in (False, True):
        core, chip, wake, span_low, span_high = exchange(sent)
        if metric_halo is None:
            metric_halo = core, chip, span_low, span_high
        line, span_line = shape(5, total, lanes), shape(5, span_rows, lanes)
        normal, *lines = call(
            functools.partial(early_kernel, dims), "early", (state, span, span_met, met),
            [field, line, line, shape(total, lanes), line, line, shape(total, lanes), line,
             span_line, span_line, shape(span_rows, lanes), span_line],
            [], cost=10**8,
        )
        plus_i, minus_i, metric_i, plus_j, minus_j, metric_j, diffused = lines[:7]
        (span_acc,) = call(
            functools.partial(span_kernel, dims), "span",
            (span, span_met, span_low, span_high, metric_halo[2], metric_halo[3], *lines[7:]),
            [field],
            [pltpu.VMEM((5, span_rows, lanes), F32)] + halo_scratch(2 * H * 8) + [pltpu.VMEM((8, 2 * H * 8, lanes), F32)],
            cost=10**8,
        )
        ins = (state, met, volume, blank, wake_partner, core, chip, metric_halo[0], metric_halo[1], wake, normal, span_acc,
               plus_i, minus_i, metric_i, plus_j, minus_j, metric_j, diffused)
        ins += (start,) if final else ()
        state, *rest = call(
            functools.partial(late_kernel, dims, final), "late", ins,
            [field] if final else [field, field] + parts(5),
            [pltpu.VMEM((5, total, lanes), F32)] + halo_scratch(halo) + [pltpu.VMEM((rows_i * 16, lanes), F32)],
            [whole] * 4 + [smem] + [whole] * (len(ins) - 5),
            cost=10**8,
        )
        if not final:
            span, *sent = rest
    return state.reshape(5, rows_i, rows_j, lanes)


def solution(mesh):
    placed = (
        P("wrap", None, "span"),
        P(None, "wrap", None, "span"),
        P("wrap", None, "span"),
        P(None, "wrap", None, "span"),
        P("wrap", None, "span"),
        P("wrap"),
        P("wrap", None, "span"),
    )
    return jax.shard_map(
        body, mesh=mesh, in_specs=placed, out_specs=P(None, "wrap", None, "span"), check_vma=False
    )
```

time: 53.7 us -> 41.9 us (0.78)
  the two profiles are of different devices: /device:TPU:3 before, /device:TPU:1 now
where the time goes in v2:
time: 41.9 us; the launch traced here: 41.7 us
  Pallas kernels  19.4 us (46%)
  starting transfers between devices  18 us (43%)
  local copies, waits for them, and re-layouts  4.09 us (10%)
    pallas_call x7, Pallas kernels, call(): pl.pallas_call(kernel, out_shape=outs, in_specs=specs or [whole] * len(in...  19.4 us
    ppermute x2, starting transfers between devices, exchange(): lax.ppermute(chip, 'wrap', chips)  7.97 us
    ppermute x2, starting transfers between devices, exchange(): lax.ppermute(span_low, 'span', ring_down)  4.84 us
    unnamed x14, local copies, waits for them, and re-layouts  4.09 us
    ppermute x2, starting transfers between devices, exchange(): lax.ppermute(wake, 'wrap', mirror)  3.28 us
    ppermute x2, starting transfers between devices, exchange(): lax.ppermute(span_high, 'span', ring_up)  1.8 us
  transfers between devices with their start and end apart: 10, of which 0 were waited for; matrix products, arithmetic and copies ran while one was open for 0% of the time, Pallas kernels for 23%

profile of v2, /device:TPU:1, one launch (start us, length us, event | category | flops | bytes accessed | tf_op | source)
XLA Modules:
  0.0 41.7 jit_solution(5842029827158386582)
XLA Ops:
  0.0 1.3 %copy-done = f32[9,16,16,128]{3,2,1,0:T(8,128)S(1)} copy-done((f32[9,16,16,128]{3,2,1,0:T(8,128)S(1)}, f32[9,16,16,128]{3,2,1,0:T(8,128)}, u32[]{:S(2)}) %copy-start) | copy-done | bytes 1179672
  1.3 1.0 %copy-done.3 = f32[3,16,16,128]{3,2,1,0:T(8,128)S(1)} copy-done((f32[3,16,16,128]{3,2,1,0:T(8,128)S(1)}, f32[3,16,16,128]{3,2,1,0:T(8,128)}, u32[]{:S(2)}) %copy-start.3) | copy-done | bytes 393240
  2.3 0.9 %copy-done.4 = f32[16,16,128]{2,1,0:T(8,128)S(1)} copy-done((f32[16,16,128]{2,1,0:T(8,128)S(1)}, f32[16,16,128]{2,1,0:T(8,128)}, u32[]{:S(2)}) %copy-start.4) | copy-done | bytes 131096
  3.2 0.9 %copy-done.5 = f32[16,16,128]{2,1,0:T(8,128)S(1)} copy-done((f32[16,16,128]{2,1,0:T(8,128)S(1)}, f32[16,16,128]{2,1,0:T(8,128)}, u32[]{:S(2)}) %copy-start.5) | copy-done | bytes 131096
  4.1 1.6 %prepare.1 = (f32[5,256,128]{2,1,0:T(8,128)S(1)}, f32[8,256,128]{2,1,0:T(8,128)S(1)}, f32[9,256,128]{2,1,0:T(8,128)S(1)}, f32[8,48,128]{2,1,0:T(8,128)S(1)}, f32...) custom-call(f32[256,128]{1,0:T(8,128)S(1)} %bitcast.13, ...), custom_call_target="tpu_custom_call" | custom-call | tf_op jit(solution)/shard_map/prepare/pallas_call | solution.py:457
  5.7 0.1 collective-permute-start
  5.9 4.5 %collective-permute-start.1 = (f32[8,48,128]{2,1,0:T(8,128)S(1)}, f32[8,48,128]{2,1,0:T(8,128)S(1)}, u32[]{:S(2)}, u32[]{:S(2)}) collective-permute-start(f32[8,48,128]{2,1,0:T(8,128)S(1)} %get-tuple-element.47), channel_id=1, source_target_pairs={{4,8},{8,4},{12,16},{16,12},{20,24},{24,20},{5,9},{9,5},{13,17},{1... | collective-permute-start | bytes 589832 | tf_op jit(solution)/shard_map/ppermute | solution.py:442
  10.3 1.6 %collective-permute-start.2 = (f32[256,128]{1,0:T(8,128)S(1)}, f32[256,128]{1,0:T(8,128)S(1)}, u32[]{:S(2)}, u32[]{:S(2)}) collective-permute-start(f32[256,128]{1,0:T(8,128)S(1)} %get-tuple-element.48), channel_id=1, source_target_pairs={{0,28},{4,24},{8,20},{12,16},{16,12},{20,8},{24,4},{28,0},{1,29},{... | collective-permute-start | bytes 393224 | tf_op jit(solution)/shard_map/ppermute | solution.py:442
  12.0 1.3 %collective-permute-start.3 = (f32[8,8,128]{2,1,0:T(8,128)S(1)}, f32[8,8,128]{2,1,0:T(8,128)S(1)}, u32[]{:S(2)}, u32[]{:S(2)}) collective-permute-start(f32[8,8,128]{2,1,0:T(8,128)S(1)} %get-tuple-element.51), channel_id=1, source_target_pairs={{0,1},{1,2},{2,3},{3,0},{4,5},{5,6},{6,7},{7,4},{8,9},{9,10},{10,1... | collective-permute-start | bytes 98312 | tf_op jit(solution)/shard_map/ppermute | solution.py:443
  13.3 2.0 %collective-permute-start.4 = (f32[8,8,128]{2,1,0:T(8,128)S(1)}, f32[8,8,128]{2,1,0:T(8,128)S(1)}, u32[]{:S(2)}, u32[]{:S(2)}) collective-permute-start(f32[8,8,128]{2,1,0:T(8,128)S(1)} %get-tuple-element.52), channel_id=1, source_target_pairs={{1,0},{2,1},{3,2},{0,3},{5,4},{6,5},{7,6},{4,7},{9,8},{10,9},{11,1... | collective-permute-start | bytes 98312 | tf_op jit(solution)/shard_map/ppermute | solution.py:443
  15.3 2.8 %early.2 = (f32[5,256,128]{2,1,0:T(8,128)S(1)}, f32[5,256,128]{2,1,0:T(8,128)S(1)}, f32[5,256,128]{2,1,0:T(8,128)S(1)}, f32[256,128]{1,0:T(8,128)S(1)}, f32[5,25...) custom-call(f32[5,256,128]{2,1,0:T(8,128)S(1)} %get-tuple-element.44, ...), custom_call_target="tpu_custom_call" | custom-call | flops 100000000 | bytes 25000000 | tf_op jit(solution)/shard_map/early/pallas_call | solution.py:457
  18.1 0.0 collective-permute-done.3.span_low_ref.met_low_ref
  18.1 0.0 copy-start.1
  18.2 0.0 copy-start.2
  18.2 0.0 copy-start.6
  18.2 2.0 %span.2.refs_11_ = f32[5,256,128]{2,1,0:T(8,128)S(1)} custom-call(f32[8,256,128]{2,1,0:T(8,128)S(1)} %get-tuple-element.49.span_ref.span_met_ref, f32[8,256,128]{2,1,0:T(8,128)S(1)} %get-tuple-element.49.span_ref.span_met_ref, f32[8,8,128]{2,1,0:T(8,128)S(1)} %collective-permute-done.3.span_low_ref.met_low_ref, ...), custom_call_target="tpu_custom_call" | custom-call | flops 100000000 | bytes 25000000 | tf_op jit(solution)/shard_map/span/pallas_call | solution.py:457
  20.2 3.8 %late.2 = (f32[5,256,128]{2,1,0:T(8,128)S(1)}, f32[5,256,128]{2,1,0:T(8,128)S(1)}, f32[5,48,128]{2,1,0:T(8,128)S(1)}, f32[5,48,128]{2,1,0:T(8,128)S(1)}, f32[256...) custom-call(f32[5,256,128]{2,1,0:T(8,128)S(1)} %get-tuple-element.44.state_ref.refs_0_.refs_19_, ...), custom_call_target="tpu_custom_call" | custom-call | flops 100000000 | bytes 25000000 | tf_op jit(solution)/shard_map/late/pallas_call | solution.py:457
  24.0 1.6 %collective-permute-start.7 = (f32[256,128]{1,0:T(8,128)S(1)}, f32[256,128]{1,0:T(8,128)S(1)}, u32[]{:S(2)}, u32[]{:S(2)}) collective-permute-start(f32[256,128]{1,0:T(8,128)S(1)} %get-tuple-element.67), channel_id=1, source_target_pairs={{0,28},{4,24},{8,20},{12,16},{16,12},{20,8},{24,4},{28,0},{1,29},{... | collective-permute-start | bytes 393224 | tf_op jit(solution)/shard_map/ppermute | solution.py:442
  25.7 3.5 %collective-permute-start.6 = (f32[5,48,128]{2,1,0:T(8,128)S(1)}, f32[5,48,128]{2,1,0:T(8,128)S(1)}, u32[]{:S(2)}, u32[]{:S(2)}) collective-permute-start(f32[5,48,128]{2,1,0:T(8,128)S(1)} %get-tuple-element.66), channel_id=1, source_target_pairs={{4,8},{8,4},{12,16},{16,12},{20,24},{24,20},{5,9},{9,5},{13,17},{1... | collective-permute-start | bytes 368648 | tf_op jit(solution)/shard_map/ppermute | solution.py:442
  29.2 0.5 %collective-permute-start.8 = (f32[5,8,128]{2,1,0:T(8,128)S(1)}, f32[5,8,128]{2,1,0:T(8,128)S(1)}, u32[]{:S(2)}, u32[]{:S(2)}) collective-permute-start(f32[5,8,128]{2,1,0:T(8,128)S(1)} %get-tuple-element.70), channel_id=1, source_target_pairs={{0,1},{1,2},{2,3},{3,0},{4,5},{5,6},{6,7},{7,4},{8,9},{9,10},{10,1... | collective-permute-start | bytes 61448 | tf_op jit(solution)/shard_map/ppermute | solution.py:443
  29.7 2.8 %collective-permute-start.9 = (f32[5,8,128]{2,1,0:T(8,128)S(1)}, f32[5,8,128]{2,1,0:T(8,128)S(1)}, u32[]{:S(2)}, u32[]{:S(2)}) collective-permute-start(f32[5,8,128]{2,1,0:T(8,128)S(1)} %get-tuple-element.71), channel_id=1, source_target_pairs={{1,0},{2,1},{3,2},{0,3},{5,4},{6,5},{7,6},{4,7},{9,8},{10,9},{11,1... | collective-permute-start | bytes 61448 | tf_op jit(solution)/shard_map/ppermute | solution.py:443
  32.5 2.8 %early.3 = (f32[5,256,128]{2,1,0:T(8,128)S(1)}, f32[5,256,128]{2,1,0:T(8,128)S(1)}, f32[5,256,128]{2,1,0:T(8,128)S(1)}, f32[256,128]{1,0:T(8,128)S(1)}, f32[5,25...) custom-call(f32[5,256,128]{2,1,0:T(8,128)S(1)} %get-tuple-element.64, ...), custom_call_target="tpu_custom_call" | custom-call | flops 100000000 | bytes 25000000 | tf_op jit(solution)/shard_map/early/pallas_call | solution.py:457
  35.3 2.0 %span.3.refs_11_ = f32[5,256,128]{2,1,0:T(8,128)S(1)} custom-call(f32[5,256,128]{2,1,0:T(8,128)S(1)} %get-tuple-element.68.span_ref, f32[8,256,128]{2,1,0:T(8,128)S(1)} %get-tuple-element.49.span_ref.span_met_ref, f32[5,8,128]{2,1,0:T(8,128)S(1)} %collective-permute-done.8.span_low_ref, f32[5,8,128]{2,1,0:T(8,128)S(1)} %collective-permute-done.9.span_high_ref, ...), custom_call_target="tpu_custom_call" | custom-call | flops 100000000 | bytes 25000000 | tf_op jit(solution)/shard_map/span/pallas_call | solution.py:457
  37.3 4.4 %late.3 = f32[5,256,128]{2,1,0:T(8,128)} custom-call(f32[5,256,128]{2,1,0:T(8,128)S(1)} %get-tuple-element.64.state_ref.refs_0_, f32[9,256,128]{2,1,0:T(8,128)S(1)} %get-tuple-element.45.met_ref.refs_1_, f32[256,128]{1,0:T(8,128)S(1)} %bitcast.9, s32[256,128]{1,0:T(8,128)S(1)} %bitcast.11, s32[16]{0:T(128)S(1)} %copy-done.6, ...), custom_call_target="tpu_custom_call" | custom-call | flops 100000000 | bytes 25000000 | tf_op jit(solution)/shard_map/late/pallas_call | solution.py:457
  (17 shorter events, 0.0 us)
Async XLA Ops:
  0.0 1.3 %copy-start = (f32[9,16,16,128]{3,2,1,0:T(8,128)S(1)}, f32[9,16,16,128]{3,2,1,0:T(8,128)}, u32[]{:S(2)}) copy-start(f32[9,16,16,128]{3,2,1,0:T(8,128)} %param.10) | copy-start | bytes 3538948
  1.3 1.0 %copy-start.3 = (f32[3,16,16,128]{3,2,1,0:T(8,128)S(1)}, f32[3,16,16,128]{3,2,1,0:T(8,128)}, u32[]{:S(2)}) copy-start(f32[3,16,16,128]{3,2,1,0:T(8,128)} %param.8) | copy-start | bytes 1179652
  2.3 0.9 %copy-start.4 = (f32[16,16,128]{2,1,0:T(8,128)S(1)}, f32[16,16,128]{2,1,0:T(8,128)}, u32[]{:S(2)}) copy-start(f32[16,16,128]{2,1,0:T(8,128)} %param.7) | copy-start | bytes 393220
  3.2 0.9 %copy-start.5 = (f32[16,16,128]{2,1,0:T(8,128)S(1)}, f32[16,16,128]{2,1,0:T(8,128)}, u32[]{:S(2)}) copy-start(f32[16,16,128]{2,1,0:T(8,128)} %param.9) | copy-start | bytes 393220
  5.7 14.5 %collective-permute-start = (f32[8,48,128]{2,1,0:T(8,128)S(1)}, f32[8,48,128]{2,1,0:T(8,128)S(1)}, u32[]{:S(2)}, u32[]{:S(2)}) collective-permute-start(f32[8,48,128]{2,1,0:T(8,128)S(1)} %get-tuple-element.46), channel_id=1, source_target_pairs={{0,4},{4,0},{8,12},{12,8},{16,20},{20,16},{24,28},{28,24},{1,5},{5... | collective-permute-start | bytes 589832 | tf_op jit(solution)/shard_map/ppermute | solution.py:442
  5.9 14.3 %collective-permute-start.1 = (f32[8,48,128]{2,1,0:T(8,128)S(1)}, f32[8,48,128]{2,1,0:T(8,128)S(1)}, u32[]{:S(2)}, u32[]{:S(2)}) collective-permute-start(f32[8,48,128]{2,1,0:T(8,128)S(1)} %get-tuple-element.47), channel_id=1, source_target_pairs={{4,8},{8,4},{12,16},{16,12},{20,24},{24,20},{5,9},{9,5},{13,17},{1... | collective-permute-start | bytes 589832 | tf_op jit(solution)/shard_map/ppermute | solution.py:442
  10.3 9.8 %collective-permute-start.2 = (f32[256,128]{1,0:T(8,128)S(1)}, f32[256,128]{1,0:T(8,128)S(1)}, u32[]{:S(2)}, u32[]{:S(2)}) collective-permute-start(f32[256,128]{1,0:T(8,128)S(1)} %get-tuple-element.48), channel_id=1, source_target_pairs={{0,28},{4,24},{8,20},{12,16},{16,12},{20,8},{24,4},{28,0},{1,29},{... | collective-permute-start | bytes 393224 | tf_op jit(solution)/shard_map/ppermute | solution.py:442
  12.0 6.2 %collective-permute-start.3 = (f32[8,8,128]{2,1,0:T(8,128)S(1)}, f32[8,8,128]{2,1,0:T(8,128)S(1)}, u32[]{:S(2)}, u32[]{:S(2)}) collective-permute-start(f32[8,8,128]{2,1,0:T(8,128)S(1)} %get-tuple-element.51), channel_id=1, source_target_pairs={{0,1},{1,2},{2,3},{3,0},{4,5},{5,6},{6,7},{7,4},{8,9},{9,10},{10,1... | collective-permute-start | bytes 98312 | tf_op jit(solution)/shard_map/ppermute | solution.py:443
  13.3 4.9 %collective-permute-start.4 = (f32[8,8,128]{2,1,0:T(8,128)S(1)}, f32[8,8,128]{2,1,0:T(8,128)S(1)}, u32[]{:S(2)}, u32[]{:S(2)}) collective-permute-start(f32[8,8,128]{2,1,0:T(8,128)S(1)} %get-tuple-element.52), channel_id=1, source_target_pairs={{1,0},{2,1},{3,2},{0,3},{5,4},{6,5},{7,6},{4,7},{9,8},{10,9},{11,1... | collective-permute-start | bytes 98312 | tf_op jit(solution)/shard_map/ppermute | solution.py:443
  18.1 2.1 %copy-start.1 = (f32[16,16,128]{2,1,0:T(8,128)S(1)}, f32[16,16,128]{2,1,0:T(8,128)}, u32[]{:S(2)}) copy-start(f32[16,16,128]{2,1,0:T(8,128)} %param.11) | copy-start | bytes 393220
  18.2 2.1 %copy-start.2 = (s32[16,16,128]{2,1,0:T(8,128)S(1)}, s32[16,16,128]{2,1,0:T(8,128)}, u32[]{:S(2)}) copy-start(s32[16,16,128]{2,1,0:T(8,128)} %param.13) | copy-start | bytes 393220
  18.2 2.1 %copy-start.6 = (s32[16]{0:T(128)S(1)}, s32[16]{0:T(128)}, u32[]{:S(2)}) copy-start(s32[16]{0:T(128)} %refs_4_.3) | copy-start | bytes 196
  24.0 13.3 %collective-permute-start.7 = (f32[256,128]{1,0:T(8,128)S(1)}, f32[256,128]{1,0:T(8,128)S(1)}, u32[]{:S(2)}, u32[]{:S(2)}) collective-permute-start(f32[256,128]{1,0:T(8,128)S(1)} %get-tuple-element.67), channel_id=1, source_target_pairs={{0,28},{4,24},{8,20},{12,16},{16,12},{20,8},{24,4},{28,0},{1,29},{... | collective-permute-start | bytes 393224 | tf_op jit(solution)/shard_map/ppermute | solution.py:442
  25.6 11.6 %collective-permute-start.5 = (f32[5,48,128]{2,1,0:T(8,128)S(1)}, f32[5,48,128]{2,1,0:T(8,128)S(1)}, u32[]{:S(2)}, u32[]{:S(2)}) collective-permute-start(f32[5,48,128]{2,1,0:T(8,128)S(1)} %get-tuple-element.65), channel_id=1, source_target_pairs={{0,4},{4,0},{8,12},{12,8},{16,20},{20,16},{24,28},{28,24},{1,5},{5... | collective-permute-start | bytes 368648 | tf_op jit(solution)/shard_map/ppermute | solution.py:442
  25.7 11.6 %collective-permute-start.6 = (f32[5,48,128]{2,1,0:T(8,128)S(1)}, f32[5,48,128]{2,1,0:T(8,128)S(1)}, u32[]{:S(2)}, u32[]{:S(2)}) collective-permute-start(f32[5,48,128]{2,1,0:T(8,128)S(1)} %get-tuple-element.66), channel_id=1, source_target_pairs={{4,8},{8,4},{12,16},{16,12},{20,24},{24,20},{5,9},{9,5},{13,17},{1... | collective-permute-start | bytes 368648 | tf_op jit(solution)/shard_map/ppermute | solution.py:442
  29.2 6.1 %collective-permute-start.8 = (f32[5,8,128]{2,1,0:T(8,128)S(1)}, f32[5,8,128]{2,1,0:T(8,128)S(1)}, u32[]{:S(2)}, u32[]{:S(2)}) collective-permute-start(f32[5,8,128]{2,1,0:T(8,128)S(1)} %get-tuple-element.70), channel_id=1, source_target_pairs={{0,1},{1,2},{2,3},{3,0},{4,5},{5,6},{6,7},{7,4},{8,9},{9,10},{10,1... | collective-permute-start | bytes 61448 | tf_op jit(solution)/shard_map/ppermute | solution.py:443
  29.7 5.6 %collective-permute-start.9 = (f32[5,8,128]{2,1,0:T(8,128)S(1)}, f32[5,8,128]{2,1,0:T(8,128)S(1)}, u32[]{:S(2)}, u32[]{:S(2)}) collective-permute-start(f32[5,8,128]{2,1,0:T(8,128)S(1)} %get-tuple-element.71), channel_id=1, source_target_pairs={{1,0},{2,1},{3,2},{0,3},{5,4},{6,5},{7,6},{4,7},{9,8},{10,9},{11,1... | collective-permute-start | bytes 61448 | tf_op jit(solution)/shard_map/ppermute | solution.py:443

commit v3 on v2

--- a/solution.py
+++ b/solution.py
@@ -44,12 +44,16 @@
     waves = [speed * one for one in state]
     plus = [a + b for a, b in zip(fluxes, waves)]
     minus = [a - b for a, b in zip(fluxes, waves)]
-    return plus, minus, metric_sq * (24.0 * viscosity * 0.5)
+    return plus, minus, metric_sq * (12.0 * viscosity * 0.5)
+
+
+def RCP(x):
+    return pl.reciprocal(x, approx=True)
 
 
 class Split:
-    def __init__(self, load):
-        self.load, self.memo = load, {}
+    def __init__(self, load, kind):
+        self.load, self.memo, self.kind = load, {}, kind
 
     def get(self, name, n):
         if (name, n) not in self.memo:
@@ -68,33 +72,39 @@
     def make_t(self, n):
         return self.get("e", n + 1) - self.get("e", n)
 
-    def make_t2(self, n):
-        return self.get("t", n) + self.get("t", n)
+    def make_near(self, n):
+        return self.get("t", n).astype(self.kind)
+
+    def make_near2(self, n):
+        return self.get("near", n) + self.get("near", n)
+
+    def make_low(self, n):
+        return self.get("d", n).astype(self.kind)
 
     def make_smooth(self, n):
-        high, low, bend = self.get("d", n), self.get("d", n - 1), self.get("e", n)
+        high, low = self.get("low", n), self.get("low", n - 1)
+        bend = self.get("e", n).astype(self.kind)
         twice = bend + bend
         a, b = high * twice, low * twice
-        centre = (a - b) * (2.0 / 3.0) + (high * low + 16.0 * epsilon / 3.0)
+        centre = (a - b) * self.kind(2.0 / 3.0) + (high * low + self.kind(16.0 * epsilon / 3.0))
         return centre + a, centre, centre - b
 
     def correction(self, outer, middle, inner, near, far):
-        left = middle * pl.reciprocal(outer, approx=True)
-        right = middle * pl.reciprocal(inner, approx=True)
-        weight_left = left * left * (1.0 / 3.0)
+        left = middle * RCP(outer)
+        right = middle * RCP(inner)
+        weight_left = left * left * self.kind(1.0 / 3.0)
         weight_right = right * right
-        total = (weight_left + weight_right) + 2.0
-        return (weight_left * near + weight_right * far) * pl.reciprocal(total, approx=True)
-
-
-def sweep(load_plus, load_minus, load_diffused, load_metric, store, first, last, open_low=False, open_high=False):
-    plus, minus = Split(load_plus), Split(load_minus)
+        total = (weight_left + weight_right) + self.kind(2.0)
+        return (weight_left * near + weight_right * far) * RCP(total)
+
+
+def sweep(kind, load_plus, load_minus, load_diffused, load_metric, store, first, last, open_low=False, open_high=False):
+    plus, minus = Split(load_plus, kind), Split(load_minus, kind)
     central, diffused, metric = {}, {}, {}
 
-    def flux_centre(n):
+    def tripled(n):
         if n not in central:
-            both = plus.get("v", n) + minus.get("v", n)
-            central[n] = 6.0 * both - (plus.get("e", n) + minus.get("e", n))
+            central[n] = 3.0 * (plus.get("v", n) + minus.get("v", n))
         return central[n]
 
     def cached(table, load, n):
@@ -108,19 +118,17 @@
             plus.get("smooth", n - 1)[0],
             plus.get("smooth", n)[1],
             plus.get("smooth", n + 1)[2],
-            plus.get("t2", n - 1),
-            plus.get("t", n),
+            plus.get("near2", n - 1),
+            plus.get("near", n),
         )
         down = minus.correction(
             minus.get("smooth", n + 2)[2],
             minus.get("smooth", n + 1)[1],
             minus.get("smooth", n)[0],
-            minus.get("t2", n + 1),
-            minus.get("t", n),
+            minus.get("near2", n + 1),
+            minus.get("near", n),
         )
-        correction = down - up
-        flux = flux_centre(n) + flux_centre(n + 1) + (plus.get("t", n) - minus.get("t", n))
-        flux = flux + (correction + correction)
+        flux = (tripled(n) + tripled(n + 1)) - (plus.get("e", n) + minus.get("e", n + 1)) + (down - up).astype(F32)
         face_metric = cached(metric, load_metric, n) + cached(metric, load_metric, n + 1)
         jump = cached(diffused, load_diffused, n + 1) - cached(diffused, load_diffused, n)
         net = face_metric * jump - flux
@@ -221,7 +229,7 @@
     copies[5].wait()
 
 
-def early_kernel(dims, state_ref, span_ref, span_met_ref, met_ref, acc_ref, plus_i, minus_i, metric_i, plus_j, minus_j,
+def early_kernel(dims, kind, state_ref, span_ref, span_met_ref, met_ref, acc_ref, plus_i, minus_i, metric_i, plus_j, minus_j,
                  metric_j, diffused_ref, plus_k, minus_k, metric_k, diffused_k):
     rows_i, height = dims
     diffused_ref[0] = jnp.zeros(diffused_ref.shape[1:], F32)
@@ -251,25 +259,23 @@
 
     lax.fori_loop(0, height // 2, spans, 0, unroll=2)
 
-    def normal(step, carry):
-        f, tile = step // 2, step % 2
-
+    def normal(f, carry):
         def rows(n):
-            return pl.ds(tile * 8 * rows_i + min(n, rows_i - 1), 8, stride=rows_i)
+            return pl.ds(min(n, rows_i - 1), rows_i, stride=rows_i)
 
         def store(n, value):
             acc_ref[f, rows(n), :] = value
 
         for n in range(2):
-            store(n, jnp.zeros((8, 128), F32))
-        sweep(lambda n: plus_j[f, rows(n), :], lambda n: minus_j[f, rows(n), :], lambda n: diffused_ref[f, rows(n), :],
+            store(n, jnp.zeros((rows_i, 128), F32))
+        sweep(kind, lambda n: plus_j[f, rows(n), :], lambda n: minus_j[f, rows(n), :], lambda n: diffused_ref[f, rows(n), :],
               lambda n: metric_j[rows(n), :], store, 2, rows_i - 1, open_low=True)
         return carry
 
-    lax.fori_loop(0, 10, normal, 0)
-
-
-def span_kernel(dims, span_ref, span_met_ref, span_low_ref, span_high_ref, met_low_ref, met_high_ref,
+    lax.fori_loop(0, 5, normal, 0)
+
+
+def span_kernel(dims, kind, span_ref, span_met_ref, span_low_ref, span_high_ref, met_low_ref, met_high_ref,
                 plus_k, minus_k, metric_k, diffused_k, out_ref,
                 acc_ref, halo_plus, halo_minus, halo_metric, halo_diffused, pad_ref):
     rows_i, height = dims
@@ -298,19 +304,21 @@
 
     def sweep_span(f, carry):
         def loader(ref, halo, lead):
-            def load(n):
+            def one(n):
                 if 0 <= n < height:
                     return ref[lead + (slice(n * 8, n * 8 + 8),)]
                 r = n + H if n < 0 else n - height + H
                 return halo[lead + (slice(r * 8, r * 8 + 8),)]
 
-            return load
+            return lambda n: jnp.concatenate([one(n), one(n + height // 2)], axis=0)
 
         def store(n, value):
-            acc_ref[f, n * 8 : n * 8 + 8, :] = value
-
-        sweep(loader(plus_k, halo_plus, (f,)), loader(minus_k, halo_minus, (f,)), loader(diffused_k, halo_diffused, (f,)),
-              loader(metric_k, halo_metric, ()), store, -1, height - 1)
+            acc_ref[f, n * 8 : n * 8 + 8, :] = value[:8]
+            m = n + height // 2
+            acc_ref[f, m * 8 : m * 8 + 8, :] = value[8:]
+
+        sweep(kind, loader(plus_k, halo_plus, (f,)), loader(minus_k, halo_minus, (f,)), loader(diffused_k, halo_diffused, (f,)),
+              loader(metric_k, halo_metric, ()), store, -1, height // 2 - 1)
         return carry
 
     lax.fori_loop(0, 5, sweep_span, 0)
@@ -320,7 +328,7 @@
             out_ref[f, half * 128 : (half + 1) * 128, :] = jnp.concatenate(parts, axis=0).T
 
 
-def late_kernel(dims, final, *refs):
+def late_kernel(dims, kind, final, *refs):
     rows_i, height = dims
     total = rows_i * rows_i
     (state_ref, met_ref, vol_ref, blank_ref, partner_ref, core_ref, chip_ref, met_core_ref, met_chip_ref, wake_ref,
@@ -357,27 +365,25 @@
         put((halo_plus, halo_minus, halo_metric), to,
             *point_fluxes(state, prims, [unit(0, m, row[m]) for m in range(3)]))
 
-    def chord(step, carry):
-        f, tile = step // 2, step % 2
-
+    def chord(f, carry):
         def loader(ref, halo, lead):
             def load(n):
                 if 0 <= n < rows_i:
-                    return ref[lead + (aligned(n * rows_i + tile * 8, 8),)]
+                    return ref[lead + (aligned(n * rows_i, rows_i),)]
                 r = n + H if n < 0 else n - rows_i + H
-                return halo[lead + (aligned(r * rows_i + tile * 8, 8),)]
+                return halo[lead + (aligned(r * rows_i, rows_i),)]
 
             return load
 
         def store(n, value):
-            rows = aligned(n * rows_i + tile * 8, 8)
+            rows = aligned(n * rows_i, rows_i)
             acc_ref[f, rows, :] = value + (normal_ref[f, rows, :] + span_acc_ref[f, rows, :])
 
-        sweep(loader(plus_i, halo_plus, (f,)), loader(minus_i, halo_minus, (f,)), loader(diffused_ref, halo_diffused, (f,)),
+        sweep(kind, loader(plus_i, halo_plus, (f,)), loader(minus_i, halo_minus, (f,)), loader(diffused_ref, halo_diffused, (f,)),
               loader(metric_i, halo_metric, ()), store, -1, rows_i - 1)
         return carry
 
-    lax.fori_loop(0, 10, chord, 0)
+    lax.fori_loop(0, 5, chord, 0)
 
     base = (count - 1 - position) * rows_i
     for i in range(rows_i):
@@ -391,30 +397,28 @@
         put((halo_plus, halo_minus, halo_metric), to,
             *point_fluxes(state, prims, [unit(1, m, met_ref[3 + m, wall, :]) for m in range(3)]))
 
-    def normal(step, carry):
-        f, tile = step // 2, step % 2
-
+    def normal(f, carry):
         def rows(n):
-            return pl.ds(tile * 8 * rows_i + n, 8, stride=rows_i)
+            return pl.ds(n, rows_i, stride=rows_i)
 
         def loader(ref, halo, lead):
             def load(n):
                 if n >= 0:
                     return ref[lead + (rows(n),)]
-                return halo[lead + (aligned((-1 - n) * rows_i + tile * 8, 8),)]
+                return halo[lead + (aligned((-1 - n) * rows_i, rows_i),)]
 
             return load
 
         def store(n, value):
             acc_ref[f, rows(n), :] = acc_ref[f, rows(n), :] + value
 
-        sweep(loader(plus_j, halo_plus, (f,)), loader(minus_j, halo_minus, (f,)), loader(diffused_ref, halo_diffused, (f,)),
+        sweep(kind, loader(plus_j, halo_plus, (f,)), loader(minus_j, halo_minus, (f,)), loader(diffused_ref, halo_diffused, (f,)),
               lambda n: metric_j[rows(max(n, 0)), :], store, -1, 1, open_high=True)
         return carry
 
-    lax.fori_loop(0, 10, normal, 0)
-
-    scale = (time_step / 24.0) * blank_ref[...].astype(F32) / vol_ref[...]
+    lax.fori_loop(0, 5, normal, 0)
+
+    scale = (time_step / 12.0) * blank_ref[...].astype(F32) / vol_ref[...]
     for f in range(5):
         moved = state_ref[f] + scale * acc_ref[f]
         out_ref[f] = 0.5 * start_ref[f] + 0.5 * moved if final else moved
@@ -473,8 +477,9 @@
     field, span_rows, halo = shape(5, total, lanes), height * 8, 2 * H * rows_i
     state, span, met, *sent = call(
         functools.partial(prepare_kernel, dims), "prepare",
-        (density.reshape(total, lanes), velocity.reshape(3, total, lanes), pressure.reshape(total, lanes),
-         metrics.reshape(9, total, lanes)),
+        [pltpu.with_memory_space_constraint(one, pltpu.HBM) for one in (
+            density.reshape(total, lanes), velocity.reshape(3, total, lanes), pressure.reshape(total, lanes),
+            metrics.reshape(9, total, lanes))],
         [field, shape(8, total, lanes), shape(9, total, lanes)] + parts(8),
         [pltpu.VMEM((total, lanes), F32), pltpu.VMEM((3, total, lanes), F32), pltpu.VMEM((total, lanes), F32),
          pltpu.SemaphoreType.DMA((6,))],
@@ -489,19 +494,20 @@
     metric_halo = None
     start = state
     for final in (False, True):
+        kind = jnp.bfloat16 if final else F32
         core, chip, wake, span_low, span_high = exchange(sent)
         if metric_halo is None:
             metric_halo = core, chip, span_low, span_high
         line, span_line = shape(5, total, lanes), shape(5, span_rows, lanes)
         normal, *lines = call(
-            functools.partial(early_kernel, dims), "early", (state, span, span_met, met),
+            functools.partial(early_kernel, dims, kind), "early", (state, span, span_met, met),
             [field, line, line, shape(total, lanes), line, line, shape(total, lanes), line,
              span_line, span_line, shape(span_rows, lanes), span_line],
             [], cost=10**8,
         )
         plus_i, minus_i, metric_i, plus_j, minus_j, metric_j, diffused = lines[:7]
         (span_acc,) = call(
-            functools.partial(span_kernel, dims), "span",
+            functools.partial(span_kernel, dims, kind), "span",
             (span, span_met, span_low, span_high, metric_halo[2], metric_halo[3], *lines[7:]),
             [field],
             [pltpu.VMEM((5, span_rows, lanes), F32)] + halo_scratch(2 * H * 8) + [pltpu.VMEM((8, 2 * H * 8, lanes), F32)],
@@ -511,7 +517,7 @@
                plus_i, minus_i, metric_i, plus_j, minus_j, metric_j, diffused)
         ins += (start,) if final else ()
         state, *rest = call(
-            functools.partial(late_kernel, dims, final), "late", ins,
+            functools.partial(late_kernel, dims, kind, final), "late", ins,
             [field] if final else [field, field] + parts(5),
             [pltpu.VMEM((5, total, lanes), F32)] + halo_scratch(halo) + [pltpu.VMEM((rows_i * 16, lanes), F32)],
             [whole] * 4 + [smem] + [whole] * (len(ins) - 5),

time: 41.9 us -> 35.8 us (0.85)
  local copies, waits for them, and re-layouts: 4.09 us -> 0.02 us
  Pallas kernels: 19.4 us -> 17.4 us
    unnamed x14 -> x6, local copies, waits for them, and re-layouts: 4.09 us -> 0.02 us
    pallas_call x7, Pallas kernels: 19.4 us -> 17.4 us  [call(): pl.pallas_call(kernel, out_shape=outs, in_specs=specs or [whole] * len(in...]
  transfers between devices with their start and end apart: 10 -> 10, of which waited for: 0 -> 0; matrix products, arithmetic and copies ran while one was open for 0% -> 0% of each run, Pallas kernels for 23% -> 25%
where the time goes in v3:
time: 35.8 us; the launch traced here: 35.7 us
  starting transfers between devices  18 us (50%)
  Pallas kernels  17.4 us (49%)
    pallas_call x7, Pallas kernels, call(): pl.pallas_call(kernel, out_shape=outs, in_specs=specs or [whole] * len(in...  17.4 us
    ppermute x2, starting transfers between devices, exchange(): lax.ppermute(chip, 'wrap', chips)  7.96 us
    ppermute x2, starting transfers between devices, exchange(): lax.ppermute(span_low, 'span', ring_down)  4.85 us
    ppermute x2, starting transfers between devices, exchange(): lax.ppermute(wake, 'wrap', mirror)  3.28 us
    ppermute x2, starting transfers between devices, exchange(): lax.ppermute(span_high, 'span', ring_up)  1.79 us
  transfers between devices with their start and end apart: 10, of which 0 were waited for; matrix products, arithmetic and copies ran while one was open for 0% of the time, Pallas kernels for 25%

profile of v3, /device:TPU:1, one launch (start us, length us, event | category | flops | bytes accessed | tf_op | source)
XLA Modules:
  0.0 35.7 jit_solution(1810919033305071814)
XLA Ops:
  0.0 1.7 %prepare.1 = (f32[5,256,128]{2,1,0:T(8,128)S(1)}, f32[8,256,128]{2,1,0:T(8,128)S(1)}, f32[9,256,128]{2,1,0:T(8,128)S(1)}, f32[8,48,128]{2,1,0:T(8,128)S(1)}, f32...) custom-call(f32[256,128]{1,0:T(8,128)} %bitcast.13, ...), custom_call_target="tpu_custom_call" | custom-call | tf_op jit(solution)/shard_map/prepare/pallas_call | solution.py:461
  1.7 0.1 collective-permute-start
  1.8 4.5 %collective-permute-start.1 = (f32[8,48,128]{2,1,0:T(8,128)S(1)}, f32[8,48,128]{2,1,0:T(8,128)S(1)}, u32[]{:S(2)}, u32[]{:S(2)}) collective-permute-start(f32[8,48,128]{2,1,0:T(8,128)S(1)} %get-tuple-element.47), channel_id=1, source_target_pairs={{4,8},{8,4},{12,16},{16,12},{20,24},{24,20},{5,9},{9,5},{13,17},{1... | collective-permute-start | bytes 589832 | tf_op jit(solution)/shard_map/ppermute | solution.py:446
  6.3 1.6 %collective-permute-start.2 = (f32[256,128]{1,0:T(8,128)S(1)}, f32[256,128]{1,0:T(8,128)S(1)}, u32[]{:S(2)}, u32[]{:S(2)}) collective-permute-start(f32[256,128]{1,0:T(8,128)S(1)} %get-tuple-element.48), channel_id=1, source_target_pairs={{0,28},{4,24},{8,20},{12,16},{16,12},{20,8},{24,4},{28,0},{1,29},{... | collective-permute-start | bytes 393224 | tf_op jit(solution)/shard_map/ppermute | solution.py:446
  7.9 1.3 %collective-permute-start.3 = (f32[8,8,128]{2,1,0:T(8,128)S(1)}, f32[8,8,128]{2,1,0:T(8,128)S(1)}, u32[]{:S(2)}, u32[]{:S(2)}) collective-permute-start(f32[8,8,128]{2,1,0:T(8,128)S(1)} %get-tuple-element.51), channel_id=1, source_target_pairs={{0,1},{1,2},{2,3},{3,0},{4,5},{5,6},{6,7},{7,4},{8,9},{9,10},{10,1... | collective-permute-start | bytes 98312 | tf_op jit(solution)/shard_map/ppermute | solution.py:447
  9.2 2.0 %collective-permute-start.4 = (f32[8,8,128]{2,1,0:T(8,128)S(1)}, f32[8,8,128]{2,1,0:T(8,128)S(1)}, u32[]{:S(2)}, u32[]{:S(2)}) collective-permute-start(f32[8,8,128]{2,1,0:T(8,128)S(1)} %get-tuple-element.52), channel_id=1, source_target_pairs={{1,0},{2,1},{3,2},{0,3},{5,4},{6,5},{7,6},{4,7},{9,8},{10,9},{11,1... | collective-permute-start | bytes 98312 | tf_op jit(solution)/shard_map/ppermute | solution.py:447
  11.3 2.8 %early.2 = (f32[5,256,128]{2,1,0:T(8,128)S(1)}, f32[5,256,128]{2,1,0:T(8,128)S(1)}, f32[5,256,128]{2,1,0:T(8,128)S(1)}, f32[256,128]{1,0:T(8,128)S(1)}, f32[5,25...) custom-call(f32[5,256,128]{2,1,0:T(8,128)S(1)} %get-tuple-element.44, ...), custom_call_target="tpu_custom_call" | custom-call | flops 100000000 | bytes 25000000 | tf_op jit(solution)/shard_map/early/pallas_call | solution.py:461
  14.0 0.0 collective-permute-done.4.span_high_ref.met_high_ref
  14.1 0.0 copy-start
  14.1 0.0 copy-start.1
  14.1 0.0 copy-start.2
  14.1 2.0 %span.2.refs_11_ = f32[5,256,128]{2,1,0:T(8,128)S(1)} custom-call(f32[8,256,128]{2,1,0:T(8,128)S(1)} %get-tuple-element.49.span_ref.span_met_ref, f32[8,256,128]{2,1,0:T(8,128)S(1)} %get-tuple-element.49.span_ref.span_met_ref, f32[8,8,128]{2,1,0:T(8,128)S(1)} %collective-permute-done.3.span_low_ref.met_low_ref, ...), custom_call_target="tpu_custom_call" | custom-call | flops 100000000 | bytes 25000000 | tf_op jit(solution)/shard_map/span/pallas_call | solution.py:461
  16.1 0.0 collective-permute-done.2.refs_9_
  16.2 0.0 collective-permute-done.refs_5_.refs_7_
  16.2 3.4 %late.2 = (f32[5,256,128]{2,1,0:T(8,128)S(1)}, f32[5,256,128]{2,1,0:T(8,128)S(1)}, f32[5,48,128]{2,1,0:T(8,128)S(1)}, f32[5,48,128]{2,1,0:T(8,128)S(1)}, f32[256...) custom-call(f32[5,256,128]{2,1,0:T(8,128)S(1)} %get-tuple-element.44.state_ref.refs_0_.refs_19_, ...), custom_call_target="tpu_custom_call" | custom-call | flops 100000000 | bytes 25000000 | tf_op jit(solution)/shard_map/late/pallas_call | solution.py:461
  19.7 1.6 %collective-permute-start.7 = (f32[256,128]{1,0:T(8,128)S(1)}, f32[256,128]{1,0:T(8,128)S(1)}, u32[]{:S(2)}, u32[]{:S(2)}) collective-permute-start(f32[256,128]{1,0:T(8,128)S(1)} %get-tuple-element.67), channel_id=1, source_target_pairs={{0,28},{4,24},{8,20},{12,16},{16,12},{20,8},{24,4},{28,0},{1,29},{... | collective-permute-start | bytes 393224 | tf_op jit(solution)/shard_map/ppermute | solution.py:446
  21.3 0.0 collective-permute-start.5
  21.3 3.5 %collective-permute-start.6 = (f32[5,48,128]{2,1,0:T(8,128)S(1)}, f32[5,48,128]{2,1,0:T(8,128)S(1)}, u32[]{:S(2)}, u32[]{:S(2)}) collective-permute-start(f32[5,48,128]{2,1,0:T(8,128)S(1)} %get-tuple-element.66), channel_id=1, source_target_pairs={{4,8},{8,4},{12,16},{16,12},{20,24},{24,20},{5,9},{9,5},{13,17},{1... | collective-permute-start | bytes 368648 | tf_op jit(solution)/shard_map/ppermute | solution.py:446
  24.8 0.5 %collective-permute-start.8 = (f32[5,8,128]{2,1,0:T(8,128)S(1)}, f32[5,8,128]{2,1,0:T(8,128)S(1)}, u32[]{:S(2)}, u32[]{:S(2)}) collective-permute-start(f32[5,8,128]{2,1,0:T(8,128)S(1)} %get-tuple-element.70), channel_id=1, source_target_pairs={{0,1},{1,2},{2,3},{3,0},{4,5},{5,6},{6,7},{7,4},{8,9},{9,10},{10,1... | collective-permute-start | bytes 61448 | tf_op jit(solution)/shard_map/ppermute | solution.py:447
  25.3 2.8 %collective-permute-start.9 = (f32[5,8,128]{2,1,0:T(8,128)S(1)}, f32[5,8,128]{2,1,0:T(8,128)S(1)}, u32[]{:S(2)}, u32[]{:S(2)}) collective-permute-start(f32[5,8,128]{2,1,0:T(8,128)S(1)} %get-tuple-element.71), channel_id=1, source_target_pairs={{1,0},{2,1},{3,2},{0,3},{5,4},{6,5},{7,6},{4,7},{9,8},{10,9},{11,1... | collective-permute-start | bytes 61448 | tf_op jit(solution)/shard_map/ppermute | solution.py:447
  28.1 2.4 %early.3 = (f32[5,256,128]{2,1,0:T(8,128)S(1)}, f32[5,256,128]{2,1,0:T(8,128)S(1)}, f32[5,256,128]{2,1,0:T(8,128)S(1)}, f32[256,128]{1,0:T(8,128)S(1)}, f32[5,25...) custom-call(f32[5,256,128]{2,1,0:T(8,128)S(1)} %get-tuple-element.64, ...), custom_call_target="tpu_custom_call" | custom-call | flops 100000000 | bytes 25000000 | tf_op jit(solution)/shard_map/early/pallas_call | solution.py:461
  30.5 0.0 collective-permute-done.8.span_low_ref
  30.6 1.5 %span.3.refs_11_ = f32[5,256,128]{2,1,0:T(8,128)S(1)} custom-call(f32[5,256,128]{2,1,0:T(8,128)S(1)} %get-tuple-element.68.span_ref, f32[8,256,128]{2,1,0:T(8,128)S(1)} %get-tuple-element.49.span_ref.span_met_ref, f32[5,8,128]{2,1,0:T(8,128)S(1)} %collective-permute-done.8.span_low_ref, f32[5,8,128]{2,1,0:T(8,128)S(1)} %collective-permute-done.9.span_high_ref, ...), custom_call_target="tpu_custom_call" | custom-call | flops 100000000 | bytes 25000000 | tf_op jit(solution)/shard_map/span/pallas_call | solution.py:461
  32.1 3.5 %late.3 = f32[5,256,128]{2,1,0:T(8,128)} custom-call(f32[5,256,128]{2,1,0:T(8,128)S(1)} %get-tuple-element.64.state_ref.refs_0_, f32[9,256,128]{2,1,0:T(8,128)S(1)} %get-tuple-element.45.met_ref.refs_1_, f32[256,128]{1,0:T(8,128)S(1)} %bitcast.8, s32[256,128]{1,0:T(8,128)S(1)} %bitcast.10, s32[16]{0:T(128)S(1)} %copy-done.2, ...), custom_call_target="tpu_custom_call" | custom-call | flops 100000000 | bytes 25000000 | tf_op jit(solution)/shard_map/late/pallas_call | solution.py:461
  (9 shorter events, 0.0 us)
Async XLA Ops:
  1.7 14.5 %collective-permute-start = (f32[8,48,128]{2,1,0:T(8,128)S(1)}, f32[8,48,128]{2,1,0:T(8,128)S(1)}, u32[]{:S(2)}, u32[]{:S(2)}) collective-permute-start(f32[8,48,128]{2,1,0:T(8,128)S(1)} %get-tuple-element.46), channel_id=1, source_target_pairs={{0,4},{4,0},{8,12},{12,8},{16,20},{20,16},{24,28},{28,24},{1,5},{5... | collective-permute-start | bytes 589832 | tf_op jit(solution)/shard_map/ppermute | solution.py:446
  1.8 14.4 %collective-permute-start.1 = (f32[8,48,128]{2,1,0:T(8,128)S(1)}, f32[8,48,128]{2,1,0:T(8,128)S(1)}, u32[]{:S(2)}, u32[]{:S(2)}) collective-permute-start(f32[8,48,128]{2,1,0:T(8,128)S(1)} %get-tuple-element.47), channel_id=1, source_target_pairs={{4,8},{8,4},{12,16},{16,12},{20,24},{24,20},{5,9},{9,5},{13,17},{1... | collective-permute-start | bytes 589832 | tf_op jit(solution)/shard_map/ppermute | solution.py:446
  6.3 9.9 %collective-permute-start.2 = (f32[256,128]{1,0:T(8,128)S(1)}, f32[256,128]{1,0:T(8,128)S(1)}, u32[]{:S(2)}, u32[]{:S(2)}) collective-permute-start(f32[256,128]{1,0:T(8,128)S(1)} %get-tuple-element.48), channel_id=1, source_target_pairs={{0,28},{4,24},{8,20},{12,16},{16,12},{20,8},{24,4},{28,0},{1,29},{... | collective-permute-start | bytes 393224 | tf_op jit(solution)/shard_map/ppermute | solution.py:446
  7.9 6.1 %collective-permute-start.3 = (f32[8,8,128]{2,1,0:T(8,128)S(1)}, f32[8,8,128]{2,1,0:T(8,128)S(1)}, u32[]{:S(2)}, u32[]{:S(2)}) collective-permute-start(f32[8,8,128]{2,1,0:T(8,128)S(1)} %get-tuple-element.51), channel_id=1, source_target_pairs={{0,1},{1,2},{2,3},{3,0},{4,5},{5,6},{6,7},{7,4},{8,9},{9,10},{10,1... | collective-permute-start | bytes 98312 | tf_op jit(solution)/shard_map/ppermute | solution.py:447
  9.2 4.8 %collective-permute-start.4 = (f32[8,8,128]{2,1,0:T(8,128)S(1)}, f32[8,8,128]{2,1,0:T(8,128)S(1)}, u32[]{:S(2)}, u32[]{:S(2)}) collective-permute-start(f32[8,8,128]{2,1,0:T(8,128)S(1)} %get-tuple-element.52), channel_id=1, source_target_pairs={{1,0},{2,1},{3,2},{0,3},{5,4},{6,5},{7,6},{4,7},{9,8},{10,9},{11,1... | collective-permute-start | bytes 98312 | tf_op jit(solution)/shard_map/ppermute | solution.py:447
  14.1 2.1 %copy-start = (f32[16,16,128]{2,1,0:T(8,128)S(1)}, f32[16,16,128]{2,1,0:T(8,128)}, u32[]{:S(2)}) copy-start(f32[16,16,128]{2,1,0:T(8,128)} %param.11) | copy-start | bytes 393220
  14.1 2.1 %copy-start.1 = (s32[16,16,128]{2,1,0:T(8,128)S(1)}, s32[16,16,128]{2,1,0:T(8,128)}, u32[]{:S(2)}) copy-start(s32[16,16,128]{2,1,0:T(8,128)} %param.13) | copy-start | bytes 393220
  14.1 2.1 %copy-start.2 = (s32[16]{0:T(128)S(1)}, s32[16]{0:T(128)}, u32[]{:S(2)}) copy-start(s32[16]{0:T(128)} %refs_4_.3) | copy-start | bytes 196
  19.7 12.5 %collective-permute-start.7 = (f32[256,128]{1,0:T(8,128)S(1)}, f32[256,128]{1,0:T(8,128)S(1)}, u32[]{:S(2)}, u32[]{:S(2)}) collective-permute-start(f32[256,128]{1,0:T(8,128)S(1)} %get-tuple-element.67), channel_id=1, source_target_pairs={{0,28},{4,24},{8,20},{12,16},{16,12},{20,8},{24,4},{28,0},{1,29},{... | collective-permute-start | bytes 393224 | tf_op jit(solution)/shard_map/ppermute | solution.py:446
  21.3 10.8 %collective-permute-start.5 = (f32[5,48,128]{2,1,0:T(8,128)S(1)}, f32[5,48,128]{2,1,0:T(8,128)S(1)}, u32[]{:S(2)}, u32[]{:S(2)}) collective-permute-start(f32[5,48,128]{2,1,0:T(8,128)S(1)} %get-tuple-element.65), channel_id=1, source_target_pairs={{0,4},{4,0},{8,12},{12,8},{16,20},{20,16},{24,28},{28,24},{1,5},{5... | collective-permute-start | bytes 368648 | tf_op jit(solution)/shard_map/ppermute | solution.py:446
  21.3 10.8 %collective-permute-start.6 = (f32[5,48,128]{2,1,0:T(8,128)S(1)}, f32[5,48,128]{2,1,0:T(8,128)S(1)}, u32[]{:S(2)}, u32[]{:S(2)}) collective-permute-start(f32[5,48,128]{2,1,0:T(8,128)S(1)} %get-tuple-element.66), channel_id=1, source_target_pairs={{4,8},{8,4},{12,16},{16,12},{20,24},{24,20},{5,9},{9,5},{13,17},{1... | collective-permute-start | bytes 368648 | tf_op jit(solution)/shard_map/ppermute | solution.py:446
  24.8 5.7 %collective-permute-start.8 = (f32[5,8,128]{2,1,0:T(8,128)S(1)}, f32[5,8,128]{2,1,0:T(8,128)S(1)}, u32[]{:S(2)}, u32[]{:S(2)}) collective-permute-start(f32[5,8,128]{2,1,0:T(8,128)S(1)} %get-tuple-element.70), channel_id=1, source_target_pairs={{0,1},{1,2},{2,3},{3,0},{4,5},{5,6},{6,7},{7,4},{8,9},{9,10},{10,1... | collective-permute-start | bytes 61448 | tf_op jit(solution)/shard_map/ppermute | solution.py:447
  25.3 5.3 %collective-permute-start.9 = (f32[5,8,128]{2,1,0:T(8,128)S(1)}, f32[5,8,128]{2,1,0:T(8,128)S(1)}, u32[]{:S(2)}, u32[]{:S(2)}) collective-permute-start(f32[5,8,128]{2,1,0:T(8,128)S(1)} %get-tuple-element.71), channel_id=1, source_target_pairs={{1,0},{2,1},{3,2},{0,3},{5,4},{6,5},{7,6},{4,7},{9,8},{10,9},{11,1... | collective-permute-start | bytes 61448 | tf_op jit(solution)/shard_map/ppermute | solution.py:447

commit v4 on v3

--- a/solution.py
+++ b/solution.py
@@ -331,7 +331,7 @@
 def late_kernel(dims, kind, final, *refs):
     rows_i, height = dims
     total = rows_i * rows_i
-    (state_ref, met_ref, vol_ref, blank_ref, partner_ref, core_ref, chip_ref, met_core_ref, met_chip_ref, wake_ref,
+    (state_ref, met_ref, vol_ref, blank_ref, partner_hbm, core_ref, chip_ref, met_core_ref, met_chip_ref, wake_ref,
      normal_ref, span_acc_ref, plus_i, minus_i, metric_i, plus_j, minus_j, metric_j, diffused_ref) = refs[:19]
     refs = refs[19:]
     if final:
@@ -340,7 +340,9 @@
     else:
         out_ref, out_span_ref = refs[:2]
         outs, refs = refs[2:7], refs[7:]
-    acc_ref, halo_plus, halo_minus, halo_metric, halo_diffused, ghost_ref = refs
+    acc_ref, halo_plus, halo_minus, halo_metric, halo_diffused, ghost_ref, partner_ref, sem = refs
+    fetch = pltpu.make_async_copy(partner_hbm, partner_ref, sem)
+    fetch.start()
     position, count = lax.axis_index("wrap"), lax.axis_size("wrap")
     even = lax.rem(position, 2) == 0
     at_end = (position == 0) | (position == count - 1)
@@ -385,6 +387,7 @@
 
     lax.fori_loop(0, 5, chord, 0)
 
+    fetch.wait()
     base = (count - 1 - position) * rows_i
     for i in range(rows_i):
         ghost_ref[i * 16 : i * 16 + 16, :] = wake_ref[aligned((partner_ref[i] - base) * 16, 16), :]
@@ -454,7 +457,7 @@
     volume, blank = volume.reshape(total, lanes), iblank.reshape(total, lanes)
     whole = pl.BlockSpec(memory_space=pltpu.VMEM)
     far = pl.BlockSpec(memory_space=pltpu.HBM)
-    smem = pl.BlockSpec(memory_space=pltpu.SMEM)
+    wake_partner = pltpu.with_memory_space_constraint(wake_partner, pltpu.HBM)
     params = pltpu.CompilerParams(vmem_limit_bytes=16 * 2**20)
 
     def call(kernel, name, ins, outs, scratch, specs=None, cost=0):
@@ -519,8 +522,9 @@
         state, *rest = call(
             functools.partial(late_kernel, dims, kind, final), "late", ins,
             [field] if final else [field, field] + parts(5),
-            [pltpu.VMEM((5, total, lanes), F32)] + halo_scratch(halo) + [pltpu.VMEM((rows_i * 16, lanes), F32)],
-            [whole] * 4 + [smem] + [whole] * (len(ins) - 5),
+            [pltpu.VMEM((5, total, lanes), F32)] + halo_scratch(halo) + [pltpu.VMEM((rows_i * 16, lanes), F32)]
+            + [pltpu.SMEM((rows_i,), jnp.int32), pltpu.SemaphoreType.DMA],
+            [whole] * 4 + [far] + [whole] * (len(ins) - 5),
             cost=10**8,
         )
         if not final:

time: 35.8 us -> 34.6 us (0.966)
  Pallas kernels: 17.4 us -> 16.3 us
    pallas_call x7, Pallas kernels: 17.4 us -> 16.3 us  [call(): pl.pallas_call(kernel, out_shape=outs, in_specs=specs or [whole] * len(in...]
where the time goes in v4:
time: 34.6 us; the launch traced here: 34.5 us
  starting transfers between devices  18 us (52%)
  Pallas kernels  16.3 us (47%)
    pallas_call x7, Pallas kernels, call(): pl.pallas_call(kernel, out_shape=outs, in_specs=specs or [whole] * len(in...  16.3 us
    ppermute x2, starting transfers between devices, exchange(): lax.ppermute(chip, 'wrap', chips)  7.97 us
    ppermute x2, starting transfers between devices, exchange(): lax.ppermute(span_low, 'span', ring_down)  4.81 us
    ppermute x2, starting transfers between devices, exchange(): lax.ppermute(wake, 'wrap', mirror)  3.27 us
    ppermute x2, starting transfers between devices, exchange(): lax.ppermute(span_high, 'span', ring_up)  1.83 us
  transfers between devices with their start and end apart: 10, of which 0 were waited for; matrix products, arithmetic and copies ran while one was open for 0% of the time, Pallas kernels for 25%

profile of v4, /device:TPU:1, one launch (start us, length us, event | category | flops | bytes accessed | tf_op | source)
XLA Modules:
  0.0 34.5 jit_solution(14841729180714567635)
XLA Ops:
  0.0 1.7 %prepare.1 = (f32[5,256,128]{2,1,0:T(8,128)S(1)}, f32[8,256,128]{2,1,0:T(8,128)S(1)}, f32[9,256,128]{2,1,0:T(8,128)S(1)}, f32[8,48,128]{2,1,0:T(8,128)S(1)}, f32...) custom-call(f32[256,128]{1,0:T(8,128)} %bitcast.13, ...), custom_call_target="tpu_custom_call" | custom-call | tf_op jit(solution)/shard_map/prepare/pallas_call | solution.py:464
  1.7 0.1 collective-permute-start
  1.8 4.5 %collective-permute-start.1 = (f32[8,48,128]{2,1,0:T(8,128)S(1)}, f32[8,48,128]{2,1,0:T(8,128)S(1)}, u32[]{:S(2)}, u32[]{:S(2)}) collective-permute-start(f32[8,48,128]{2,1,0:T(8,128)S(1)} %get-tuple-element.47), channel_id=1, source_target_pairs={{4,8},{8,4},{12,16},{16,12},{20,24},{24,20},{5,9},{9,5},{13,17},{1... | collective-permute-start | bytes 589832 | tf_op jit(solution)/shard_map/ppermute | solution.py:449
  6.3 1.6 %collective-permute-start.2 = (f32[256,128]{1,0:T(8,128)S(1)}, f32[256,128]{1,0:T(8,128)S(1)}, u32[]{:S(2)}, u32[]{:S(2)}) collective-permute-start(f32[256,128]{1,0:T(8,128)S(1)} %get-tuple-element.48), channel_id=1, source_target_pairs={{0,28},{4,24},{8,20},{12,16},{16,12},{20,8},{24,4},{28,0},{1,29},{... | collective-permute-start | bytes 393224 | tf_op jit(solution)/shard_map/ppermute | solution.py:449
  7.9 1.3 %collective-permute-start.3 = (f32[8,8,128]{2,1,0:T(8,128)S(1)}, f32[8,8,128]{2,1,0:T(8,128)S(1)}, u32[]{:S(2)}, u32[]{:S(2)}) collective-permute-start(f32[8,8,128]{2,1,0:T(8,128)S(1)} %get-tuple-element.51), channel_id=1, source_target_pairs={{0,1},{1,2},{2,3},{3,0},{4,5},{5,6},{6,7},{7,4},{8,9},{9,10},{10,1... | collective-permute-start | bytes 98312 | tf_op jit(solution)/shard_map/ppermute | solution.py:450
  9.2 2.0 %collective-permute-start.4 = (f32[8,8,128]{2,1,0:T(8,128)S(1)}, f32[8,8,128]{2,1,0:T(8,128)S(1)}, u32[]{:S(2)}, u32[]{:S(2)}) collective-permute-start(f32[8,8,128]{2,1,0:T(8,128)S(1)} %get-tuple-element.52), channel_id=1, source_target_pairs={{1,0},{2,1},{3,2},{0,3},{5,4},{6,5},{7,6},{4,7},{9,8},{10,9},{11,1... | collective-permute-start | bytes 98312 | tf_op jit(solution)/shard_map/ppermute | solution.py:450
  11.3 2.7 %early.2 = (f32[5,256,128]{2,1,0:T(8,128)S(1)}, f32[5,256,128]{2,1,0:T(8,128)S(1)}, f32[5,256,128]{2,1,0:T(8,128)S(1)}, f32[256,128]{1,0:T(8,128)S(1)}, f32[5,25...) custom-call(f32[5,256,128]{2,1,0:T(8,128)S(1)} %get-tuple-element.44, ...), custom_call_target="tpu_custom_call" | custom-call | flops 100000000 | bytes 25000000 | tf_op jit(solution)/shard_map/early/pallas_call | solution.py:464
  14.0 0.0 collective-permute-done.3.span_low_ref.met_low_ref
  14.0 0.0 collective-permute-done.4.span_high_ref.met_high_ref
  14.0 0.0 copy-start
  14.0 0.0 copy-start.1
  14.1 2.0 %span.2.refs_11_ = f32[5,256,128]{2,1,0:T(8,128)S(1)} custom-call(f32[8,256,128]{2,1,0:T(8,128)S(1)} %get-tuple-element.49.span_ref.span_met_ref, f32[8,256,128]{2,1,0:T(8,128)S(1)} %get-tuple-element.49.span_ref.span_met_ref, f32[8,8,128]{2,1,0:T(8,128)S(1)} %collective-permute-done.3.span_low_ref.met_low_ref, ...), custom_call_target="tpu_custom_call" | custom-call | flops 100000000 | bytes 25000000 | tf_op jit(solution)/shard_map/span/pallas_call | solution.py:464
  16.1 0.0 collective-permute-done.1.refs_6_.refs_8_
  16.2 2.9 %late.2 = (f32[5,256,128]{2,1,0:T(8,128)S(1)}, f32[5,256,128]{2,1,0:T(8,128)S(1)}, f32[5,48,128]{2,1,0:T(8,128)S(1)}, f32[5,48,128]{2,1,0:T(8,128)S(1)}, f32[256...) custom-call(f32[5,256,128]{2,1,0:T(8,128)S(1)} %get-tuple-element.44.state_ref.refs_0_.refs_19_, ...), custom_call_target="tpu_custom_call" | custom-call | flops 100000000 | bytes 25000000 | tf_op jit(solution)/shard_map/late/pallas_call | solution.py:464
  19.1 1.6 %collective-permute-start.7 = (f32[256,128]{1,0:T(8,128)S(1)}, f32[256,128]{1,0:T(8,128)S(1)}, u32[]{:S(2)}, u32[]{:S(2)}) collective-permute-start(f32[256,128]{1,0:T(8,128)S(1)} %get-tuple-element.67), channel_id=1, source_target_pairs={{0,28},{4,24},{8,20},{12,16},{16,12},{20,8},{24,4},{28,0},{1,29},{... | collective-permute-start | bytes 393224 | tf_op jit(solution)/shard_map/ppermute | solution.py:449
  20.7 3.5 %collective-permute-start.6 = (f32[5,48,128]{2,1,0:T(8,128)S(1)}, f32[5,48,128]{2,1,0:T(8,128)S(1)}, u32[]{:S(2)}, u32[]{:S(2)}) collective-permute-start(f32[5,48,128]{2,1,0:T(8,128)S(1)} %get-tuple-element.66), channel_id=1, source_target_pairs={{4,8},{8,4},{12,16},{16,12},{20,24},{24,20},{5,9},{9,5},{13,17},{1... | collective-permute-start | bytes 368648 | tf_op jit(solution)/shard_map/ppermute | solution.py:449
  24.2 0.5 %collective-permute-start.8 = (f32[5,8,128]{2,1,0:T(8,128)S(1)}, f32[5,8,128]{2,1,0:T(8,128)S(1)}, u32[]{:S(2)}, u32[]{:S(2)}) collective-permute-start(f32[5,8,128]{2,1,0:T(8,128)S(1)} %get-tuple-element.70), channel_id=1, source_target_pairs={{0,1},{1,2},{2,3},{3,0},{4,5},{5,6},{6,7},{7,4},{8,9},{9,10},{10,1... | collective-permute-start | bytes 61448 | tf_op jit(solution)/shard_map/ppermute | solution.py:450
  24.7 2.8 %collective-permute-start.9 = (f32[5,8,128]{2,1,0:T(8,128)S(1)}, f32[5,8,128]{2,1,0:T(8,128)S(1)}, u32[]{:S(2)}, u32[]{:S(2)}) collective-permute-start(f32[5,8,128]{2,1,0:T(8,128)S(1)} %get-tuple-element.71), channel_id=1, source_target_pairs={{1,0},{2,1},{3,2},{0,3},{5,4},{6,5},{7,6},{4,7},{9,8},{10,9},{11,1... | collective-permute-start | bytes 61448 | tf_op jit(solution)/shard_map/ppermute | solution.py:450
  27.5 2.4 %early.3 = (f32[5,256,128]{2,1,0:T(8,128)S(1)}, f32[5,256,128]{2,1,0:T(8,128)S(1)}, f32[5,256,128]{2,1,0:T(8,128)S(1)}, f32[256,128]{1,0:T(8,128)S(1)}, f32[5,25...) custom-call(f32[5,256,128]{2,1,0:T(8,128)S(1)} %get-tuple-element.64, ...), custom_call_target="tpu_custom_call" | custom-call | flops 100000000 | bytes 25000000 | tf_op jit(solution)/shard_map/early/pallas_call | solution.py:464
  29.9 0.0 collective-permute-done.8.span_low_ref
  29.9 0.0 collective-permute-done.9.span_high_ref
  29.9 1.5 %span.3.refs_11_ = f32[5,256,128]{2,1,0:T(8,128)S(1)} custom-call(f32[5,256,128]{2,1,0:T(8,128)S(1)} %get-tuple-element.68.span_ref, f32[8,256,128]{2,1,0:T(8,128)S(1)} %get-tuple-element.49.span_ref.span_met_ref, f32[5,8,128]{2,1,0:T(8,128)S(1)} %collective-permute-done.8.span_low_ref, f32[5,8,128]{2,1,0:T(8,128)S(1)} %collective-permute-done.9.span_high_ref, ...), custom_call_target="tpu_custom_call" | custom-call | flops 100000000 | bytes 25000000 | tf_op jit(solution)/shard_map/span/pallas_call | solution.py:464
  31.5 0.0 collective-permute-done.7.refs_9_
  31.5 3.0 %late.3 = f32[5,256,128]{2,1,0:T(8,128)} custom-call(f32[5,256,128]{2,1,0:T(8,128)S(1)} %get-tuple-element.64.state_ref.refs_0_, f32[9,256,128]{2,1,0:T(8,128)S(1)} %get-tuple-element.45.met_ref.refs_1_, f32[256,128]{1,0:T(8,128)S(1)} %bitcast.8, s32[256,128]{1,0:T(8,128)S(1)} %bitcast.10, s32[16]{0:T(128)} %refs_4_.3, ...), custom_call_target="tpu_custom_call" | custom-call | flops 100000000 | bytes 25000000 | tf_op jit(solution)/shard_map/late/pallas_call | solution.py:464
  (7 shorter events, 0.0 us)
Async XLA Ops:
  1.7 14.4 %collective-permute-start = (f32[8,48,128]{2,1,0:T(8,128)S(1)}, f32[8,48,128]{2,1,0:T(8,128)S(1)}, u32[]{:S(2)}, u32[]{:S(2)}) collective-permute-start(f32[8,48,128]{2,1,0:T(8,128)S(1)} %get-tuple-element.46), channel_id=1, source_target_pairs={{0,4},{4,0},{8,12},{12,8},{16,20},{20,16},{24,28},{28,24},{1,5},{5... | collective-permute-start | bytes 589832 | tf_op jit(solution)/shard_map/ppermute | solution.py:449
  1.8 14.3 %collective-permute-start.1 = (f32[8,48,128]{2,1,0:T(8,128)S(1)}, f32[8,48,128]{2,1,0:T(8,128)S(1)}, u32[]{:S(2)}, u32[]{:S(2)}) collective-permute-start(f32[8,48,128]{2,1,0:T(8,128)S(1)} %get-tuple-element.47), channel_id=1, source_target_pairs={{4,8},{8,4},{12,16},{16,12},{20,24},{24,20},{5,9},{9,5},{13,17},{1... | collective-permute-start | bytes 589832 | tf_op jit(solution)/shard_map/ppermute | solution.py:449
  6.3 9.8 %collective-permute-start.2 = (f32[256,128]{1,0:T(8,128)S(1)}, f32[256,128]{1,0:T(8,128)S(1)}, u32[]{:S(2)}, u32[]{:S(2)}) collective-permute-start(f32[256,128]{1,0:T(8,128)S(1)} %get-tuple-element.48), channel_id=1, source_target_pairs={{0,28},{4,24},{8,20},{12,16},{16,12},{20,8},{24,4},{28,0},{1,29},{... | collective-permute-start | bytes 393224 | tf_op jit(solution)/shard_map/ppermute | solution.py:449
  7.9 6.1 %collective-permute-start.3 = (f32[8,8,128]{2,1,0:T(8,128)S(1)}, f32[8,8,128]{2,1,0:T(8,128)S(1)}, u32[]{:S(2)}, u32[]{:S(2)}) collective-permute-start(f32[8,8,128]{2,1,0:T(8,128)S(1)} %get-tuple-element.51), channel_id=1, source_target_pairs={{0,1},{1,2},{2,3},{3,0},{4,5},{5,6},{6,7},{7,4},{8,9},{9,10},{10,1... | collective-permute-start | bytes 98312 | tf_op jit(solution)/shard_map/ppermute | solution.py:450
  9.2 4.8 %collective-permute-start.4 = (f32[8,8,128]{2,1,0:T(8,128)S(1)}, f32[8,8,128]{2,1,0:T(8,128)S(1)}, u32[]{:S(2)}, u32[]{:S(2)}) collective-permute-start(f32[8,8,128]{2,1,0:T(8,128)S(1)} %get-tuple-element.52), channel_id=1, source_target_pairs={{1,0},{2,1},{3,2},{0,3},{5,4},{6,5},{7,6},{4,7},{9,8},{10,9},{11,1... | collective-permute-start | bytes 98312 | tf_op jit(solution)/shard_map/ppermute | solution.py:450
  14.0 2.1 %copy-start = (f32[16,16,128]{2,1,0:T(8,128)S(1)}, f32[16,16,128]{2,1,0:T(8,128)}, u32[]{:S(2)}) copy-start(f32[16,16,128]{2,1,0:T(8,128)} %param.11) | copy-start | bytes 393220
  14.0 2.1 %copy-start.1 = (s32[16,16,128]{2,1,0:T(8,128)S(1)}, s32[16,16,128]{2,1,0:T(8,128)}, u32[]{:S(2)}) copy-start(s32[16,16,128]{2,1,0:T(8,128)} %param.13) | copy-start | bytes 393220
  19.1 12.5 %collective-permute-start.7 = (f32[256,128]{1,0:T(8,128)S(1)}, f32[256,128]{1,0:T(8,128)S(1)}, u32[]{:S(2)}, u32[]{:S(2)}) collective-permute-start(f32[256,128]{1,0:T(8,128)S(1)} %get-tuple-element.67), channel_id=1, source_target_pairs={{0,28},{4,24},{8,20},{12,16},{16,12},{20,8},{24,4},{28,0},{1,29},{... | collective-permute-start | bytes 393224 | tf_op jit(solution)/shard_map/ppermute | solution.py:449
  20.7 10.8 %collective-permute-start.5 = (f32[5,48,128]{2,1,0:T(8,128)S(1)}, f32[5,48,128]{2,1,0:T(8,128)S(1)}, u32[]{:S(2)}, u32[]{:S(2)}) collective-permute-start(f32[5,48,128]{2,1,0:T(8,128)S(1)} %get-tuple-element.65), channel_id=1, source_target_pairs={{0,4},{4,0},{8,12},{12,8},{16,20},{20,16},{24,28},{28,24},{1,5},{5... | collective-permute-start | bytes 368648 | tf_op jit(solution)/shard_map/ppermute | solution.py:449
  20.7 10.8 %collective-permute-start.6 = (f32[5,48,128]{2,1,0:T(8,128)S(1)}, f32[5,48,128]{2,1,0:T(8,128)S(1)}, u32[]{:S(2)}, u32[]{:S(2)}) collective-permute-start(f32[5,48,128]{2,1,0:T(8,128)S(1)} %get-tuple-element.66), channel_id=1, source_target_pairs={{4,8},{8,4},{12,16},{16,12},{20,24},{24,20},{5,9},{9,5},{13,17},{1... | collective-permute-start | bytes 368648 | tf_op jit(solution)/shard_map/ppermute | solution.py:449
  24.2 5.7 %collective-permute-start.8 = (f32[5,8,128]{2,1,0:T(8,128)S(1)}, f32[5,8,128]{2,1,0:T(8,128)S(1)}, u32[]{:S(2)}, u32[]{:S(2)}) collective-permute-start(f32[5,8,128]{2,1,0:T(8,128)S(1)} %get-tuple-element.70), channel_id=1, source_target_pairs={{0,1},{1,2},{2,3},{3,0},{4,5},{5,6},{6,7},{7,4},{8,9},{9,10},{10,1... | collective-permute-start | bytes 61448 | tf_op jit(solution)/shard_map/ppermute | solution.py:450
  24.7 5.2 %collective-permute-start.9 = (f32[5,8,128]{2,1,0:T(8,128)S(1)}, f32[5,8,128]{2,1,0:T(8,128)S(1)}, u32[]{:S(2)}, u32[]{:S(2)}) collective-permute-start(f32[5,8,128]{2,1,0:T(8,128)S(1)} %get-tuple-element.71), channel_id=1, source_target_pairs={{1,0},{2,1},{3,2},{0,3},{5,4},{6,5},{7,6},{4,7},{9,8},{10,9},{11,1... | collective-permute-start | bytes 61448 | tf_op jit(solution)/shard_map/ppermute | solution.py:450

commit v5 on v4

--- a/solution.py
+++ b/solution.py
@@ -442,7 +442,7 @@
     core, chip, wake, span_low, span_high = sent
     n, s = lax.axis_size("wrap"), lax.axis_size("span")
     cores = [(i, i ^ 1) for i in range(n)]
-    chips = [pair for i in range(1, n - 1, 2) for pair in ((i, i + 1), (i + 1, i))]
+    chips = [pair for i in range(1, n, 2) for pair in ((i, (i + 1) % n), ((i + 1) % n, i))]
     mirror = [(i, n - 1 - i) for i in range(n)]
     ring_up = [(i, (i + 1) % s) for i in range(s)]
     ring_down = [((i + 1) % s, i) for i in range(s)]

time: 34.6 us -> 31.2 us (0.902)
  the two profiles are of different devices: /device:TPU:1 before, /device:TPU:0 now
where the time goes in v5:
time: 31.2 us; the launch traced here: 31.1 us
  Pallas kernels  16.3 us (52%)
  starting transfers between devices  14.6 us (47%)
    pallas_call x7, Pallas kernels, call(): pl.pallas_call(kernel, out_shape=outs, in_specs=specs or [whole] * len(in...  16.3 us
    ppermute x2, starting transfers between devices, exchange(): lax.ppermute(span_low, 'span', ring_down)  5 us
    ppermute x2, starting transfers between devices, exchange(): lax.ppermute(chip, 'wrap', chips)  4.23 us
    ppermute x2, starting transfers between devices, exchange(): lax.ppermute(span_high, 'span', ring_up)  2.64 us
    ppermute x2, starting transfers between devices, exchange(): lax.ppermute(wake, 'wrap', mirror)  2.21 us
  transfers between devices with their start and end apart: 10, of which 0 were waited for; matrix products, arithmetic and copies ran while one was open for 0% of the time, Pallas kernels for 28%

profile of v5, /device:TPU:0, one launch (start us, length us, event | category | flops | bytes accessed | tf_op | source)
XLA Modules:
  0.0 31.1 jit_solution(13923921605181128024)
XLA Ops:
  0.0 1.7 %prepare.1 = (f32[5,256,128]{2,1,0:T(8,128)S(1)}, f32[8,256,128]{2,1,0:T(8,128)S(1)}, f32[9,256,128]{2,1,0:T(8,128)S(1)}, f32[8,48,128]{2,1,0:T(8,128)S(1)}, f32...) custom-call(f32[256,128]{1,0:T(8,128)} %bitcast.13, ...), custom_call_target="tpu_custom_call" | custom-call | tf_op jit(solution)/shard_map/prepare/pallas_call | solution.py:464
  1.7 0.5 %collective-permute-start = (f32[8,48,128]{2,1,0:T(8,128)S(1)}, f32[8,48,128]{2,1,0:T(8,128)S(1)}, u32[]{:S(2)}, u32[]{:S(2)}) collective-permute-start(f32[8,48,128]{2,1,0:T(8,128)S(1)} %get-tuple-element.46), channel_id=1, source_target_pairs={{0,4},{4,0},{8,12},{12,8},{16,20},{20,16},{24,28},{28,24},{1,5},{5... | collective-permute-start | bytes 589832 | tf_op jit(solution)/shard_map/ppermute | solution.py:449
  2.2 3.6 %collective-permute-start.1 = (f32[8,48,128]{2,1,0:T(8,128)S(1)}, f32[8,48,128]{2,1,0:T(8,128)S(1)}, u32[]{:S(2)}, u32[]{:S(2)}) collective-permute-start(f32[8,48,128]{2,1,0:T(8,128)S(1)} %get-tuple-element.47), channel_id=1, source_target_pairs={{4,8},{8,4},{12,16},{16,12},{20,24},{24,20},{28,0},{0,28},{5,9},{9... | collective-permute-start | bytes 589832 | tf_op jit(solution)/shard_map/ppermute | solution.py:449
  5.8 0.0 collective-permute-start.2
  5.8 1.7 %collective-permute-start.3 = (f32[8,8,128]{2,1,0:T(8,128)S(1)}, f32[8,8,128]{2,1,0:T(8,128)S(1)}, u32[]{:S(2)}, u32[]{:S(2)}) collective-permute-start(f32[8,8,128]{2,1,0:T(8,128)S(1)} %get-tuple-element.51), channel_id=1, source_target_pairs={{0,1},{1,2},{2,3},{3,0},{4,5},{5,6},{6,7},{7,4},{8,9},{9,10},{10,1... | collective-permute-start | bytes 98312 | tf_op jit(solution)/shard_map/ppermute | solution.py:450
  7.5 2.1 %collective-permute-start.4 = (f32[8,8,128]{2,1,0:T(8,128)S(1)}, f32[8,8,128]{2,1,0:T(8,128)S(1)}, u32[]{:S(2)}, u32[]{:S(2)}) collective-permute-start(f32[8,8,128]{2,1,0:T(8,128)S(1)} %get-tuple-element.52), channel_id=1, source_target_pairs={{1,0},{2,1},{3,2},{0,3},{5,4},{6,5},{7,6},{4,7},{9,8},{10,9},{11,1... | collective-permute-start | bytes 98312 | tf_op jit(solution)/shard_map/ppermute | solution.py:450
  9.6 2.7 %early.2 = (f32[5,256,128]{2,1,0:T(8,128)S(1)}, f32[5,256,128]{2,1,0:T(8,128)S(1)}, f32[5,256,128]{2,1,0:T(8,128)S(1)}, f32[256,128]{1,0:T(8,128)S(1)}, f32[5,25...) custom-call(f32[5,256,128]{2,1,0:T(8,128)S(1)} %get-tuple-element.44, ...), custom_call_target="tpu_custom_call" | custom-call | flops 100000000 | bytes 25000000 | tf_op jit(solution)/shard_map/early/pallas_call | solution.py:464
  12.4 0.0 collective-permute-done.3.span_low_ref.met_low_ref
  12.4 0.0 collective-permute-done.4.span_high_ref.met_high_ref
  12.4 0.0 copy-start
  12.4 0.0 copy-start.1
  12.4 2.0 %span.2.refs_11_ = f32[5,256,128]{2,1,0:T(8,128)S(1)} custom-call(f32[8,256,128]{2,1,0:T(8,128)S(1)} %get-tuple-element.49.span_ref.span_met_ref, f32[8,256,128]{2,1,0:T(8,128)S(1)} %get-tuple-element.49.span_ref.span_met_ref, f32[8,8,128]{2,1,0:T(8,128)S(1)} %collective-permute-done.3.span_low_ref.met_low_ref, ...), custom_call_target="tpu_custom_call" | custom-call | flops 100000000 | bytes 25000000 | tf_op jit(solution)/shard_map/span/pallas_call | solution.py:464
  14.5 0.0 collective-permute-done.refs_5_.refs_7_
  14.5 2.9 %late.2 = (f32[5,256,128]{2,1,0:T(8,128)S(1)}, f32[5,256,128]{2,1,0:T(8,128)S(1)}, f32[5,48,128]{2,1,0:T(8,128)S(1)}, f32[5,48,128]{2,1,0:T(8,128)S(1)}, f32[256...) custom-call(f32[5,256,128]{2,1,0:T(8,128)S(1)} %get-tuple-element.44.state_ref.refs_0_.refs_19_, ...), custom_call_target="tpu_custom_call" | custom-call | flops 100000000 | bytes 25000000 | tf_op jit(solution)/shard_map/late/pallas_call | solution.py:464
  17.4 2.2 %collective-permute-start.7 = (f32[256,128]{1,0:T(8,128)S(1)}, f32[256,128]{1,0:T(8,128)S(1)}, u32[]{:S(2)}, u32[]{:S(2)}) collective-permute-start(f32[256,128]{1,0:T(8,128)S(1)} %get-tuple-element.67), channel_id=1, source_target_pairs={{0,28},{4,24},{8,20},{12,16},{16,12},{20,8},{24,4},{28,0},{1,29},{... | collective-permute-start | bytes 393224 | tf_op jit(solution)/shard_map/ppermute | solution.py:449
  19.6 0.7 %collective-permute-start.6 = (f32[5,48,128]{2,1,0:T(8,128)S(1)}, f32[5,48,128]{2,1,0:T(8,128)S(1)}, u32[]{:S(2)}, u32[]{:S(2)}) collective-permute-start(f32[5,48,128]{2,1,0:T(8,128)S(1)} %get-tuple-element.66), channel_id=1, source_target_pairs={{4,8},{8,4},{12,16},{16,12},{20,24},{24,20},{28,0},{0,28},{5,9},{9... | collective-permute-start | bytes 368648 | tf_op jit(solution)/shard_map/ppermute | solution.py:449
  20.3 0.9 %collective-permute-start.8 = (f32[5,8,128]{2,1,0:T(8,128)S(1)}, f32[5,8,128]{2,1,0:T(8,128)S(1)}, u32[]{:S(2)}, u32[]{:S(2)}) collective-permute-start(f32[5,8,128]{2,1,0:T(8,128)S(1)} %get-tuple-element.70), channel_id=1, source_target_pairs={{0,1},{1,2},{2,3},{3,0},{4,5},{5,6},{6,7},{7,4},{8,9},{9,10},{10,1... | collective-permute-start | bytes 61448 | tf_op jit(solution)/shard_map/ppermute | solution.py:450
  21.2 2.9 %collective-permute-start.9 = (f32[5,8,128]{2,1,0:T(8,128)S(1)}, f32[5,8,128]{2,1,0:T(8,128)S(1)}, u32[]{:S(2)}, u32[]{:S(2)}) collective-permute-start(f32[5,8,128]{2,1,0:T(8,128)S(1)} %get-tuple-element.71), channel_id=1, source_target_pairs={{1,0},{2,1},{3,2},{0,3},{5,4},{6,5},{7,6},{4,7},{9,8},{10,9},{11,1... | collective-permute-start | bytes 61448 | tf_op jit(solution)/shard_map/ppermute | solution.py:450
  24.1 2.4 %early.3 = (f32[5,256,128]{2,1,0:T(8,128)S(1)}, f32[5,256,128]{2,1,0:T(8,128)S(1)}, f32[5,256,128]{2,1,0:T(8,128)S(1)}, f32[256,128]{1,0:T(8,128)S(1)}, f32[5,25...) custom-call(f32[5,256,128]{2,1,0:T(8,128)S(1)} %get-tuple-element.64, ...), custom_call_target="tpu_custom_call" | custom-call | flops 100000000 | bytes 25000000 | tf_op jit(solution)/shard_map/early/pallas_call | solution.py:464
  26.5 0.0 collective-permute-done.9.span_high_ref
  26.5 1.5 %span.3.refs_11_ = f32[5,256,128]{2,1,0:T(8,128)S(1)} custom-call(f32[5,256,128]{2,1,0:T(8,128)S(1)} %get-tuple-element.68.span_ref, f32[8,256,128]{2,1,0:T(8,128)S(1)} %get-tuple-element.49.span_ref.span_met_ref, f32[5,8,128]{2,1,0:T(8,128)S(1)} %collective-permute-done.8.span_low_ref, f32[5,8,128]{2,1,0:T(8,128)S(1)} %collective-permute-done.9.span_high_ref, ...), custom_call_target="tpu_custom_call" | custom-call | flops 100000000 | bytes 25000000 | tf_op jit(solution)/shard_map/span/pallas_call | solution.py:464
  28.1 0.0 collective-permute-done.5.refs_5_
  28.1 0.0 collective-permute-done.7.refs_9_
  28.1 3.0 %late.3 = f32[5,256,128]{2,1,0:T(8,128)} custom-call(f32[5,256,128]{2,1,0:T(8,128)S(1)} %get-tuple-element.64.state_ref.refs_0_, f32[9,256,128]{2,1,0:T(8,128)S(1)} %get-tuple-element.45.met_ref.refs_1_, f32[256,128]{1,0:T(8,128)S(1)} %bitcast.8, s32[256,128]{1,0:T(8,128)S(1)} %bitcast.10, s32[16]{0:T(128)} %refs_4_.3, ...), custom_call_target="tpu_custom_call" | custom-call | flops 100000000 | bytes 25000000 | tf_op jit(solution)/shard_map/late/pallas_call | solution.py:464
  (7 shorter events, 0.0 us)
Async XLA Ops:
  1.7 12.8 %collective-permute-start = (f32[8,48,128]{2,1,0:T(8,128)S(1)}, f32[8,48,128]{2,1,0:T(8,128)S(1)}, u32[]{:S(2)}, u32[]{:S(2)}) collective-permute-start(f32[8,48,128]{2,1,0:T(8,128)S(1)} %get-tuple-element.46), channel_id=1, source_target_pairs={{0,4},{4,0},{8,12},{12,8},{16,20},{20,16},{24,28},{28,24},{1,5},{5... | collective-permute-start | bytes 589832 | tf_op jit(solution)/shard_map/ppermute | solution.py:449
  2.2 12.3 %collective-permute-start.1 = (f32[8,48,128]{2,1,0:T(8,128)S(1)}, f32[8,48,128]{2,1,0:T(8,128)S(1)}, u32[]{:S(2)}, u32[]{:S(2)}) collective-permute-start(f32[8,48,128]{2,1,0:T(8,128)S(1)} %get-tuple-element.47), channel_id=1, source_target_pairs={{4,8},{8,4},{12,16},{16,12},{20,24},{24,20},{28,0},{0,28},{5,9},{9... | collective-permute-start | bytes 589832 | tf_op jit(solution)/shard_map/ppermute | solution.py:449
  5.8 8.7 %collective-permute-start.2 = (f32[256,128]{1,0:T(8,128)S(1)}, f32[256,128]{1,0:T(8,128)S(1)}, u32[]{:S(2)}, u32[]{:S(2)}) collective-permute-start(f32[256,128]{1,0:T(8,128)S(1)} %get-tuple-element.48), channel_id=1, source_target_pairs={{0,28},{4,24},{8,20},{12,16},{16,12},{20,8},{24,4},{28,0},{1,29},{... | collective-permute-start | bytes 393224 | tf_op jit(solution)/shard_map/ppermute | solution.py:449
  5.8 6.6 %collective-permute-start.3 = (f32[8,8,128]{2,1,0:T(8,128)S(1)}, f32[8,8,128]{2,1,0:T(8,128)S(1)}, u32[]{:S(2)}, u32[]{:S(2)}) collective-permute-start(f32[8,8,128]{2,1,0:T(8,128)S(1)} %get-tuple-element.51), channel_id=1, source_target_pairs={{0,1},{1,2},{2,3},{3,0},{4,5},{5,6},{6,7},{7,4},{8,9},{9,10},{10,1... | collective-permute-start | bytes 98312 | tf_op jit(solution)/shard_map/ppermute | solution.py:450
  7.5 4.9 %collective-permute-start.4 = (f32[8,8,128]{2,1,0:T(8,128)S(1)}, f32[8,8,128]{2,1,0:T(8,128)S(1)}, u32[]{:S(2)}, u32[]{:S(2)}) collective-permute-start(f32[8,8,128]{2,1,0:T(8,128)S(1)} %get-tuple-element.52), channel_id=1, source_target_pairs={{1,0},{2,1},{3,2},{0,3},{5,4},{6,5},{7,6},{4,7},{9,8},{10,9},{11,1... | collective-permute-start | bytes 98312 | tf_op jit(solution)/shard_map/ppermute | solution.py:450
  12.4 2.1 %copy-start = (f32[16,16,128]{2,1,0:T(8,128)S(1)}, f32[16,16,128]{2,1,0:T(8,128)}, u32[]{:S(2)}) copy-start(f32[16,16,128]{2,1,0:T(8,128)} %param.11) | copy-start | bytes 393220
  12.4 2.1 %copy-start.1 = (s32[16,16,128]{2,1,0:T(8,128)S(1)}, s32[16,16,128]{2,1,0:T(8,128)}, u32[]{:S(2)}) copy-start(s32[16,16,128]{2,1,0:T(8,128)} %param.13) | copy-start | bytes 393220
  17.4 10.7 %collective-permute-start.7 = (f32[256,128]{1,0:T(8,128)S(1)}, f32[256,128]{1,0:T(8,128)S(1)}, u32[]{:S(2)}, u32[]{:S(2)}) collective-permute-start(f32[256,128]{1,0:T(8,128)S(1)} %get-tuple-element.67), channel_id=1, source_target_pairs={{0,28},{4,24},{8,20},{12,16},{16,12},{20,8},{24,4},{28,0},{1,29},{... | collective-permute-start | bytes 393224 | tf_op jit(solution)/shard_map/ppermute | solution.py:449
  19.6 8.5 %collective-permute-start.5 = (f32[5,48,128]{2,1,0:T(8,128)S(1)}, f32[5,48,128]{2,1,0:T(8,128)S(1)}, u32[]{:S(2)}, u32[]{:S(2)}) collective-permute-start(f32[5,48,128]{2,1,0:T(8,128)S(1)} %get-tuple-element.65), channel_id=1, source_target_pairs={{0,4},{4,0},{8,12},{12,8},{16,20},{20,16},{24,28},{28,24},{1,5},{5... | collective-permute-start | bytes 368648 | tf_op jit(solution)/shard_map/ppermute | solution.py:449
  19.6 8.5 %collective-permute-start.6 = (f32[5,48,128]{2,1,0:T(8,128)S(1)}, f32[5,48,128]{2,1,0:T(8,128)S(1)}, u32[]{:S(2)}, u32[]{:S(2)}) collective-permute-start(f32[5,48,128]{2,1,0:T(8,128)S(1)} %get-tuple-element.66), channel_id=1, source_target_pairs={{4,8},{8,4},{12,16},{16,12},{20,24},{24,20},{28,0},{0,28},{5,9},{9... | collective-permute-start | bytes 368648 | tf_op jit(solution)/shard_map/ppermute | solution.py:449
  20.3 6.2 %collective-permute-start.8 = (f32[5,8,128]{2,1,0:T(8,128)S(1)}, f32[5,8,128]{2,1,0:T(8,128)S(1)}, u32[]{:S(2)}, u32[]{:S(2)}) collective-permute-start(f32[5,8,128]{2,1,0:T(8,128)S(1)} %get-tuple-element.70), channel_id=1, source_target_pairs={{0,1},{1,2},{2,3},{3,0},{4,5},{5,6},{6,7},{7,4},{8,9},{9,10},{10,1... | collective-permute-start | bytes 61448 | tf_op jit(solution)/shard_map/ppermute | solution.py:450
  21.2 5.3 %collective-permute-start.9 = (f32[5,8,128]{2,1,0:T(8,128)S(1)}, f32[5,8,128]{2,1,0:T(8,128)S(1)}, u32[]{:S(2)}, u32[]{:S(2)}) collective-permute-start(f32[5,8,128]{2,1,0:T(8,128)S(1)} %get-tuple-element.71), channel_id=1, source_target_pairs={{1,0},{2,1},{3,2},{0,3},{5,4},{6,5},{7,6},{4,7},{9,8},{10,9},{11,1... | collective-permute-start | bytes 61448 | tf_op jit(solution)/shard_map/ppermute | solution.py:450

commit v6 on v5

--- a/solution.py
+++ b/solution.py
@@ -174,7 +174,7 @@
 def send_parts(state_ref, span_ref, fields, outs, dims):
     rows_i, height = dims
     total = rows_i * rows_i
-    core_ref, chip_ref, wake_ref, span_low_ref, span_high_ref = outs
+    core_ref, chip_ref, wake_ref, span_near_ref, span_far_ref = outs
     even = lax.rem(lax.axis_index("wrap"), 2) == 0
     edge = H * rows_i
     to_core, to_chip = jnp.where(even, total - edge, 0), jnp.where(even, 0, total - edge)
@@ -183,11 +183,13 @@
         chip_ref[f] = state_ref[f, aligned(to_chip, edge), :]
         for r in range(H):
             wake_ref[pl.ds(f * H + r, rows_i, stride=16), :] = state_ref[f, pl.ds(r + 1, rows_i, stride=rows_i), :]
+    even = lax.rem(lax.axis_index("span"), 2) == 0
     for f in range(fields):
         for r in range(H):
-            span_low_ref[f, 2 * r : 2 * r + 2, :] = span_ref[f, r * 8 : r * 8 + 2, :]
             top = (height - H + r) * 8
-            span_high_ref[f, 2 * r : 2 * r + 2, :] = span_ref[f, top + 6 : top + 8, :]
+            low, high = span_ref[f, r * 8 : r * 8 + 2, :], span_ref[f, top + 6 : top + 8, :]
+            span_near_ref[f, 2 * r : 2 * r + 2, :] = jnp.where(even, high, low)
+            span_far_ref[f, 2 * r : 2 * r + 2, :] = jnp.where(even, low, high)
 
 
 def prepare_kernel(dims, rho_hbm, vel_hbm, pre_hbm, met_hbm, state_ref, span_ref, met_ref, *refs):
@@ -275,74 +277,10 @@
     lax.fori_loop(0, 5, normal, 0)
 
 
-def span_kernel(dims, kind, span_ref, span_met_ref, span_low_ref, span_high_ref, met_low_ref, met_high_ref,
-                plus_k, minus_k, metric_k, diffused_k, out_ref,
-                acc_ref, halo_plus, halo_minus, halo_metric, halo_diffused, pad_ref):
-    rows_i, height = dims
-    sublane = lax.broadcasted_iota(jnp.int32, (8, 128), 0)
-    halo_diffused[0] = jnp.zeros(halo_diffused.shape[1:], F32)
-    for r in range(H):
-        for f in range(8):
-            low, high = (span_low_ref, span_high_ref) if f < 5 else (met_low_ref, met_high_ref)
-            pad_ref[f, r * 8 : r * 8 + 2, :] = low[f, 2 * r : 2 * r + 2, :]
-            pad_ref[f, (H + r) * 8 + 6 : (H + r) * 8 + 8, :] = high[f, 2 * r : 2 * r + 2, :]
-    for r in range(2 * H):
-        rows = slice(r * 8, r * 8 + 8)
-        values = []
-        for f in range(8):
-            ref = span_ref if f < 5 else span_met_ref
-            if r < H:
-                own = pltpu.roll(ref[f, (height - H + r) * 8 : (height - H + r) * 8 + 8, :], 2, 0)
-                values.append(jnp.where(sublane < 2, pad_ref[f, rows, :], own))
-            else:
-                own = pltpu.roll(ref[f, (r - H) * 8 : (r - H) * 8 + 8, :], 6, 0)
-                values.append(jnp.where(sublane >= 6, pad_ref[f, rows, :], own))
-        prims = primitives(values[:5])
-        put_diffused(halo_diffused, rows, prims)
-        put((halo_plus, halo_minus, halo_metric), rows,
-            *point_fluxes(values[:5], prims, [unit(2, m, values[5 + m]) for m in range(3)]))
-
-    def sweep_span(f, carry):
-        def loader(ref, halo, lead):
-            def one(n):
-                if 0 <= n < height:
-                    return ref[lead + (slice(n * 8, n * 8 + 8),)]
-                r = n + H if n < 0 else n - height + H
-                return halo[lead + (slice(r * 8, r * 8 + 8),)]
-
-            return lambda n: jnp.concatenate([one(n), one(n + height // 2)], axis=0)
-
-        def store(n, value):
-            acc_ref[f, n * 8 : n * 8 + 8, :] = value[:8]
-            m = n + height // 2
-            acc_ref[f, m * 8 : m * 8 + 8, :] = value[8:]
-
-        sweep(kind, loader(plus_k, halo_plus, (f,)), loader(minus_k, halo_minus, (f,)), loader(diffused_k, halo_diffused, (f,)),
-              loader(metric_k, halo_metric, ()), store, -1, height // 2 - 1)
-        return carry
-
-    lax.fori_loop(0, 5, sweep_span, 0)
-    for f in range(5):
-        for half in range(2):
-            parts = [acc_ref[f, pl.ds(q * 2 + half, height, stride=8), :] for q in range(4)]
-            out_ref[f, half * 128 : (half + 1) * 128, :] = jnp.concatenate(parts, axis=0).T
-
-
-def late_kernel(dims, kind, final, *refs):
+def chord_kernel(dims, kind, state_ref, met_ref, core_ref, chip_ref, met_core_ref, met_chip_ref, normal_ref,
+                 plus_i, minus_i, metric_i, diffused_ref, acc_ref, halo_plus, halo_minus, halo_metric, halo_diffused):
     rows_i, height = dims
     total = rows_i * rows_i
-    (state_ref, met_ref, vol_ref, blank_ref, partner_hbm, core_ref, chip_ref, met_core_ref, met_chip_ref, wake_ref,
-     normal_ref, span_acc_ref, plus_i, minus_i, metric_i, plus_j, minus_j, metric_j, diffused_ref) = refs[:19]
-    refs = refs[19:]
-    if final:
-        start_ref, out_ref = refs[:2]
-        refs = refs[2:]
-    else:
-        out_ref, out_span_ref = refs[:2]
-        outs, refs = refs[2:7], refs[7:]
-    acc_ref, halo_plus, halo_minus, halo_metric, halo_diffused, ghost_ref, partner_ref, sem = refs
-    fetch = pltpu.make_async_copy(partner_hbm, partner_ref, sem)
-    fetch.start()
     position, count = lax.axis_index("wrap"), lax.axis_size("wrap")
     even = lax.rem(position, 2) == 0
     at_end = (position == 0) | (position == count - 1)
@@ -379,13 +317,80 @@
 
         def store(n, value):
             rows = aligned(n * rows_i, rows_i)
-            acc_ref[f, rows, :] = value + (normal_ref[f, rows, :] + span_acc_ref[f, rows, :])
+            acc_ref[f, rows, :] = value + normal_ref[f, rows, :]
 
         sweep(kind, loader(plus_i, halo_plus, (f,)), loader(minus_i, halo_minus, (f,)), loader(diffused_ref, halo_diffused, (f,)),
               loader(metric_i, halo_metric, ()), store, -1, rows_i - 1)
         return carry
 
     lax.fori_loop(0, 5, chord, 0)
+
+
+def span_kernel(dims, kind, final, *refs):
+    rows_i, height = dims
+    (span_ref, span_met_ref, span_near_ref, span_far_ref, met_near_ref, met_far_ref, plus_k, minus_k, metric_k, diffused_k,
+     partner_hbm, state_ref, met_ref, vol_ref, blank_ref, wake_ref, plane_ref, plus_j, minus_j, metric_j,
+     diffused_ref) = refs[:21]
+    refs = refs[21:]
+    if final:
+        start_ref, out_ref = refs[:2]
+        refs = refs[2:]
+    else:
+        out_ref, out_span_ref = refs[:2]
+        outs, refs = refs[2:7], refs[7:]
+    (acc_ref, halo_plus, halo_minus, halo_metric, halo_diffused, pad_ref, wall_ref, sum_ref,
+     ghost_plus, ghost_minus, ghost_metric, ghost_diffused, ghost_ref, partner_ref, sem) = refs[:15]
+    if final:
+        staged_ref, out_sems = refs[15:]
+    fetch = pltpu.make_async_copy(partner_hbm, partner_ref, sem)
+    fetch.start()
+    position, count = lax.axis_index("wrap"), lax.axis_size("wrap")
+    ghost_diffused[0] = jnp.zeros(ghost_diffused.shape[1:], F32)
+    even = lax.rem(lax.axis_index("span"), 2) == 0
+    sublane = lax.broadcasted_iota(jnp.int32, (8, 128), 0)
+    halo_diffused[0] = jnp.zeros(halo_diffused.shape[1:], F32)
+    for r in range(H):
+        for f in range(8):
+            near_ref, far_ref = (span_near_ref, span_far_ref) if f < 5 else (met_near_ref, met_far_ref)
+            near, far = near_ref[f, 2 * r : 2 * r + 2, :], far_ref[f, 2 * r : 2 * r + 2, :]
+            pad_ref[f, r * 8 : r * 8 + 2, :] = jnp.where(even, far, near)
+            pad_ref[f, (H + r) * 8 + 6 : (H + r) * 8 + 8, :] = jnp.where(even, near, far)
+    for r in range(2 * H):
+        rows = slice(r * 8, r * 8 + 8)
+        values = []
+        for f in range(8):
+            ref = span_ref if f < 5 else span_met_ref
+            if r < H:
+                own = pltpu.roll(ref[f, (height - H + r) * 8 : (height - H + r) * 8 + 8, :], 2, 0)
+                values.append(jnp.where(sublane < 2, pad_ref[f, rows, :], own))
+            else:
+                own = pltpu.roll(ref[f, (r - H) * 8 : (r - H) * 8 + 8, :], 6, 0)
+                values.append(jnp.where(sublane >= 6, pad_ref[f, rows, :], own))
+        prims = primitives(values[:5])
+        put_diffused(halo_diffused, rows, prims)
+        put((halo_plus, halo_minus, halo_metric), rows,
+            *point_fluxes(values[:5], prims, [unit(2, m, values[5 + m]) for m in range(3)]))
+
+    def sweep_span(f, carry):
+        def loader(ref, halo, lead):
+            def one(n):
+                if 0 <= n < height:
+                    return ref[lead + (slice(n * 8, n * 8 + 8),)]
+                r = n + H if n < 0 else n - height + H
+                return halo[lead + (slice(r * 8, r * 8 + 8),)]
+
+            return lambda n: jnp.concatenate([one(n), one(n + height // 2)], axis=0)
+
+        def store(n, value):
+            acc_ref[f, n * 8 : n * 8 + 8, :] = value[:8]
+            m = n + height // 2
+            acc_ref[f, m * 8 : m * 8 + 8, :] = value[8:]
+
+        sweep(kind, loader(plus_k, halo_plus, (f,)), loader(minus_k, halo_minus, (f,)), loader(diffused_k, halo_diffused, (f,)),
+              loader(metric_k, halo_metric, ()), store, -1, height // 2 - 1)
+        return carry
+
+    lax.fori_loop(0, 5, sweep_span, 0)
 
     fetch.wait()
     base = (count - 1 - position) * rows_i
@@ -396,8 +401,8 @@
         state = [ghost_ref[pl.ds(f * H + r, rows_i, stride=16), :] for f in range(5)]
         prims = primitives(state)
         to = slice(r * rows_i, (r + 1) * rows_i)
-        put_diffused(halo_diffused, to, prims)
-        put((halo_plus, halo_minus, halo_metric), to,
+        put_diffused(ghost_diffused, to, prims)
+        put((ghost_plus, ghost_minus, ghost_metric), to,
             *point_fluxes(state, prims, [unit(1, m, met_ref[3 + m, wall, :]) for m in range(3)]))
 
     def normal(f, carry):
@@ -413,9 +418,9 @@
             return load
 
         def store(n, value):
-            acc_ref[f, rows(n), :] = acc_ref[f, rows(n), :] + value
-
-        sweep(kind, loader(plus_j, halo_plus, (f,)), loader(minus_j, halo_minus, (f,)), loader(diffused_ref, halo_diffused, (f,)),
+            wall_ref[f, n * rows_i : (n + 1) * rows_i, :] = value
+
+        sweep(kind, loader(plus_j, ghost_plus, (f,)), loader(minus_j, ghost_minus, (f,)), loader(diffused_ref, ghost_diffused, (f,)),
               lambda n: metric_j[rows(max(n, 0)), :], store, -1, 1, open_high=True)
         return carry
 
@@ -423,8 +428,22 @@
 
     scale = (time_step / 12.0) * blank_ref[...].astype(F32) / vol_ref[...]
     for f in range(5):
-        moved = state_ref[f] + scale * acc_ref[f]
-        out_ref[f] = 0.5 * start_ref[f] + 0.5 * moved if final else moved
+        for half in range(2):
+            parts = [acc_ref[f, pl.ds(q * 2 + half, height, stride=8), :] for q in range(4)]
+            rows = slice(half * 128, (half + 1) * 128)
+            sum_ref[f, rows, :] = plane_ref[f, rows, :] + jnp.concatenate(parts, axis=0).T
+        for n in range(H):
+            rows = pl.ds(n, rows_i, stride=rows_i)
+            sum_ref[f, rows, :] = sum_ref[f, rows, :] + wall_ref[f, n * rows_i : (n + 1) * rows_i, :]
+        moved = state_ref[f] + scale * sum_ref[f]
+        if final:
+            staged_ref[f] = 0.5 * start_ref[f] + 0.5 * moved
+            pltpu.make_async_copy(staged_ref.at[f], out_ref.at[f], out_sems.at[f]).start()
+        else:
+            out_ref[f] = moved
+    if final:
+        for f in range(5):
+            pltpu.make_async_copy(staged_ref.at[f], out_ref.at[f], out_sems.at[f]).wait()
     if not final:
         for f in range(5):
             def store(start, block, f=f):
@@ -439,15 +458,15 @@
 
 
 def exchange(sent):
-    core, chip, wake, span_low, span_high = sent
+    core, chip, wake, span_near, span_far = sent
     n, s = lax.axis_size("wrap"), lax.axis_size("span")
     cores = [(i, i ^ 1) for i in range(n)]
     chips = [pair for i in range(1, n, 2) for pair in ((i, (i + 1) % n), ((i + 1) % n, i))]
     mirror = [(i, n - 1 - i) for i in range(n)]
-    ring_up = [(i, (i + 1) % s) for i in range(s)]
-    ring_down = [((i + 1) % s, i) for i in range(s)]
+    near = [(i, i ^ 1) for i in range(s)]
+    far = [pair for i in range(1, s, 2) for pair in ((i, (i + 1) % s), ((i + 1) % s, i))]
     return (lax.ppermute(core, "wrap", cores), lax.ppermute(chip, "wrap", chips), lax.ppermute(wake, "wrap", mirror),
-            lax.ppermute(span_high, "span", ring_up), lax.ppermute(span_low, "span", ring_down))
+            lax.ppermute(span_near, "span", near), lax.ppermute(span_far, "span", far))
 
 
 def body(density, velocity, pressure, metrics, volume, wake_partner, iblank):
@@ -460,12 +479,12 @@
     wake_partner = pltpu.with_memory_space_constraint(wake_partner, pltpu.HBM)
     params = pltpu.CompilerParams(vmem_limit_bytes=16 * 2**20)
 
-    def call(kernel, name, ins, outs, scratch, specs=None, cost=0):
+    def call(kernel, name, ins, outs, scratch, specs=None, cost=0, out_specs=None):
         return pl.pallas_call(
             kernel,
             out_shape=outs,
             in_specs=specs or [whole] * len(ins),
-            out_specs=[whole] * len(outs),
+            out_specs=out_specs or [whole] * len(outs),
             scratch_shapes=scratch,
             compiler_params=params,
             cost_estimate=pl.CostEstimate(flops=cost, bytes_accessed=cost // 4, transcendentals=0),
@@ -498,9 +517,9 @@
     start = state
     for final in (False, True):
         kind = jnp.bfloat16 if final else F32
-        core, chip, wake, span_low, span_high = exchange(sent)
+        core, chip, wake, span_near, span_far = exchange(sent)
         if metric_halo is None:
-            metric_halo = core, chip, span_low, span_high
+            metric_halo = core, chip, span_near, span_far
         line, span_line = shape(5, total, lanes), shape(5, span_rows, lanes)
         normal, *lines = call(
             functools.partial(early_kernel, dims, kind), "early", (state, span, span_met, met),
@@ -509,23 +528,23 @@
             [], cost=10**8,
         )
         plus_i, minus_i, metric_i, plus_j, minus_j, metric_j, diffused = lines[:7]
-        (span_acc,) = call(
-            functools.partial(span_kernel, dims, kind), "span",
-            (span, span_met, span_low, span_high, metric_halo[2], metric_halo[3], *lines[7:]),
-            [field],
-            [pltpu.VMEM((5, span_rows, lanes), F32)] + halo_scratch(2 * H * 8) + [pltpu.VMEM((8, 2 * H * 8, lanes), F32)],
-            cost=10**8,
+        (plane,) = call(
+            functools.partial(chord_kernel, dims, kind), "chord",
+            (state, met, core, chip, metric_halo[0], metric_halo[1], normal, plus_i, minus_i, metric_i, diffused),
+            [field], halo_scratch(halo), cost=10**8,
         )
-        ins = (state, met, volume, blank, wake_partner, core, chip, metric_halo[0], metric_halo[1], wake, normal, span_acc,
-               plus_i, minus_i, metric_i, plus_j, minus_j, metric_j, diffused)
+        ins = (span, span_met, span_near, span_far, metric_halo[2], metric_halo[3], *lines[7:], wake_partner, state, met,
+               volume, blank, wake, plane, plus_j, minus_j, metric_j, diffused)
         ins += (start,) if final else ()
         state, *rest = call(
-            functools.partial(late_kernel, dims, kind, final), "late", ins,
+            functools.partial(span_kernel, dims, kind, final), "span", ins,
             [field] if final else [field, field] + parts(5),
-            [pltpu.VMEM((5, total, lanes), F32)] + halo_scratch(halo) + [pltpu.VMEM((rows_i * 16, lanes), F32)]
-            + [pltpu.SMEM((rows_i,), jnp.int32), pltpu.SemaphoreType.DMA],
-            [whole] * 4 + [far] + [whole] * (len(ins) - 5),
-            cost=10**8,
+            [pltpu.VMEM((5, span_rows, lanes), F32)] + halo_scratch(2 * H * 8) + [pltpu.VMEM((8, 2 * H * 8, lanes), F32)]
+            + [pltpu.VMEM((5, H * rows_i, lanes), F32), pltpu.VMEM((5, total, lanes), F32)] + halo_scratch(H * rows_i)
+            + [pltpu.VMEM((rows_i * 16, lanes), F32), pltpu.SMEM((rows_i,), jnp.int32), pltpu.SemaphoreType.DMA]
+            + ([pltpu.VMEM((5, total, lanes), F32), pltpu.SemaphoreType.DMA((5,))] if final else []),
+            [whole] * 10 + [far] + [whole] * (len(ins) - 11),
+            cost=10**8, out_specs=[far] if final else None,
         )
         if not final:
             span, *sent = rest

time: 31.2 us -> 30.8 us (0.987)
    ppermute x2, starting transfers between devices: 2.21 us -> 0.75 us  [exchange(): lax.ppermute(wake, 'wrap', mirror)]
    ppermute x2, starting transfers between devices: 4.23 us -> 5.55 us  [exchange(): lax.ppermute(chip, 'wrap', chips)]
  transfers between devices with their start and end apart: 10 -> 10, of which waited for: 0 -> 0; matrix products, arithmetic and copies ran while one was open for 0% -> 0% of each run, Pallas kernels for 28% -> 27%
where the time goes in v6:
time: 30.8 us; the launch traced here: 30.7 us
  Pallas kernels  16.1 us (52%)
  starting transfers between devices  14.4 us (47%)
    pallas_call x7, Pallas kernels, call(): pl.pallas_call(kernel, out_shape=outs, in_specs=specs or [whole] * len(in...  16.1 us
    ppermute x2, starting transfers between devices, exchange(): lax.ppermute(chip, 'wrap', chips)  5.55 us
    ppermute x2, starting transfers between devices, exchange(): lax.ppermute(span_far, 'span', far)  4.95 us
    ppermute x2, starting transfers between devices, exchange(): lax.ppermute(span_near, 'span', near)  2.53 us
    ppermute x2, starting transfers between devices, exchange(): lax.ppermute(wake, 'wrap', mirror)  0.75 us
  transfers between devices with their start and end apart: 10, of which 0 were waited for; matrix products, arithmetic and copies ran while one was open for 0% of the time, Pallas kernels for 27%

profile of v6, /device:TPU:0, one launch (start us, length us, event | category | flops | bytes accessed | tf_op | source)
XLA Modules:
  0.0 30.7 jit_solution(9292523911999626749)
XLA Ops:
  0.0 1.7 %prepare.1 = (f32[5,256,128]{2,1,0:T(8,128)S(1)}, f32[8,256,128]{2,1,0:T(8,128)S(1)}, f32[9,256,128]{2,1,0:T(8,128)S(1)}, f32[8,48,128]{2,1,0:T(8,128)S(1)}, f32...) custom-call(f32[256,128]{1,0:T(8,128)} %bitcast.13, ...), custom_call_target="tpu_custom_call" | custom-call | tf_op jit(solution)/shard_map/prepare/pallas_call | solution.py:483
  1.7 0.5 %collective-permute-start.3 = (f32[8,48,128]{2,1,0:T(8,128)S(1)}, f32[8,48,128]{2,1,0:T(8,128)S(1)}, u32[]{:S(2)}, u32[]{:S(2)}) collective-permute-start(f32[8,48,128]{2,1,0:T(8,128)S(1)} %get-tuple-element.54), channel_id=1, source_target_pairs={{0,4},{4,0},{8,12},{12,8},{16,20},{20,16},{24,28},{28,24},{1,5},{5... | collective-permute-start | bytes 589832 | tf_op jit(solution)/shard_map/ppermute | solution.py:468
  2.2 3.6 %collective-permute-start.4 = (f32[8,48,128]{2,1,0:T(8,128)S(1)}, f32[8,48,128]{2,1,0:T(8,128)S(1)}, u32[]{:S(2)}, u32[]{:S(2)}) collective-permute-start(f32[8,48,128]{2,1,0:T(8,128)S(1)} %get-tuple-element.55), channel_id=1, source_target_pairs={{4,8},{8,4},{12,16},{16,12},{20,24},{24,20},{28,0},{0,28},{5,9},{9... | collective-permute-start | bytes 589832 | tf_op jit(solution)/shard_map/ppermute | solution.py:468
  5.8 0.0 collective-permute-start.2
  5.8 1.7 %collective-permute-start = (f32[8,8,128]{2,1,0:T(8,128)S(1)}, f32[8,8,128]{2,1,0:T(8,128)S(1)}, u32[]{:S(2)}, u32[]{:S(2)}) collective-permute-start(f32[8,8,128]{2,1,0:T(8,128)S(1)} %get-tuple-element.45), channel_id=1, source_target_pairs={{0,1},{1,0},{2,3},{3,2},{4,5},{5,4},{6,7},{7,6},{8,9},{9,8},{10,11... | collective-permute-start | bytes 98312 | tf_op jit(solution)/shard_map/ppermute | solution.py:469
  7.5 2.5 %collective-permute-start.1 = (f32[8,8,128]{2,1,0:T(8,128)S(1)}, f32[8,8,128]{2,1,0:T(8,128)S(1)}, u32[]{:S(2)}, u32[]{:S(2)}) collective-permute-start(f32[8,8,128]{2,1,0:T(8,128)S(1)} %get-tuple-element.46), channel_id=1, source_target_pairs={{1,2},{2,1},{3,0},{0,3},{5,6},{6,5},{7,4},{4,7},{9,10},{10,9},{11,... | collective-permute-start | bytes 98312 | tf_op jit(solution)/shard_map/ppermute | solution.py:469
  10.0 2.7 %early.2 = (f32[5,256,128]{2,1,0:T(8,128)S(1)}, f32[5,256,128]{2,1,0:T(8,128)S(1)}, f32[5,256,128]{2,1,0:T(8,128)S(1)}, f32[256,128]{1,0:T(8,128)S(1)}, f32[5,25...) custom-call(f32[5,256,128]{2,1,0:T(8,128)S(1)} %get-tuple-element.47, ...), custom_call_target="tpu_custom_call" | custom-call | flops 100000000 | bytes 25000000 | tf_op jit(solution)/shard_map/early/pallas_call | solution.py:483
  12.7 0.0 collective-permute-done.4.chip_ref.met_chip_ref
  12.7 0.0 copy-start
  12.7 0.0 copy-start.1
  12.7 1.9 %chord.2.refs_16_ = f32[5,256,128]{2,1,0:T(8,128)S(1)} custom-call(f32[5,256,128]{2,1,0:T(8,128)S(1)} %get-tuple-element.47.state_ref.refs_11_.refs_21_, f32[9,256,128]{2,1,0:T(8,128)S(1)} %get-tuple-element.48.met_ref.refs_12_, f32[8,48,128]{2,1,0:T(8,128)S(1)} %collective-permute-done.3.core_ref.met_core_ref, ...), custom_call_target="tpu_custom_call" | custom-call | flops 100000000 | bytes 25000000 | tf_op jit(solution)/shard_map/chord/pallas_call | solution.py:483
  14.6 0.0 collective-permute-done.1.refs_3_.refs_5_
  14.6 0.0 collective-permute-done.2.refs_15_
  14.7 3.1 %span.2 = (f32[5,256,128]{2,1,0:T(8,128)S(1)}, f32[5,256,128]{2,1,0:T(8,128)S(1)}, f32[5,48,128]{2,1,0:T(8,128)S(1)}, f32[5,48,128]{2,1,0:T(8,128)S(1)}, f32[256...) custom-call(f32[8,256,128]{2,1,0:T(8,128)S(1)} %get-tuple-element.44.span_ref.span_met_ref.refs_0_.refs_1_, ...), custom_call_target="tpu_custom_call" | custom-call | flops 100000000 | bytes 25000000 | tf_op jit(solution)/shard_map/span/pallas_call | solution.py:483
  17.7 0.1 collective-permute-start.8
  17.8 2.0 %collective-permute-start.9 = (f32[5,48,128]{2,1,0:T(8,128)S(1)}, f32[5,48,128]{2,1,0:T(8,128)S(1)}, u32[]{:S(2)}, u32[]{:S(2)}) collective-permute-start(f32[5,48,128]{2,1,0:T(8,128)S(1)} %get-tuple-element.74), channel_id=1, source_target_pairs={{4,8},{8,4},{12,16},{16,12},{20,24},{24,20},{28,0},{0,28},{5,9},{9... | collective-permute-start | bytes 368648 | tf_op jit(solution)/shard_map/ppermute | solution.py:468
  19.8 0.7 %collective-permute-start.7 = (f32[256,128]{1,0:T(8,128)S(1)}, f32[256,128]{1,0:T(8,128)S(1)}, u32[]{:S(2)}, u32[]{:S(2)}) collective-permute-start(f32[256,128]{1,0:T(8,128)S(1)} %get-tuple-element.72), channel_id=1, source_target_pairs={{0,28},{4,24},{8,20},{12,16},{16,12},{20,8},{24,4},{28,0},{1,29},{... | collective-permute-start | bytes 393224 | tf_op jit(solution)/shard_map/ppermute | solution.py:468
  20.5 0.8 %collective-permute-start.5 = (f32[5,8,128]{2,1,0:T(8,128)S(1)}, f32[5,8,128]{2,1,0:T(8,128)S(1)}, u32[]{:S(2)}, u32[]{:S(2)}) collective-permute-start(f32[5,8,128]{2,1,0:T(8,128)S(1)} %get-tuple-element.65), channel_id=1, source_target_pairs={{0,1},{1,0},{2,3},{3,2},{4,5},{5,4},{6,7},{7,6},{8,9},{9,8},{10,11... | collective-permute-start | bytes 61448 | tf_op jit(solution)/shard_map/ppermute | solution.py:469
  21.3 2.5 %collective-permute-start.6 = (f32[5,8,128]{2,1,0:T(8,128)S(1)}, f32[5,8,128]{2,1,0:T(8,128)S(1)}, u32[]{:S(2)}, u32[]{:S(2)}) collective-permute-start(f32[5,8,128]{2,1,0:T(8,128)S(1)} %get-tuple-element.66), channel_id=1, source_target_pairs={{1,2},{2,1},{3,0},{0,3},{5,6},{6,5},{7,4},{4,7},{9,10},{10,9},{11,... | collective-permute-start | bytes 61448 | tf_op jit(solution)/shard_map/ppermute | solution.py:469
  23.8 2.4 %early.3 = (f32[5,256,128]{2,1,0:T(8,128)S(1)}, f32[5,256,128]{2,1,0:T(8,128)S(1)}, f32[5,256,128]{2,1,0:T(8,128)S(1)}, f32[256,128]{1,0:T(8,128)S(1)}, f32[5,25...) custom-call(f32[5,256,128]{2,1,0:T(8,128)S(1)} %get-tuple-element.67, ...), custom_call_target="tpu_custom_call" | custom-call | flops 100000000 | bytes 25000000 | tf_op jit(solution)/shard_map/early/pallas_call | solution.py:483
  26.3 0.0 collective-permute-done.8.core_ref
  26.3 0.0 collective-permute-done.9.chip_ref
  26.3 1.4 %chord.3.refs_16_ = f32[5,256,128]{2,1,0:T(8,128)S(1)} custom-call(f32[5,256,128]{2,1,0:T(8,128)S(1)} %get-tuple-element.67.state_ref.refs_11_, f32[9,256,128]{2,1,0:T(8,128)S(1)} %get-tuple-element.48.met_ref.refs_12_, f32[5,48,128]{2,1,0:T(8,128)S(1)} %collective-permute-done.8.core_ref, f32[5,48,128]{2,1,0:T(8,128)S(1)} %collective-permute-done.9.chip_ref, ...), custom_call_target="tpu_custom_call" | custom-call | flops 100000000 | bytes 25000000 | tf_op jit(solution)/shard_map/chord/pallas_call | solution.py:483
  27.7 2.9 %span.3 = f32[5,256,128]{2,1,0:T(8,128)} custom-call(f32[5,256,128]{2,1,0:T(8,128)S(1)} %get-tuple-element.64.span_ref.refs_0_, f32[8,256,128]{2,1,0:T(8,128)S(1)} %get-tuple-element.44.span_ref.span_met_ref.refs_0_.refs_1_, f32[5,8,128]{2,1,0:T(8,128)S(1)} %collective-permute-done.5.refs_2_, f32[5,8,128]{2,1,0:T(8,128)S(1)} %collective-permute-done.6.refs_3_, ...), custom_call_target="tpu_custom_call" | custom-call | flops 100000000 | bytes 25000000 | tf_op jit(solution)/shard_map/span/pallas_call | solution.py:483
  (7 shorter events, 0.0 us)
Async XLA Ops:
  1.7 11.0 %collective-permute-start.3 = (f32[8,48,128]{2,1,0:T(8,128)S(1)}, f32[8,48,128]{2,1,0:T(8,128)S(1)}, u32[]{:S(2)}, u32[]{:S(2)}) collective-permute-start(f32[8,48,128]{2,1,0:T(8,128)S(1)} %get-tuple-element.54), channel_id=1, source_target_pairs={{0,4},{4,0},{8,12},{12,8},{16,20},{20,16},{24,28},{28,24},{1,5},{5... | collective-permute-start | bytes 589832 | tf_op jit(solution)/shard_map/ppermute | solution.py:468
  2.2 10.5 %collective-permute-start.4 = (f32[8,48,128]{2,1,0:T(8,128)S(1)}, f32[8,48,128]{2,1,0:T(8,128)S(1)}, u32[]{:S(2)}, u32[]{:S(2)}) collective-permute-start(f32[8,48,128]{2,1,0:T(8,128)S(1)} %get-tuple-element.55), channel_id=1, source_target_pairs={{4,8},{8,4},{12,16},{16,12},{20,24},{24,20},{28,0},{0,28},{5,9},{9... | collective-permute-start | bytes 589832 | tf_op jit(solution)/shard_map/ppermute | solution.py:468
  5.8 8.9 %collective-permute-start.2 = (f32[256,128]{1,0:T(8,128)S(1)}, f32[256,128]{1,0:T(8,128)S(1)}, u32[]{:S(2)}, u32[]{:S(2)}) collective-permute-start(f32[256,128]{1,0:T(8,128)S(1)} %get-tuple-element.53), channel_id=1, source_target_pairs={{0,28},{4,24},{8,20},{12,16},{16,12},{20,8},{24,4},{28,0},{1,29},{... | collective-permute-start | bytes 393224 | tf_op jit(solution)/shard_map/ppermute | solution.py:468
  5.8 8.8 %collective-permute-start = (f32[8,8,128]{2,1,0:T(8,128)S(1)}, f32[8,8,128]{2,1,0:T(8,128)S(1)}, u32[]{:S(2)}, u32[]{:S(2)}) collective-permute-start(f32[8,8,128]{2,1,0:T(8,128)S(1)} %get-tuple-element.45), channel_id=1, source_target_pairs={{0,1},{1,0},{2,3},{3,2},{4,5},{5,4},{6,7},{7,6},{8,9},{9,8},{10,11... | collective-permute-start | bytes 98312 | tf_op jit(solution)/shard_map/ppermute | solution.py:469
  7.5 7.1 %collective-permute-start.1 = (f32[8,8,128]{2,1,0:T(8,128)S(1)}, f32[8,8,128]{2,1,0:T(8,128)S(1)}, u32[]{:S(2)}, u32[]{:S(2)}) collective-permute-start(f32[8,8,128]{2,1,0:T(8,128)S(1)} %get-tuple-element.46), channel_id=1, source_target_pairs={{1,2},{2,1},{3,0},{0,3},{5,6},{6,5},{7,4},{4,7},{9,10},{10,9},{11,... | collective-permute-start | bytes 98312 | tf_op jit(solution)/shard_map/ppermute | solution.py:469
  12.7 1.9 %copy-start = (f32[16,16,128]{2,1,0:T(8,128)S(1)}, f32[16,16,128]{2,1,0:T(8,128)}, u32[]{:S(2)}) copy-start(f32[16,16,128]{2,1,0:T(8,128)} %param.11) | copy-start | bytes 393220
  12.7 1.9 %copy-start.1 = (s32[16,16,128]{2,1,0:T(8,128)S(1)}, s32[16,16,128]{2,1,0:T(8,128)}, u32[]{:S(2)}) copy-start(s32[16,16,128]{2,1,0:T(8,128)} %param.13) | copy-start | bytes 393220
  17.7 8.5 %collective-permute-start.8 = (f32[5,48,128]{2,1,0:T(8,128)S(1)}, f32[5,48,128]{2,1,0:T(8,128)S(1)}, u32[]{:S(2)}, u32[]{:S(2)}) collective-permute-start(f32[5,48,128]{2,1,0:T(8,128)S(1)} %get-tuple-element.73), channel_id=1, source_target_pairs={{0,4},{4,0},{8,12},{12,8},{16,20},{20,16},{24,28},{28,24},{1,5},{5... | collective-permute-start | bytes 368648 | tf_op jit(solution)/shard_map/ppermute | solution.py:468
  17.8 8.5 %collective-permute-start.9 = (f32[5,48,128]{2,1,0:T(8,128)S(1)}, f32[5,48,128]{2,1,0:T(8,128)S(1)}, u32[]{:S(2)}, u32[]{:S(2)}) collective-permute-start(f32[5,48,128]{2,1,0:T(8,128)S(1)} %get-tuple-element.74), channel_id=1, source_target_pairs={{4,8},{8,4},{12,16},{16,12},{20,24},{24,20},{28,0},{0,28},{5,9},{9... | collective-permute-start | bytes 368648 | tf_op jit(solution)/shard_map/ppermute | solution.py:468
  19.8 7.9 %collective-permute-start.7 = (f32[256,128]{1,0:T(8,128)S(1)}, f32[256,128]{1,0:T(8,128)S(1)}, u32[]{:S(2)}, u32[]{:S(2)}) collective-permute-start(f32[256,128]{1,0:T(8,128)S(1)} %get-tuple-element.72), channel_id=1, source_target_pairs={{0,28},{4,24},{8,20},{12,16},{16,12},{20,8},{24,4},{28,0},{1,29},{... | collective-permute-start | bytes 393224 | tf_op jit(solution)/shard_map/ppermute | solution.py:468
  20.5 7.2 %collective-permute-start.5 = (f32[5,8,128]{2,1,0:T(8,128)S(1)}, f32[5,8,128]{2,1,0:T(8,128)S(1)}, u32[]{:S(2)}, u32[]{:S(2)}) collective-permute-start(f32[5,8,128]{2,1,0:T(8,128)S(1)} %get-tuple-element.65), channel_id=1, source_target_pairs={{0,1},{1,0},{2,3},{3,2},{4,5},{5,4},{6,7},{7,6},{8,9},{9,8},{10,11... | collective-permute-start | bytes 61448 | tf_op jit(solution)/shard_map/ppermute | solution.py:469
  21.3 6.3 %collective-permute-start.6 = (f32[5,8,128]{2,1,0:T(8,128)S(1)}, f32[5,8,128]{2,1,0:T(8,128)S(1)}, u32[]{:S(2)}, u32[]{:S(2)}) collective-permute-start(f32[5,8,128]{2,1,0:T(8,128)S(1)} %get-tuple-element.66), channel_id=1, source_target_pairs={{1,2},{2,1},{3,0},{0,3},{5,6},{6,5},{7,4},{4,7},{9,10},{10,9},{11,... | collective-permute-start | bytes 61448 | tf_op jit(solution)/shard_map/ppermute | solution.py:469

commit v7 on v6

--- a/solution.py
+++ b/solution.py
@@ -11,6 +11,7 @@
 viscosity = 0.8
 conduction = 1.0
 time_step = 0.05
+metric_scale = 12.0 * viscosity * 0.5
 H = 3
 F32 = jnp.float32
 
@@ -23,16 +24,17 @@
     pressure = 0.4 * (energy - 0.5 * rho * speed_sq)
     ratio = pressure * inverse
     heat = 0.5 * speed_sq + conduction * ratio
-    return velocity, pressure, energy + pressure, 1.4 * ratio, heat
-
-
-def point_fluxes(state, prims, row):
+    return velocity, pressure, energy + pressure, (1.4 / metric_scale) * ratio, heat
+
+
+def point_fluxes(state, prims, row, metric=None):
     rho, m0, m1, m2, _ = state
     (u0, u1, u2), pressure, enthalpy, sound_sq, _ = prims
     x0, x1, x2 = row
     contra = x0 * u0 + x1 * u1 + x2 * u2
-    metric_sq = x0 * x0 + x1 * x1 + x2 * x2
-    square = sound_sq * metric_sq
+    if metric is None:
+        metric = (x0 * x0 + x1 * x1 + x2 * x2) * metric_scale
+    square = sound_sq * metric
     speed = jnp.abs(contra) + square * lax.rsqrt(jnp.maximum(square, 1e-30))
     fluxes = (
         rho * contra,
@@ -44,50 +46,74 @@
     waves = [speed * one for one in state]
     plus = [a + b for a, b in zip(fluxes, waves)]
     minus = [a - b for a, b in zip(fluxes, waves)]
-    return plus, minus, metric_sq * (12.0 * viscosity * 0.5)
+    return plus, minus, metric
 
 
 def RCP(x):
     return pl.reciprocal(x, approx=True)
 
 
+def add(a, b):
+    if a is None or b is None:
+        return b if a is None else a
+    return a + b
+
+
+def subtract(a, b):
+    if b is None:
+        return a
+    return -b if a is None else a - b
+
+
+def multiply(a, b):
+    return None if a is None or b is None else a * b
+
+
 class Split:
-    def __init__(self, load, kind):
-        self.load, self.memo, self.kind = load, {}, kind
+    def __init__(self, load, kind, flat=None):
+        self.load, self.memo, self.kind, self.flat = load, {}, kind, flat
 
     def get(self, name, n):
         if (name, n) not in self.memo:
             self.memo[name, n] = getattr(self, "make_" + name)(n)
         return self.memo[name, n]
 
+    def cast(self, value):
+        return None if value is None else value.astype(self.kind)
+
     def make_v(self, n):
         return self.load(n)
 
     def make_d(self, n):
+        if self.flat is not None and n >= self.flat:
+            return None
         return self.get("v", n + 1) - self.get("v", n)
 
     def make_e(self, n):
-        return self.get("d", n) - self.get("d", n - 1)
+        return subtract(self.get("d", n), self.get("d", n - 1))
 
     def make_t(self, n):
-        return self.get("e", n + 1) - self.get("e", n)
+        return subtract(self.get("e", n + 1), self.get("e", n))
 
     def make_near(self, n):
-        return self.get("t", n).astype(self.kind)
+        return self.cast(self.get("t", n))
 
     def make_near2(self, n):
-        return self.get("near", n) + self.get("near", n)
+        return add(self.get("near", n), self.get("near", n))
 
     def make_low(self, n):
-        return self.get("d", n).astype(self.kind)
+        return self.cast(self.get("d", n))
 
     def make_smooth(self, n):
         high, low = self.get("low", n), self.get("low", n - 1)
-        bend = self.get("e", n).astype(self.kind)
+        bend = self.cast(self.get("e", n))
+        least = self.kind(16.0 * epsilon / 3.0)
+        if bend is None:
+            return (jnp.full(self.get("v", self.flat).shape, least, self.kind),) * 3
         twice = bend + bend
-        a, b = high * twice, low * twice
-        centre = (a - b) * self.kind(2.0 / 3.0) + (high * low + self.kind(16.0 * epsilon / 3.0))
-        return centre + a, centre, centre - b
+        a, b = multiply(high, twice), multiply(low, twice)
+        centre = subtract(a, b) * self.kind(2.0 / 3.0) + add(multiply(high, low), least)
+        return add(a, centre), centre, subtract(centre, b)
 
     def correction(self, outer, middle, inner, near, far):
         left = middle * RCP(outer)
@@ -95,14 +121,16 @@
         weight_left = left * left * self.kind(1.0 / 3.0)
         weight_right = right * right
         total = (weight_left + weight_right) + self.kind(2.0)
-        return (weight_left * near + weight_right * far) * RCP(total)
-
-
-def sweep(kind, load_plus, load_minus, load_diffused, load_metric, store, first, last, open_low=False, open_high=False):
-    plus, minus = Split(load_plus, kind), Split(load_minus, kind)
+        return add(multiply(weight_left, near), multiply(weight_right, far)) * RCP(total)
+
+
+def sweep(kind, load_plus, load_minus, load_diffused, load_metric, store, first, last, open_low=False, open_high=False,
+          flat=None):
+    plus, minus = Split(load_plus, kind, flat), Split(load_minus, kind, flat)
     central, diffused, metric = {}, {}, {}
 
     def tripled(n):
+        n = n if flat is None else min(n, flat)
         if n not in central:
             central[n] = 3.0 * (plus.get("v", n) + minus.get("v", n))
         return central[n]
@@ -128,10 +156,13 @@
             minus.get("near2", n + 1),
             minus.get("near", n),
         )
-        flux = (tripled(n) + tripled(n + 1)) - (plus.get("e", n) + minus.get("e", n + 1)) + (down - up).astype(F32)
-        face_metric = cached(metric, load_metric, n) + cached(metric, load_metric, n + 1)
-        jump = cached(diffused, load_diffused, n + 1) - cached(diffused, load_diffused, n)
-        net = face_metric * jump - flux
+        flux = (tripled(n) + tripled(n + 1)) - add(plus.get("e", n), minus.get("e", n + 1)) + (down - up).astype(F32)
+        if flat is not None and n >= flat:
+            net = -flux
+        else:
+            face_metric = cached(metric, load_metric, n) + cached(metric, load_metric, n + 1)
+            jump = cached(diffused, load_diffused, n + 1) - cached(diffused, load_diffused, n)
+            net = face_metric * jump - flux
         if before is not None:
             store(n, net - before)
         elif open_low:
@@ -231,35 +262,41 @@
     copies[5].wait()
 
 
-def early_kernel(dims, kind, state_ref, span_ref, span_met_ref, met_ref, acc_ref, plus_i, minus_i, metric_i, plus_j, minus_j,
-                 metric_j, diffused_ref, plus_k, minus_k, metric_k, diffused_k):
+def early_kernel(dims, kind, kept, state_ref, span_ref, span_met_ref, met_ref, *refs):
     rows_i, height = dims
+    if kept:
+        metric_i, metric_j, metric_k = refs[:3]
+        refs = refs[3:]
+    acc_ref, plus_i, minus_i, plus_j, minus_j, diffused_ref, plus_k, minus_k, diffused_k = refs[:9]
+    if not kept:
+        metric_i, metric_j, metric_k = refs[9:]
     diffused_ref[0] = jnp.zeros(diffused_ref.shape[1:], F32)
     diffused_k[0] = jnp.zeros(diffused_k.shape[1:], F32)
+
+    def place(refs, metric_ref, rows, state, prims, row):
+        plus, minus, metric = point_fluxes(state, prims, row, metric_ref[rows, :] if kept else None)
+        put((*refs, metric_ref), rows, plus, minus, None if kept else metric)
 
     def planes(n, carry):
         rows = aligned(n * rows_i, rows_i)
         state = [state_ref[f, rows, :] for f in range(5)]
         prims = primitives(state)
         put_diffused(diffused_ref, rows, prims)
-        put((plus_i, minus_i, metric_i), rows,
-            *point_fluxes(state, prims, [unit(0, m, met_ref[m, rows, :]) for m in range(3)]))
-        put((plus_j, minus_j, metric_j), rows,
-            *point_fluxes(state, prims, [unit(1, m, met_ref[3 + m, rows, :]) for m in range(3)]))
+        place((plus_i, minus_i), metric_i, rows, state, prims, [unit(0, m, met_ref[m, rows, :]) for m in range(3)])
+        place((plus_j, minus_j), metric_j, rows, state, prims, [unit(1, m, met_ref[3 + m, rows, :]) for m in range(3)])
         return carry
 
-    lax.fori_loop(0, rows_i, planes, 0, unroll=2)
+    lax.fori_loop(0, rows_i, planes, 0, unroll=4)
 
     def spans(n, carry):
         rows = aligned(n * 16, 16)
         state = [span_ref[f, rows, :] for f in range(5)]
         prims = primitives(state)
         put_diffused(diffused_k, rows, prims)
-        put((plus_k, minus_k, metric_k), rows,
-            *point_fluxes(state, prims, [unit(2, m, span_met_ref[5 + m, rows, :]) for m in range(3)]))
+        place((plus_k, minus_k), metric_k, rows, state, prims, [unit(2, m, span_met_ref[5 + m, rows, :]) for m in range(3)])
         return carry
 
-    lax.fori_loop(0, height // 2, spans, 0, unroll=2)
+    lax.fori_loop(0, height // 2, spans, 0, unroll=4)
 
     def normal(f, carry):
         def rows(n):
@@ -271,7 +308,8 @@
         for n in range(2):
             store(n, jnp.zeros((rows_i, 128), F32))
         sweep(kind, lambda n: plus_j[f, rows(n), :], lambda n: minus_j[f, rows(n), :], lambda n: diffused_ref[f, rows(n), :],
-              lambda n: metric_j[rows(n), :], store, 2, rows_i - 1, open_low=True)
+              lambda n: metric_j[rows(n), :], store, 2, rows_i - 1, open_low=True,
+              flat=rows_i - 1)
         return carry
 
     lax.fori_loop(0, 5, normal, 0)
@@ -405,7 +443,7 @@
         put((ghost_plus, ghost_minus, ghost_metric), to,
             *point_fluxes(state, prims, [unit(1, m, met_ref[3 + m, wall, :]) for m in range(3)]))
 
-    def normal(f, carry):
+    def normal(f):
         def rows(n):
             return pl.ds(n, rows_i, stride=rows_i)
 
@@ -422,12 +460,11 @@
 
         sweep(kind, loader(plus_j, ghost_plus, (f,)), loader(minus_j, ghost_minus, (f,)), loader(diffused_ref, ghost_diffused, (f,)),
               lambda n: metric_j[rows(max(n, 0)), :], store, -1, 1, open_high=True)
-        return carry
-
-    lax.fori_loop(0, 5, normal, 0)
+
 
     scale = (time_step / 12.0) * blank_ref[...].astype(F32) / vol_ref[...]
     for f in range(5):
+        normal(f)
         for half in range(2):
             parts = [acc_ref[f, pl.ds(q * 2 + half, height, stride=8), :] for q in range(4)]
             rows = slice(half * 128, (half + 1) * 128)
@@ -513,7 +550,7 @@
         return [pltpu.VMEM((5, rows, lanes), F32), pltpu.VMEM((5, rows, lanes), F32), pltpu.VMEM((rows, lanes), F32),
                 pltpu.VMEM((5, rows, lanes), F32)]
 
-    metric_halo = None
+    metric_halo, kept = None, ()
     start = state
     for final in (False, True):
         kind = jnp.bfloat16 if final else F32
@@ -521,19 +558,20 @@
         if metric_halo is None:
             metric_halo = core, chip, span_near, span_far
         line, span_line = shape(5, total, lanes), shape(5, span_rows, lanes)
-        normal, *lines = call(
-            functools.partial(early_kernel, dims, kind), "early", (state, span, span_met, met),
-            [field, line, line, shape(total, lanes), line, line, shape(total, lanes), line,
-             span_line, span_line, shape(span_rows, lanes), span_line],
+        normal, plus_i, minus_i, plus_j, minus_j, diffused, plus_k, minus_k, diffused_k, *squares = call(
+            functools.partial(early_kernel, dims, kind, bool(kept)), "early", (state, span, span_met, met, *kept),
+            [field, line, line, line, line, line, span_line, span_line, span_line]
+            + ([] if kept else [shape(total, lanes), shape(total, lanes), shape(span_rows, lanes)]),
             [], cost=10**8,
         )
-        plus_i, minus_i, metric_i, plus_j, minus_j, metric_j, diffused = lines[:7]
+        kept = kept or tuple(squares)
+        metric_i, metric_j, metric_k = kept
         (plane,) = call(
             functools.partial(chord_kernel, dims, kind), "chord",
             (state, met, core, chip, metric_halo[0], metric_halo[1], normal, plus_i, minus_i, metric_i, diffused),
             [field], halo_scratch(halo), cost=10**8,
         )
-        ins = (span, span_met, span_near, span_far, metric_halo[2], metric_halo[3], *lines[7:], wake_partner, state, met,
+        ins = (span, span_met, span_near, span_far, metric_halo[2], metric_halo[3], plus_k, minus_k, metric_k, diffused_k, wake_partner, state, met,
                volume, blank, wake, plane, plus_j, minus_j, metric_j, diffused)
         ins += (start,) if final else ()
         state, *rest = call(

time: 30.8 us -> 30.4 us (0.987)
  Pallas kernels: 16.1 us -> 15.5 us
    pallas_call x7, Pallas kernels: 16.1 us -> 15.5 us  [call(): pl.pallas_call(kernel, out_shape=outs, in_specs=specs or [whole] * len(in...]
where the time goes in v7:
time: 30.4 us; the launch traced here: 30.3 us
  Pallas kernels  15.5 us (51%)
  starting transfers between devices  14.5 us (48%)
    pallas_call x7, Pallas kernels, call(): pl.pallas_call(kernel, out_shape=outs, in_specs=specs or [whole] * len(in...  15.5 us
    ppermute x2, starting transfers between devices, exchange(): lax.ppermute(chip, 'wrap', chips)  5.54 us
    ppermute x2, starting transfers between devices, exchange(): lax.ppermute(span_far, 'span', far)  4.95 us
    ppermute x2, starting transfers between devices, exchange(): lax.ppermute(span_near, 'span', near)  2.68 us
    ppermute x2, starting transfers between devices, exchange(): lax.ppermute(wake, 'wrap', mirror)  0.76 us
  transfers between devices with their start and end apart: 10, of which 0 were waited for; matrix products, arithmetic and copies ran while one was open for 0% of the time, Pallas kernels for 27%

profile of v7, /device:TPU:0, one launch (start us, length us, event | category | flops | bytes accessed | tf_op | source)
XLA Modules:
  0.0 30.3 jit_solution(7431339323110467675)
XLA Ops:
  0.0 1.7 %prepare.1 = (f32[5,256,128]{2,1,0:T(8,128)S(1)}, f32[8,256,128]{2,1,0:T(8,128)S(1)}, f32[9,256,128]{2,1,0:T(8,128)S(1)}, f32[8,48,128]{2,1,0:T(8,128)S(1)}, f32...) custom-call(f32[256,128]{1,0:T(8,128)} %bitcast.13, ...), custom_call_target="tpu_custom_call" | custom-call | tf_op jit(solution)/shard_map/prepare/pallas_call | solution.py:520
  1.7 0.5 %collective-permute-start.3 = (f32[8,48,128]{2,1,0:T(8,128)S(1)}, f32[8,48,128]{2,1,0:T(8,128)S(1)}, u32[]{:S(2)}, u32[]{:S(2)}) collective-permute-start(f32[8,48,128]{2,1,0:T(8,128)S(1)} %get-tuple-element.51), channel_id=1, source_target_pairs={{0,4},{4,0},{8,12},{12,8},{16,20},{20,16},{24,28},{28,24},{1,5},{5... | collective-permute-start | bytes 589832 | tf_op jit(solution)/shard_map/ppermute | solution.py:505
  2.2 3.6 %collective-permute-start.4 = (f32[8,48,128]{2,1,0:T(8,128)S(1)}, f32[8,48,128]{2,1,0:T(8,128)S(1)}, u32[]{:S(2)}, u32[]{:S(2)}) collective-permute-start(f32[8,48,128]{2,1,0:T(8,128)S(1)} %get-tuple-element.52), channel_id=1, source_target_pairs={{4,8},{8,4},{12,16},{16,12},{20,24},{24,20},{28,0},{0,28},{5,9},{9... | collective-permute-start | bytes 589832 | tf_op jit(solution)/shard_map/ppermute | solution.py:505
  5.8 0.0 collective-permute-start.2
  5.8 1.7 %collective-permute-start = (f32[8,8,128]{2,1,0:T(8,128)S(1)}, f32[8,8,128]{2,1,0:T(8,128)S(1)}, u32[]{:S(2)}, u32[]{:S(2)}) collective-permute-start(f32[8,8,128]{2,1,0:T(8,128)S(1)} %get-tuple-element.42), channel_id=1, source_target_pairs={{0,1},{1,0},{2,3},{3,2},{4,5},{5,4},{6,7},{7,6},{8,9},{9,8},{10,11... | collective-permute-start | bytes 98312 | tf_op jit(solution)/shard_map/ppermute | solution.py:506
  7.5 2.5 %collective-permute-start.1 = (f32[8,8,128]{2,1,0:T(8,128)S(1)}, f32[8,8,128]{2,1,0:T(8,128)S(1)}, u32[]{:S(2)}, u32[]{:S(2)}) collective-permute-start(f32[8,8,128]{2,1,0:T(8,128)S(1)} %get-tuple-element.43), channel_id=1, source_target_pairs={{1,2},{2,1},{3,0},{0,3},{5,6},{6,5},{7,4},{4,7},{9,10},{10,9},{11,... | collective-permute-start | bytes 98312 | tf_op jit(solution)/shard_map/ppermute | solution.py:506
  10.0 2.6 %early.2 = (f32[5,256,128]{2,1,0:T(8,128)S(1)}, f32[5,256,128]{2,1,0:T(8,128)S(1)}, f32[5,256,128]{2,1,0:T(8,128)S(1)}, f32[5,256,128]{2,1,0:T(8,128)S(1)}, f32[...) custom-call(f32[5,256,128]{2,1,0:T(8,128)S(1)} %get-tuple-element.44, ...), custom_call_target="tpu_custom_call" | custom-call | flops 100000000 | bytes 25000000 | tf_op jit(solution)/shard_map/early/pallas_call | solution.py:520
  12.5 0.0 collective-permute-done.3.core_ref.met_core_ref
  12.5 0.0 copy-start
  12.6 0.0 copy-start.1
  12.6 1.9 %chord.2.refs_16_ = f32[5,256,128]{2,1,0:T(8,128)S(1)} custom-call(f32[5,256,128]{2,1,0:T(8,128)S(1)} %get-tuple-element.44.state_ref.refs_11_.refs_21_, f32[9,256,128]{2,1,0:T(8,128)S(1)} %get-tuple-element.45.met_ref.refs_12_, f32[8,48,128]{2,1,0:T(8,128)S(1)} %collective-permute-done.3.core_ref.met_core_ref, ...), custom_call_target="tpu_custom_call" | custom-call | flops 100000000 | bytes 25000000 | tf_op jit(solution)/shard_map/chord/pallas_call | solution.py:520
  14.5 0.0 collective-permute-done.2.refs_15_
  14.5 2.9 %span.2 = (f32[5,256,128]{2,1,0:T(8,128)S(1)}, f32[5,256,128]{2,1,0:T(8,128)S(1)}, f32[5,48,128]{2,1,0:T(8,128)S(1)}, f32[5,48,128]{2,1,0:T(8,128)S(1)}, f32[256...) custom-call(f32[8,256,128]{2,1,0:T(8,128)S(1)} %get-tuple-element.41.span_ref.span_met_ref.refs_0_.refs_1_, ...), custom_call_target="tpu_custom_call" | custom-call | flops 100000000 | bytes 25000000 | tf_op jit(solution)/shard_map/span/pallas_call | solution.py:520
  17.4 0.1 collective-permute-start.8
  17.5 2.0 %collective-permute-start.9 = (f32[5,48,128]{2,1,0:T(8,128)S(1)}, f32[5,48,128]{2,1,0:T(8,128)S(1)}, u32[]{:S(2)}, u32[]{:S(2)}) collective-permute-start(f32[5,48,128]{2,1,0:T(8,128)S(1)} %get-tuple-element.70), channel_id=1, source_target_pairs={{4,8},{8,4},{12,16},{16,12},{20,24},{24,20},{28,0},{0,28},{5,9},{9... | collective-permute-start | bytes 368648 | tf_op jit(solution)/shard_map/ppermute | solution.py:505
  19.5 0.7 %collective-permute-start.7 = (f32[256,128]{1,0:T(8,128)S(1)}, f32[256,128]{1,0:T(8,128)S(1)}, u32[]{:S(2)}, u32[]{:S(2)}) collective-permute-start(f32[256,128]{1,0:T(8,128)S(1)} %get-tuple-element.68), channel_id=1, source_target_pairs={{0,28},{4,24},{8,20},{12,16},{16,12},{20,8},{24,4},{28,0},{1,29},{... | collective-permute-start | bytes 393224 | tf_op jit(solution)/shard_map/ppermute | solution.py:505
  20.2 1.0 %collective-permute-start.5 = (f32[5,8,128]{2,1,0:T(8,128)S(1)}, f32[5,8,128]{2,1,0:T(8,128)S(1)}, u32[]{:S(2)}, u32[]{:S(2)}) collective-permute-start(f32[5,8,128]{2,1,0:T(8,128)S(1)} %get-tuple-element.62), channel_id=1, source_target_pairs={{0,1},{1,0},{2,3},{3,2},{4,5},{5,4},{6,7},{7,6},{8,9},{9,8},{10,11... | collective-permute-start | bytes 61448 | tf_op jit(solution)/shard_map/ppermute | solution.py:506
  21.2 2.5 %collective-permute-start.6 = (f32[5,8,128]{2,1,0:T(8,128)S(1)}, f32[5,8,128]{2,1,0:T(8,128)S(1)}, u32[]{:S(2)}, u32[]{:S(2)}) collective-permute-start(f32[5,8,128]{2,1,0:T(8,128)S(1)} %get-tuple-element.63), channel_id=1, source_target_pairs={{1,2},{2,1},{3,0},{0,3},{5,6},{6,5},{7,4},{4,7},{9,10},{10,9},{11,... | collective-permute-start | bytes 61448 | tf_op jit(solution)/shard_map/ppermute | solution.py:506
  23.6 2.3 %early.3 = (f32[5,256,128]{2,1,0:T(8,128)S(1)}, f32[5,256,128]{2,1,0:T(8,128)S(1)}, f32[5,256,128]{2,1,0:T(8,128)S(1)}, f32[5,256,128]{2,1,0:T(8,128)S(1)}, f32[...) custom-call(f32[5,256,128]{2,1,0:T(8,128)S(1)} %get-tuple-element.64, ...), custom_call_target="tpu_custom_call" | custom-call | flops 100000000 | bytes 25000000 | tf_op jit(solution)/shard_map/early/pallas_call | solution.py:520
  25.9 0.0 collective-permute-done.8.core_ref
  26.0 1.4 %chord.3.refs_16_ = f32[5,256,128]{2,1,0:T(8,128)S(1)} custom-call(f32[5,256,128]{2,1,0:T(8,128)S(1)} %get-tuple-element.64.state_ref.refs_11_, f32[9,256,128]{2,1,0:T(8,128)S(1)} %get-tuple-element.45.met_ref.refs_12_, f32[5,48,128]{2,1,0:T(8,128)S(1)} %collective-permute-done.8.core_ref, f32[5,48,128]{2,1,0:T(8,128)S(1)} %collective-permute-done.9.chip_ref, ...), custom_call_target="tpu_custom_call" | custom-call | flops 100000000 | bytes 25000000 | tf_op jit(solution)/shard_map/chord/pallas_call | solution.py:520
  27.4 0.0 collective-permute-done.6.refs_3_
  27.4 0.0 collective-permute-done.7.refs_15_
  27.4 2.9 %span.3 = f32[5,256,128]{2,1,0:T(8,128)} custom-call(f32[5,256,128]{2,1,0:T(8,128)S(1)} %get-tuple-element.61.span_ref.refs_0_, f32[8,256,128]{2,1,0:T(8,128)S(1)} %get-tuple-element.41.span_ref.span_met_ref.refs_0_.refs_1_, f32[5,8,128]{2,1,0:T(8,128)S(1)} %collective-permute-done.5.refs_2_, f32[5,8,128]{2,1,0:T(8,128)S(1)} %collective-permute-done.6.refs_3_, ...), custom_call_target="tpu_custom_call" | custom-call | flops 100000000 | bytes 25000000 | tf_op jit(solution)/shard_map/span/pallas_call | solution.py:520
  (7 shorter events, 0.0 us)
Async XLA Ops:
  1.7 10.9 %collective-permute-start.3 = (f32[8,48,128]{2,1,0:T(8,128)S(1)}, f32[8,48,128]{2,1,0:T(8,128)S(1)}, u32[]{:S(2)}, u32[]{:S(2)}) collective-permute-start(f32[8,48,128]{2,1,0:T(8,128)S(1)} %get-tuple-element.51), channel_id=1, source_target_pairs={{0,4},{4,0},{8,12},{12,8},{16,20},{20,16},{24,28},{28,24},{1,5},{5... | collective-permute-start | bytes 589832 | tf_op jit(solution)/shard_map/ppermute | solution.py:505
  2.2 10.3 %collective-permute-start.4 = (f32[8,48,128]{2,1,0:T(8,128)S(1)}, f32[8,48,128]{2,1,0:T(8,128)S(1)}, u32[]{:S(2)}, u32[]{:S(2)}) collective-permute-start(f32[8,48,128]{2,1,0:T(8,128)S(1)} %get-tuple-element.52), channel_id=1, source_target_pairs={{4,8},{8,4},{12,16},{16,12},{20,24},{24,20},{28,0},{0,28},{5,9},{9... | collective-permute-start | bytes 589832 | tf_op jit(solution)/shard_map/ppermute | solution.py:505
  5.8 8.7 %collective-permute-start.2 = (f32[256,128]{1,0:T(8,128)S(1)}, f32[256,128]{1,0:T(8,128)S(1)}, u32[]{:S(2)}, u32[]{:S(2)}) collective-permute-start(f32[256,128]{1,0:T(8,128)S(1)} %get-tuple-element.50), channel_id=1, source_target_pairs={{0,28},{4,24},{8,20},{12,16},{16,12},{20,8},{24,4},{28,0},{1,29},{... | collective-permute-start | bytes 393224 | tf_op jit(solution)/shard_map/ppermute | solution.py:505
  5.8 8.7 %collective-permute-start = (f32[8,8,128]{2,1,0:T(8,128)S(1)}, f32[8,8,128]{2,1,0:T(8,128)S(1)}, u32[]{:S(2)}, u32[]{:S(2)}) collective-permute-start(f32[8,8,128]{2,1,0:T(8,128)S(1)} %get-tuple-element.42), channel_id=1, source_target_pairs={{0,1},{1,0},{2,3},{3,2},{4,5},{5,4},{6,7},{7,6},{8,9},{9,8},{10,11... | collective-permute-start | bytes 98312 | tf_op jit(solution)/shard_map/ppermute | solution.py:506
  7.5 7.0 %collective-permute-start.1 = (f32[8,8,128]{2,1,0:T(8,128)S(1)}, f32[8,8,128]{2,1,0:T(8,128)S(1)}, u32[]{:S(2)}, u32[]{:S(2)}) collective-permute-start(f32[8,8,128]{2,1,0:T(8,128)S(1)} %get-tuple-element.43), channel_id=1, source_target_pairs={{1,2},{2,1},{3,0},{0,3},{5,6},{6,5},{7,4},{4,7},{9,10},{10,9},{11,... | collective-permute-start | bytes 98312 | tf_op jit(solution)/shard_map/ppermute | solution.py:506
  12.5 2.0 %copy-start = (f32[16,16,128]{2,1,0:T(8,128)S(1)}, f32[16,16,128]{2,1,0:T(8,128)}, u32[]{:S(2)}) copy-start(f32[16,16,128]{2,1,0:T(8,128)} %param.11) | copy-start | bytes 393220
  12.6 2.0 %copy-start.1 = (s32[16,16,128]{2,1,0:T(8,128)S(1)}, s32[16,16,128]{2,1,0:T(8,128)}, u32[]{:S(2)}) copy-start(s32[16,16,128]{2,1,0:T(8,128)} %param.13) | copy-start | bytes 393220
  17.4 8.5 %collective-permute-start.8 = (f32[5,48,128]{2,1,0:T(8,128)S(1)}, f32[5,48,128]{2,1,0:T(8,128)S(1)}, u32[]{:S(2)}, u32[]{:S(2)}) collective-permute-start(f32[5,48,128]{2,1,0:T(8,128)S(1)} %get-tuple-element.69), channel_id=1, source_target_pairs={{0,4},{4,0},{8,12},{12,8},{16,20},{20,16},{24,28},{28,24},{1,5},{5... | collective-permute-start | bytes 368648 | tf_op jit(solution)/shard_map/ppermute | solution.py:505
  17.5 8.5 %collective-permute-start.9 = (f32[5,48,128]{2,1,0:T(8,128)S(1)}, f32[5,48,128]{2,1,0:T(8,128)S(1)}, u32[]{:S(2)}, u32[]{:S(2)}) collective-permute-start(f32[5,48,128]{2,1,0:T(8,128)S(1)} %get-tuple-element.70), channel_id=1, source_target_pairs={{4,8},{8,4},{12,16},{16,12},{20,24},{24,20},{28,0},{0,28},{5,9},{9... | collective-permute-start | bytes 368648 | tf_op jit(solution)/shard_map/ppermute | solution.py:505
  19.5 7.9 %collective-permute-start.7 = (f32[256,128]{1,0:T(8,128)S(1)}, f32[256,128]{1,0:T(8,128)S(1)}, u32[]{:S(2)}, u32[]{:S(2)}) collective-permute-start(f32[256,128]{1,0:T(8,128)S(1)} %get-tuple-element.68), channel_id=1, source_target_pairs={{0,28},{4,24},{8,20},{12,16},{16,12},{20,8},{24,4},{28,0},{1,29},{... | collective-permute-start | bytes 393224 | tf_op jit(solution)/shard_map/ppermute | solution.py:505
  20.2 7.2 %collective-permute-start.5 = (f32[5,8,128]{2,1,0:T(8,128)S(1)}, f32[5,8,128]{2,1,0:T(8,128)S(1)}, u32[]{:S(2)}, u32[]{:S(2)}) collective-permute-start(f32[5,8,128]{2,1,0:T(8,128)S(1)} %get-tuple-element.62), channel_id=1, source_target_pairs={{0,1},{1,0},{2,3},{3,2},{4,5},{5,4},{6,7},{7,6},{8,9},{9,8},{10,11... | collective-permute-start | bytes 61448 | tf_op jit(solution)/shard_map/ppermute | solution.py:506
  21.2 6.2 %collective-permute-start.6 = (f32[5,8,128]{2,1,0:T(8,128)S(1)}, f32[5,8,128]{2,1,0:T(8,128)S(1)}, u32[]{:S(2)}, u32[]{:S(2)}) collective-permute-start(f32[5,8,128]{2,1,0:T(8,128)S(1)} %get-tuple-element.63), channel_id=1, source_target_pairs={{1,2},{2,1},{3,0},{0,3},{5,6},{6,5},{7,4},{4,7},{9,10},{10,9},{11,... | collective-permute-start | bytes 61448 | tf_op jit(solution)/shard_map/ppermute | solution.py:506

commit v8 on v7

--- a/solution.py
+++ b/solution.py
@@ -46,7 +46,7 @@
     waves = [speed * one for one in state]
     plus = [a + b for a, b in zip(fluxes, waves)]
     minus = [a - b for a, b in zip(fluxes, waves)]
-    return plus, minus, metric
+    return plus, minus, [6.0 * one for one in fluxes], metric
 
 
 def RCP(x):
@@ -124,16 +124,10 @@
         return add(multiply(weight_left, near), multiply(weight_right, far)) * RCP(total)
 
 
-def sweep(kind, load_plus, load_minus, load_diffused, load_metric, store, first, last, open_low=False, open_high=False,
+def sweep(kind, load_plus, load_minus, load_centre, load_diffused, load_face, store, first, last, open_low=False, open_high=False,
           flat=None):
     plus, minus = Split(load_plus, kind, flat), Split(load_minus, kind, flat)
-    central, diffused, metric = {}, {}, {}
-
-    def tripled(n):
-        n = n if flat is None else min(n, flat)
-        if n not in central:
-            central[n] = 3.0 * (plus.get("v", n) + minus.get("v", n))
-        return central[n]
+    central, diffused = {}, {}
 
     def cached(table, load, n):
         if n not in table:
@@ -156,13 +150,13 @@
             minus.get("near2", n + 1),
             minus.get("near", n),
         )
-        flux = (tripled(n) + tripled(n + 1)) - add(plus.get("e", n), minus.get("e", n + 1)) + (down - up).astype(F32)
+        centres = [cached(central, load_centre, m if flat is None else min(m, flat)) for m in (n, n + 1)]
+        flux = (centres[0] + centres[1]) - add(plus.get("e", n), minus.get("e", n + 1)) + (down - up).astype(F32)
         if flat is not None and n >= flat:
             net = -flux
         else:
-            face_metric = cached(metric, load_metric, n) + cached(metric, load_metric, n + 1)
             jump = cached(diffused, load_diffused, n + 1) - cached(diffused, load_diffused, n)
-            net = face_metric * jump - flux
+            net = load_face(n) * jump - flux
         if before is not None:
             store(n, net - before)
         elif open_low:
@@ -172,11 +166,12 @@
         store(last + 1, -before)
 
 
-def put(refs, rows, plus, minus, metric=None):
-    plus_ref, minus_ref, metric_ref = refs
+def put(refs, rows, plus, minus, centre, metric=None):
+    plus_ref, minus_ref, centre_ref, metric_ref = refs
     for f in range(5):
         plus_ref[f, rows, :] = plus[f]
         minus_ref[f, rows, :] = minus[f]
+        centre_ref[f, rows, :] = centre[f]
     if metric is not None:
         metric_ref[rows, :] = metric
 
@@ -267,23 +262,24 @@
     if kept:
         metric_i, metric_j, metric_k = refs[:3]
         refs = refs[3:]
-    acc_ref, plus_i, minus_i, plus_j, minus_j, diffused_ref, plus_k, minus_k, diffused_k = refs[:9]
+    acc_ref, plus_i, minus_i, centre_i, plus_j, minus_j, centre_j, diffused_ref, plus_k, minus_k, centre_k, diffused_k = refs[:12]
     if not kept:
-        metric_i, metric_j, metric_k = refs[9:]
+        metric_i, metric_j, metric_k = refs[12:15]
+    face_ref = refs[-1]
     diffused_ref[0] = jnp.zeros(diffused_ref.shape[1:], F32)
     diffused_k[0] = jnp.zeros(diffused_k.shape[1:], F32)
 
     def place(refs, metric_ref, rows, state, prims, row):
-        plus, minus, metric = point_fluxes(state, prims, row, metric_ref[rows, :] if kept else None)
-        put((*refs, metric_ref), rows, plus, minus, None if kept else metric)
+        *fluxes, metric = point_fluxes(state, prims, row, metric_ref[rows, :] if kept else None)
+        put((*refs, metric_ref), rows, *fluxes, None if kept else metric)
 
     def planes(n, carry):
         rows = aligned(n * rows_i, rows_i)
         state = [state_ref[f, rows, :] for f in range(5)]
         prims = primitives(state)
         put_diffused(diffused_ref, rows, prims)
-        place((plus_i, minus_i), metric_i, rows, state, prims, [unit(0, m, met_ref[m, rows, :]) for m in range(3)])
-        place((plus_j, minus_j), metric_j, rows, state, prims, [unit(1, m, met_ref[3 + m, rows, :]) for m in range(3)])
+        place((plus_i, minus_i, centre_i), metric_i, rows, state, prims, [unit(0, m, met_ref[m, rows, :]) for m in range(3)])
+        place((plus_j, minus_j, centre_j), metric_j, rows, state, prims, [unit(1, m, met_ref[3 + m, rows, :]) for m in range(3)])
         return carry
 
     lax.fori_loop(0, rows_i, planes, 0, unroll=4)
@@ -293,10 +289,14 @@
         state = [span_ref[f, rows, :] for f in range(5)]
         prims = primitives(state)
         put_diffused(diffused_k, rows, prims)
-        place((plus_k, minus_k), metric_k, rows, state, prims, [unit(2, m, span_met_ref[5 + m, rows, :]) for m in range(3)])
+        place((plus_k, minus_k, centre_k), metric_k, rows, state, prims, [unit(2, m, span_met_ref[5 + m, rows, :]) for m in range(3)])
         return carry
 
     lax.fori_loop(0, height // 2, spans, 0, unroll=4)
+
+    for n in range(2, rows_i - 1):
+        low, high = (metric_j[pl.ds(m, rows_i, stride=rows_i), :] for m in (n, n + 1))
+        face_ref[n * rows_i : (n + 1) * rows_i, :] = low + high
 
     def normal(f, carry):
         def rows(n):
@@ -307,8 +307,9 @@
 
         for n in range(2):
             store(n, jnp.zeros((rows_i, 128), F32))
-        sweep(kind, lambda n: plus_j[f, rows(n), :], lambda n: minus_j[f, rows(n), :], lambda n: diffused_ref[f, rows(n), :],
-              lambda n: metric_j[rows(n), :], store, 2, rows_i - 1, open_low=True,
+        sweep(kind, lambda n: plus_j[f, rows(n), :], lambda n: minus_j[f, rows(n), :], lambda n: centre_j[f, rows(n), :],
+              lambda n: diffused_ref[f, rows(n), :], lambda n: face_ref[n * rows_i : (n + 1) * rows_i, :],
+              store, 2, rows_i - 1, open_low=True,
               flat=rows_i - 1)
         return carry
 
@@ -316,7 +317,8 @@
 
 
 def chord_kernel(dims, kind, state_ref, met_ref, core_ref, chip_ref, met_core_ref, met_chip_ref, normal_ref,
-                 plus_i, minus_i, metric_i, diffused_ref, acc_ref, halo_plus, halo_minus, halo_metric, halo_diffused):
+                 plus_i, minus_i, centre_i, metric_i, diffused_ref, acc_ref,
+                 halo_plus, halo_minus, halo_centre, halo_metric, halo_diffused, face_ref):
     rows_i, height = dims
     total = rows_i * rows_i
     position, count = lax.axis_index("wrap"), lax.axis_size("wrap")
@@ -332,7 +334,7 @@
         prims = primitives(state)
         to = aligned((core_rows + r) * rows_i, rows_i)
         put_diffused(halo_diffused, to, prims)
-        put((halo_plus, halo_minus, halo_metric), to,
+        put((halo_plus, halo_minus, halo_centre, halo_metric), to,
             *point_fluxes(state, prims, [unit(0, m, met_core_ref[5 + m, rows, :]) for m in range(3)]))
         edge = aligned(own, rows_i)
         state = [jnp.where(at_end, state_ref[f, edge, :], chip_ref[f, rows, :]) for f in range(5)]
@@ -340,25 +342,30 @@
         prims = primitives(state)
         to = aligned((chip_rows + r) * rows_i, rows_i)
         put_diffused(halo_diffused, to, prims)
-        put((halo_plus, halo_minus, halo_metric), to,
+        put((halo_plus, halo_minus, halo_centre, halo_metric), to,
             *point_fluxes(state, prims, [unit(0, m, row[m]) for m in range(3)]))
 
+    def loader(ref, halo, lead):
+        def load(n):
+            if 0 <= n < rows_i:
+                return ref[lead + (aligned(n * rows_i, rows_i),)]
+            r = n + H if n < 0 else n - rows_i + H
+            return halo[lead + (aligned(r * rows_i, rows_i),)]
+
+        return load
+
+    metric = loader(metric_i, halo_metric, ())
+    for n in range(-1, rows_i):
+        face_ref[(n + 1) * rows_i : (n + 2) * rows_i, :] = metric(n) + metric(n + 1)
+
     def chord(f, carry):
-        def loader(ref, halo, lead):
-            def load(n):
-                if 0 <= n < rows_i:
-                    return ref[lead + (aligned(n * rows_i, rows_i),)]
-                r = n + H if n < 0 else n - rows_i + H
-                return halo[lead + (aligned(r * rows_i, rows_i),)]
-
-            return load
-
         def store(n, value):
             rows = aligned(n * rows_i, rows_i)
             acc_ref[f, rows, :] = value + normal_ref[f, rows, :]
 
-        sweep(kind, loader(plus_i, halo_plus, (f,)), loader(minus_i, halo_minus, (f,)), loader(diffused_ref, halo_diffused, (f,)),
-              loader(metric_i, halo_metric, ()), store, -1, rows_i - 1)
+        sweep(kind, loader(plus_i, halo_plus, (f,)), loader(minus_i, halo_minus, (f,)), loader(centre_i, halo_centre, (f,)),
+              loader(diffused_ref, halo_diffused, (f,)), lambda n: face_ref[(n + 1) * rows_i : (n + 2) * rows_i, :],
+              store, -1, rows_i - 1)
         return carry
 
     lax.fori_loop(0, 5, chord, 0)
@@ -366,20 +373,20 @@
 
 def span_kernel(dims, kind, final, *refs):
     rows_i, height = dims
-    (span_ref, span_met_ref, span_near_ref, span_far_ref, met_near_ref, met_far_ref, plus_k, minus_k, metric_k, diffused_k,
-     partner_hbm, state_ref, met_ref, vol_ref, blank_ref, wake_ref, plane_ref, plus_j, minus_j, metric_j,
-     diffused_ref) = refs[:21]
-    refs = refs[21:]
+    (span_ref, span_met_ref, span_near_ref, span_far_ref, met_near_ref, met_far_ref, plus_k, minus_k, centre_k, metric_k,
+     diffused_k,     partner_hbm, state_ref, met_ref, vol_ref, blank_ref, wake_ref, plane_ref, plus_j, minus_j, centre_j, metric_j,
+     diffused_ref) = refs[:23]
+    refs = refs[23:]
     if final:
         start_ref, out_ref = refs[:2]
         refs = refs[2:]
     else:
         out_ref, out_span_ref = refs[:2]
         outs, refs = refs[2:7], refs[7:]
-    (acc_ref, halo_plus, halo_minus, halo_metric, halo_diffused, pad_ref, wall_ref, sum_ref,
-     ghost_plus, ghost_minus, ghost_metric, ghost_diffused, ghost_ref, partner_ref, sem) = refs[:15]
+    (acc_ref, halo_plus, halo_minus, halo_centre, halo_metric, halo_diffused, pad_ref, wall_ref, sum_ref,
+     ghost_plus, ghost_minus, ghost_centre, ghost_metric, ghost_diffused, ghost_ref, partner_ref, sem, face_ref) = refs[:18]
     if final:
-        staged_ref, out_sems = refs[15:]
+        staged_ref, out_sems = refs[18:]
     fetch = pltpu.make_async_copy(partner_hbm, partner_ref, sem)
     fetch.start()
     position, count = lax.axis_index("wrap"), lax.axis_size("wrap")
@@ -406,26 +413,31 @@
                 values.append(jnp.where(sublane >= 6, pad_ref[f, rows, :], own))
         prims = primitives(values[:5])
         put_diffused(halo_diffused, rows, prims)
-        put((halo_plus, halo_minus, halo_metric), rows,
+        put((halo_plus, halo_minus, halo_centre, halo_metric), rows,
             *point_fluxes(values[:5], prims, [unit(2, m, values[5 + m]) for m in range(3)]))
 
+    def loader(ref, halo, lead):
+        def one(n):
+            if 0 <= n < height:
+                return ref[lead + (slice(n * 8, n * 8 + 8),)]
+            r = n + H if n < 0 else n - height + H
+            return halo[lead + (slice(r * 8, r * 8 + 8),)]
+
+        return lambda n: jnp.concatenate([one(n), one(n + height // 2)], axis=0)
+
+    metric = loader(metric_k, halo_metric, ())
+    for n in range(-1, height // 2):
+        face_ref[(n + 1) * 16 : (n + 2) * 16, :] = metric(n) + metric(n + 1)
+
     def sweep_span(f, carry):
-        def loader(ref, halo, lead):
-            def one(n):
-                if 0 <= n < height:
-                    return ref[lead + (slice(n * 8, n * 8 + 8),)]
-                r = n + H if n < 0 else n - height + H
-                return halo[lead + (slice(r * 8, r * 8 + 8),)]
-
-            return lambda n: jnp.concatenate([one(n), one(n + height // 2)], axis=0)
-
         def store(n, value):
             acc_ref[f, n * 8 : n * 8 + 8, :] = value[:8]
             m = n + height // 2
             acc_ref[f, m * 8 : m * 8 + 8, :] = value[8:]
 
-        sweep(kind, loader(plus_k, halo_plus, (f,)), loader(minus_k, halo_minus, (f,)), loader(diffused_k, halo_diffused, (f,)),
-              loader(metric_k, halo_metric, ()), store, -1, height // 2 - 1)
+        sweep(kind, loader(plus_k, halo_plus, (f,)), loader(minus_k, halo_minus, (f,)), loader(centre_k, halo_centre, (f,)),
+              loader(diffused_k, halo_diffused, (f,)), lambda n: face_ref[(n + 1) * 16 : (n + 2) * 16, :],
+              store, -1, height // 2 - 1)
         return carry
 
     lax.fori_loop(0, 5, sweep_span, 0)
@@ -440,7 +452,7 @@
         prims = primitives(state)
         to = slice(r * rows_i, (r + 1) * rows_i)
         put_diffused(ghost_diffused, to, prims)
-        put((ghost_plus, ghost_minus, ghost_metric), to,
+        put((ghost_plus, ghost_minus, ghost_centre, ghost_metric), to,
             *point_fluxes(state, prims, [unit(1, m, met_ref[3 + m, wall, :]) for m in range(3)]))
 
     def normal(f):
@@ -458,8 +470,9 @@
         def store(n, value):
             wall_ref[f, n * rows_i : (n + 1) * rows_i, :] = value
 
-        sweep(kind, loader(plus_j, ghost_plus, (f,)), loader(minus_j, ghost_minus, (f,)), loader(diffused_ref, ghost_diffused, (f,)),
-              lambda n: metric_j[rows(max(n, 0)), :], store, -1, 1, open_high=True)
+        sweep(kind, loader(plus_j, ghost_plus, (f,)), loader(minus_j, ghost_minus, (f,)),
+              loader(centre_j, ghost_centre, (f,)), loader(diffused_ref, ghost_diffused, (f,)),
+              lambda n: metric_j[rows(max(n, 0)), :] + metric_j[rows(n + 1), :], store, -1, 1, open_high=True)
 
 
     scale = (time_step / 12.0) * blank_ref[...].astype(F32) / vol_ref[...]
@@ -547,8 +560,9 @@
     span_met = span
 
     def halo_scratch(rows):
-        return [pltpu.VMEM((5, rows, lanes), F32), pltpu.VMEM((5, rows, lanes), F32), pltpu.VMEM((rows, lanes), F32),
-                pltpu.VMEM((5, rows, lanes), F32)]
+        return [pltpu.VMEM((5, rows, lanes), F32)] * 3 + [pltpu.VMEM((rows, lanes), F32), pltpu.VMEM((5, rows, lanes), F32)]
+
+    faces = [pltpu.VMEM(((rows_i + 1) * rows_i, lanes), F32)]
 
     metric_halo, kept = None, ()
     start = state
@@ -558,30 +572,32 @@
         if metric_halo is None:
             metric_halo = core, chip, span_near, span_far
         line, span_line = shape(5, total, lanes), shape(5, span_rows, lanes)
-        normal, plus_i, minus_i, plus_j, minus_j, diffused, plus_k, minus_k, diffused_k, *squares = call(
+        (normal, plus_i, minus_i, centre_i, plus_j, minus_j, centre_j, diffused, plus_k, minus_k, centre_k, diffused_k,
+         *squares) = call(
             functools.partial(early_kernel, dims, kind, bool(kept)), "early", (state, span, span_met, met, *kept),
-            [field, line, line, line, line, line, span_line, span_line, span_line]
+            [field] + [line] * 7 + [span_line] * 4
             + ([] if kept else [shape(total, lanes), shape(total, lanes), shape(span_rows, lanes)]),
-            [], cost=10**8,
+            faces, cost=10**8,
         )
         kept = kept or tuple(squares)
         metric_i, metric_j, metric_k = kept
         (plane,) = call(
             functools.partial(chord_kernel, dims, kind), "chord",
-            (state, met, core, chip, metric_halo[0], metric_halo[1], normal, plus_i, minus_i, metric_i, diffused),
-            [field], halo_scratch(halo), cost=10**8,
+            (state, met, core, chip, metric_halo[0], metric_halo[1], normal, plus_i, minus_i, centre_i, metric_i,
+             diffused),
+            [field], halo_scratch(halo) + faces, cost=10**8,
         )
-        ins = (span, span_met, span_near, span_far, metric_halo[2], metric_halo[3], plus_k, minus_k, metric_k, diffused_k, wake_partner, state, met,
-               volume, blank, wake, plane, plus_j, minus_j, metric_j, diffused)
+        ins = (span, span_met, span_near, span_far, metric_halo[2], metric_halo[3], plus_k, minus_k, centre_k, metric_k,
+               diffused_k, wake_partner, state, met, volume, blank, wake, plane, plus_j, minus_j, centre_j, metric_j, diffused)
         ins += (start,) if final else ()
         state, *rest = call(
             functools.partial(span_kernel, dims, kind, final), "span", ins,
             [field] if final else [field, field] + parts(5),
             [pltpu.VMEM((5, span_rows, lanes), F32)] + halo_scratch(2 * H * 8) + [pltpu.VMEM((8, 2 * H * 8, lanes), F32)]
             + [pltpu.VMEM((5, H * rows_i, lanes), F32), pltpu.VMEM((5, total, lanes), F32)] + halo_scratch(H * rows_i)
-            + [pltpu.VMEM((rows_i * 16, lanes), F32), pltpu.SMEM((rows_i,), jnp.int32), pltpu.SemaphoreType.DMA]
+            + [pltpu.VMEM((rows_i * 16, lanes), F32), pltpu.SMEM((rows_i,), jnp.int32), pltpu.SemaphoreType.DMA] + faces
             + ([pltpu.VMEM((5, total, lanes), F32), pltpu.SemaphoreType.DMA((5,))] if final else []),
-            [whole] * 10 + [far] + [whole] * (len(ins) - 11),
+            [whole] * 11 + [far] + [whole] * (len(ins) - 12),
             cost=10**8, out_specs=[far] if final else None,
         )
         if not final:

time: 30.4 us -> 30.1 us (level)
    pallas_call x7, Pallas kernels: 15.5 us -> 15.2 us  [call(): pl.pallas_call(kernel, out_shape=outs, in_specs=specs or [whole] * len(in...]
where the time goes in v8:
time: 30.1 us; the launch traced here: 30 us
  Pallas kernels  15.2 us (50%)
  starting transfers between devices  14.5 us (48%)
    pallas_call x7, Pallas kernels, call(): pl.pallas_call(kernel, out_shape=outs, in_specs=specs or [whole] * len(in...  15.2 us
    ppermute x2, starting transfers between devices, exchange(): lax.ppermute(chip, 'wrap', chips)  5.54 us
    ppermute x2, starting transfers between devices, exchange(): lax.ppermute(span_far, 'span', far)  4.95 us
    ppermute x2, starting transfers between devices, exchange(): lax.ppermute(span_near, 'span', near)  2.7 us
    ppermute x2, starting transfers between devices, exchange(): lax.ppermute(wake, 'wrap', mirror)  0.76 us
  transfers between devices with their start and end apart: 10, of which 0 were waited for; matrix products, arithmetic and copies ran while one was open for 0% of the time, Pallas kernels for 27%

profile of v8, /device:TPU:0, one launch (start us, length us, event | category | flops | bytes accessed | tf_op | source)
XLA Modules:
  0.0 30.0 jit_solution(6980558435993854761)
XLA Ops:
  0.0 1.7 %prepare.1 = (f32[5,256,128]{2,1,0:T(8,128)S(1)}, f32[8,256,128]{2,1,0:T(8,128)S(1)}, f32[9,256,128]{2,1,0:T(8,128)S(1)}, f32[8,48,128]{2,1,0:T(8,128)S(1)}, f32...) custom-call(f32[256,128]{1,0:T(8,128)} %bitcast.13, ...), custom_call_target="tpu_custom_call" | custom-call | tf_op jit(solution)/shard_map/prepare/pallas_call | solution.py:533
  1.7 0.5 %collective-permute-start.3 = (f32[8,48,128]{2,1,0:T(8,128)S(1)}, f32[8,48,128]{2,1,0:T(8,128)S(1)}, u32[]{:S(2)}, u32[]{:S(2)}) collective-permute-start(f32[8,48,128]{2,1,0:T(8,128)S(1)} %get-tuple-element.58), channel_id=1, source_target_pairs={{0,4},{4,0},{8,12},{12,8},{16,20},{20,16},{24,28},{28,24},{1,5},{5... | collective-permute-start | bytes 589832 | tf_op jit(solution)/shard_map/ppermute | solution.py:518
  2.2 3.6 %collective-permute-start.4 = (f32[8,48,128]{2,1,0:T(8,128)S(1)}, f32[8,48,128]{2,1,0:T(8,128)S(1)}, u32[]{:S(2)}, u32[]{:S(2)}) collective-permute-start(f32[8,48,128]{2,1,0:T(8,128)S(1)} %get-tuple-element.59), channel_id=1, source_target_pairs={{4,8},{8,4},{12,16},{16,12},{20,24},{24,20},{28,0},{0,28},{5,9},{9... | collective-permute-start | bytes 589832 | tf_op jit(solution)/shard_map/ppermute | solution.py:518
  5.7 0.0 collective-permute-start.2
  5.8 1.7 %collective-permute-start = (f32[8,8,128]{2,1,0:T(8,128)S(1)}, f32[8,8,128]{2,1,0:T(8,128)S(1)}, u32[]{:S(2)}, u32[]{:S(2)}) collective-permute-start(f32[8,8,128]{2,1,0:T(8,128)S(1)} %get-tuple-element.48), channel_id=1, source_target_pairs={{0,1},{1,0},{2,3},{3,2},{4,5},{5,4},{6,7},{7,6},{8,9},{9,8},{10,11... | collective-permute-start | bytes 98312 | tf_op jit(solution)/shard_map/ppermute | solution.py:519
  7.5 2.5 %collective-permute-start.1 = (f32[8,8,128]{2,1,0:T(8,128)S(1)}, f32[8,8,128]{2,1,0:T(8,128)S(1)}, u32[]{:S(2)}, u32[]{:S(2)}) collective-permute-start(f32[8,8,128]{2,1,0:T(8,128)S(1)} %get-tuple-element.49), channel_id=1, source_target_pairs={{1,2},{2,1},{3,0},{0,3},{5,6},{6,5},{7,4},{4,7},{9,10},{10,9},{11,... | collective-permute-start | bytes 98312 | tf_op jit(solution)/shard_map/ppermute | solution.py:519
  10.0 2.6 %early.2 = (f32[5,256,128]{2,1,0:T(8,128)S(1)}, f32[5,256,128]{2,1,0:T(8,128)S(1)}, f32[5,256,128]{2,1,0:T(8,128)S(1)}, f32[5,256,128]{2,1,0:T(8,128)S(1)}, f32[...) custom-call(f32[5,256,128]{2,1,0:T(8,128)S(1)} %get-tuple-element.50, ...), custom_call_target="tpu_custom_call" | custom-call | flops 100000000 | bytes 25000000 | tf_op jit(solution)/shard_map/early/pallas_call | solution.py:533
  12.6 0.0 collective-permute-done.3.core_ref.met_core_ref
  12.6 0.0 collective-permute-done.4.chip_ref.met_chip_ref
  12.6 0.0 copy-start
  12.6 0.0 copy-start.1
  12.6 1.8 %chord.2.refs_17_ = f32[5,256,128]{2,1,0:T(8,128)S(1)} custom-call(f32[5,256,128]{2,1,0:T(8,128)S(1)} %get-tuple-element.50.state_ref.refs_12_.refs_23_, f32[9,256,128]{2,1,0:T(8,128)S(1)} %get-tuple-element.51.met_ref.refs_13_, f32[8,48,128]{2,1,0:T(8,128)S(1)} %collective-permute-done.3.core_ref.met_core_ref, ...), custom_call_target="tpu_custom_call" | custom-call | flops 100000000 | bytes 25000000 | tf_op jit(solution)/shard_map/chord/pallas_call | solution.py:533
  14.4 0.0 collective-permute-done.refs_2_.refs_4_
  14.4 0.0 collective-permute-done.2.refs_16_
  14.5 2.8 %span.2 = (f32[5,256,128]{2,1,0:T(8,128)S(1)}, f32[5,256,128]{2,1,0:T(8,128)S(1)}, f32[5,48,128]{2,1,0:T(8,128)S(1)}, f32[5,48,128]{2,1,0:T(8,128)S(1)}, f32[256...) custom-call(f32[8,256,128]{2,1,0:T(8,128)S(1)} %get-tuple-element.47.span_ref.span_met_ref.refs_0_.refs_1_, ...), custom_call_target="tpu_custom_call" | custom-call | flops 100000000 | bytes 25000000 | tf_op jit(solution)/shard_map/span/pallas_call | solution.py:533
  17.3 0.1 collective-permute-start.8
  17.4 2.0 %collective-permute-start.9 = (f32[5,48,128]{2,1,0:T(8,128)S(1)}, f32[5,48,128]{2,1,0:T(8,128)S(1)}, u32[]{:S(2)}, u32[]{:S(2)}) collective-permute-start(f32[5,48,128]{2,1,0:T(8,128)S(1)} %get-tuple-element.80), channel_id=1, source_target_pairs={{4,8},{8,4},{12,16},{16,12},{20,24},{24,20},{28,0},{0,28},{5,9},{9... | collective-permute-start | bytes 368648 | tf_op jit(solution)/shard_map/ppermute | solution.py:518
  19.4 0.7 %collective-permute-start.7 = (f32[256,128]{1,0:T(8,128)S(1)}, f32[256,128]{1,0:T(8,128)S(1)}, u32[]{:S(2)}, u32[]{:S(2)}) collective-permute-start(f32[256,128]{1,0:T(8,128)S(1)} %get-tuple-element.78), channel_id=1, source_target_pairs={{0,28},{4,24},{8,20},{12,16},{16,12},{20,8},{24,4},{28,0},{1,29},{... | collective-permute-start | bytes 393224 | tf_op jit(solution)/shard_map/ppermute | solution.py:518
  20.1 1.0 %collective-permute-start.5 = (f32[5,8,128]{2,1,0:T(8,128)S(1)}, f32[5,8,128]{2,1,0:T(8,128)S(1)}, u32[]{:S(2)}, u32[]{:S(2)}) collective-permute-start(f32[5,8,128]{2,1,0:T(8,128)S(1)} %get-tuple-element.71), channel_id=1, source_target_pairs={{0,1},{1,0},{2,3},{3,2},{4,5},{5,4},{6,7},{7,6},{8,9},{9,8},{10,11... | collective-permute-start | bytes 61448 | tf_op jit(solution)/shard_map/ppermute | solution.py:519
  21.1 2.5 %collective-permute-start.6 = (f32[5,8,128]{2,1,0:T(8,128)S(1)}, f32[5,8,128]{2,1,0:T(8,128)S(1)}, u32[]{:S(2)}, u32[]{:S(2)}) collective-permute-start(f32[5,8,128]{2,1,0:T(8,128)S(1)} %get-tuple-element.72), channel_id=1, source_target_pairs={{1,2},{2,1},{3,0},{0,3},{5,6},{6,5},{7,4},{4,7},{9,10},{10,9},{11,... | collective-permute-start | bytes 61448 | tf_op jit(solution)/shard_map/ppermute | solution.py:519
  23.6 2.3 %early.3 = (f32[5,256,128]{2,1,0:T(8,128)S(1)}, f32[5,256,128]{2,1,0:T(8,128)S(1)}, f32[5,256,128]{2,1,0:T(8,128)S(1)}, f32[5,256,128]{2,1,0:T(8,128)S(1)}, f32[...) custom-call(f32[5,256,128]{2,1,0:T(8,128)S(1)} %get-tuple-element.73, ...), custom_call_target="tpu_custom_call" | custom-call | flops 100000000 | bytes 25000000 | tf_op jit(solution)/shard_map/early/pallas_call | solution.py:533
  25.9 0.0 collective-permute-done.9.chip_ref
  25.9 1.3 %chord.3.refs_17_ = f32[5,256,128]{2,1,0:T(8,128)S(1)} custom-call(f32[5,256,128]{2,1,0:T(8,128)S(1)} %get-tuple-element.73.state_ref.refs_12_, f32[9,256,128]{2,1,0:T(8,128)S(1)} %get-tuple-element.51.met_ref.refs_13_, f32[5,48,128]{2,1,0:T(8,128)S(1)} %collective-permute-done.8.core_ref, f32[5,48,128]{2,1,0:T(8,128)S(1)} %collective-permute-done.9.chip_ref, ...), custom_call_target="tpu_custom_call" | custom-call | flops 100000000 | bytes 25000000 | tf_op jit(solution)/shard_map/chord/pallas_call | solution.py:533
  27.2 2.7 %span.3 = f32[5,256,128]{2,1,0:T(8,128)} custom-call(f32[5,256,128]{2,1,0:T(8,128)S(1)} %get-tuple-element.70.span_ref.refs_0_, f32[8,256,128]{2,1,0:T(8,128)S(1)} %get-tuple-element.47.span_ref.span_met_ref.refs_0_.refs_1_, f32[5,8,128]{2,1,0:T(8,128)S(1)} %collective-permute-done.5.refs_2_, f32[5,8,128]{2,1,0:T(8,128)S(1)} %collective-permute-done.6.refs_3_, ...), custom_call_target="tpu_custom_call" | custom-call | flops 100000000 | bytes 25000000 | tf_op jit(solution)/shard_map/span/pallas_call | solution.py:533
  (7 shorter events, 0.0 us)
Async XLA Ops:
  1.7 10.9 %collective-permute-start.3 = (f32[8,48,128]{2,1,0:T(8,128)S(1)}, f32[8,48,128]{2,1,0:T(8,128)S(1)}, u32[]{:S(2)}, u32[]{:S(2)}) collective-permute-start(f32[8,48,128]{2,1,0:T(8,128)S(1)} %get-tuple-element.58), channel_id=1, source_target_pairs={{0,4},{4,0},{8,12},{12,8},{16,20},{20,16},{24,28},{28,24},{1,5},{5... | collective-permute-start | bytes 589832 | tf_op jit(solution)/shard_map/ppermute | solution.py:518
  2.2 10.4 %collective-permute-start.4 = (f32[8,48,128]{2,1,0:T(8,128)S(1)}, f32[8,48,128]{2,1,0:T(8,128)S(1)}, u32[]{:S(2)}, u32[]{:S(2)}) collective-permute-start(f32[8,48,128]{2,1,0:T(8,128)S(1)} %get-tuple-element.59), channel_id=1, source_target_pairs={{4,8},{8,4},{12,16},{16,12},{20,24},{24,20},{28,0},{0,28},{5,9},{9... | collective-permute-start | bytes 589832 | tf_op jit(solution)/shard_map/ppermute | solution.py:518
  5.7 8.7 %collective-permute-start.2 = (f32[256,128]{1,0:T(8,128)S(1)}, f32[256,128]{1,0:T(8,128)S(1)}, u32[]{:S(2)}, u32[]{:S(2)}) collective-permute-start(f32[256,128]{1,0:T(8,128)S(1)} %get-tuple-element.57), channel_id=1, source_target_pairs={{0,28},{4,24},{8,20},{12,16},{16,12},{20,8},{24,4},{28,0},{1,29},{... | collective-permute-start | bytes 393224 | tf_op jit(solution)/shard_map/ppermute | solution.py:518
  5.8 8.6 %collective-permute-start = (f32[8,8,128]{2,1,0:T(8,128)S(1)}, f32[8,8,128]{2,1,0:T(8,128)S(1)}, u32[]{:S(2)}, u32[]{:S(2)}) collective-permute-start(f32[8,8,128]{2,1,0:T(8,128)S(1)} %get-tuple-element.48), channel_id=1, source_target_pairs={{0,1},{1,0},{2,3},{3,2},{4,5},{5,4},{6,7},{7,6},{8,9},{9,8},{10,11... | collective-permute-start | bytes 98312 | tf_op jit(solution)/shard_map/ppermute | solution.py:519
  7.5 7.0 %collective-permute-start.1 = (f32[8,8,128]{2,1,0:T(8,128)S(1)}, f32[8,8,128]{2,1,0:T(8,128)S(1)}, u32[]{:S(2)}, u32[]{:S(2)}) collective-permute-start(f32[8,8,128]{2,1,0:T(8,128)S(1)} %get-tuple-element.49), channel_id=1, source_target_pairs={{1,2},{2,1},{3,0},{0,3},{5,6},{6,5},{7,4},{4,7},{9,10},{10,9},{11,... | collective-permute-start | bytes 98312 | tf_op jit(solution)/shard_map/ppermute | solution.py:519
  12.6 1.9 %copy-start = (f32[16,16,128]{2,1,0:T(8,128)S(1)}, f32[16,16,128]{2,1,0:T(8,128)}, u32[]{:S(2)}) copy-start(f32[16,16,128]{2,1,0:T(8,128)} %param.11) | copy-start | bytes 393220
  12.6 1.9 %copy-start.1 = (s32[16,16,128]{2,1,0:T(8,128)S(1)}, s32[16,16,128]{2,1,0:T(8,128)}, u32[]{:S(2)}) copy-start(s32[16,16,128]{2,1,0:T(8,128)} %param.13) | copy-start | bytes 393220
  17.3 8.5 %collective-permute-start.8 = (f32[5,48,128]{2,1,0:T(8,128)S(1)}, f32[5,48,128]{2,1,0:T(8,128)S(1)}, u32[]{:S(2)}, u32[]{:S(2)}) collective-permute-start(f32[5,48,128]{2,1,0:T(8,128)S(1)} %get-tuple-element.79), channel_id=1, source_target_pairs={{0,4},{4,0},{8,12},{12,8},{16,20},{20,16},{24,28},{28,24},{1,5},{5... | collective-permute-start | bytes 368648 | tf_op jit(solution)/shard_map/ppermute | solution.py:518
  17.4 8.5 %collective-permute-start.9 = (f32[5,48,128]{2,1,0:T(8,128)S(1)}, f32[5,48,128]{2,1,0:T(8,128)S(1)}, u32[]{:S(2)}, u32[]{:S(2)}) collective-permute-start(f32[5,48,128]{2,1,0:T(8,128)S(1)} %get-tuple-element.80), channel_id=1, source_target_pairs={{4,8},{8,4},{12,16},{16,12},{20,24},{24,20},{28,0},{0,28},{5,9},{9... | collective-permute-start | bytes 368648 | tf_op jit(solution)/shard_map/ppermute | solution.py:518
  19.4 7.8 %collective-permute-start.7 = (f32[256,128]{1,0:T(8,128)S(1)}, f32[256,128]{1,0:T(8,128)S(1)}, u32[]{:S(2)}, u32[]{:S(2)}) collective-permute-start(f32[256,128]{1,0:T(8,128)S(1)} %get-tuple-element.78), channel_id=1, source_target_pairs={{0,28},{4,24},{8,20},{12,16},{16,12},{20,8},{24,4},{28,0},{1,29},{... | collective-permute-start | bytes 393224 | tf_op jit(solution)/shard_map/ppermute | solution.py:518
  20.1 7.1 %collective-permute-start.5 = (f32[5,8,128]{2,1,0:T(8,128)S(1)}, f32[5,8,128]{2,1,0:T(8,128)S(1)}, u32[]{:S(2)}, u32[]{:S(2)}) collective-permute-start(f32[5,8,128]{2,1,0:T(8,128)S(1)} %get-tuple-element.71), channel_id=1, source_target_pairs={{0,1},{1,0},{2,3},{3,2},{4,5},{5,4},{6,7},{7,6},{8,9},{9,8},{10,11... | collective-permute-start | bytes 61448 | tf_op jit(solution)/shard_map/ppermute | solution.py:519
  21.1 6.1 %collective-permute-start.6 = (f32[5,8,128]{2,1,0:T(8,128)S(1)}, f32[5,8,128]{2,1,0:T(8,128)S(1)}, u32[]{:S(2)}, u32[]{:S(2)}) collective-permute-start(f32[5,8,128]{2,1,0:T(8,128)S(1)} %get-tuple-element.72), channel_id=1, source_target_pairs={{1,2},{2,1},{3,0},{0,3},{5,6},{6,5},{7,4},{4,7},{9,10},{10,9},{11,... | collective-permute-start | bytes 61448 | tf_op jit(solution)/shard_map/ppermute | solution.py:519

commit v9 on v8

--- a/solution.py
+++ b/solution.py
@@ -313,7 +313,7 @@
               flat=rows_i - 1)
         return carry
 
-    lax.fori_loop(0, 5, normal, 0)
+    lax.fori_loop(0, 5, normal, 0, unroll=5)
 
 
 def chord_kernel(dims, kind, state_ref, met_ref, core_ref, chip_ref, met_core_ref, met_chip_ref, normal_ref,
@@ -368,7 +368,7 @@
               store, -1, rows_i - 1)
         return carry
 
-    lax.fori_loop(0, 5, chord, 0)
+    lax.fori_loop(0, 5, chord, 0, unroll=5)
 
 
 def span_kernel(dims, kind, final, *refs):
@@ -440,7 +440,7 @@
               store, -1, height // 2 - 1)
         return carry
 
-    lax.fori_loop(0, 5, sweep_span, 0)
+    lax.fori_loop(0, 5, sweep_span, 0, unroll=5)
 
     fetch.wait()
     base = (count - 1 - position) * rows_i

time: 30.1 us -> 29.8 us (0.990)
  Pallas kernels: 15.2 us -> 14.8 us
    pallas_call x7, Pallas kernels: 15.2 us -> 14.8 us  [call(): pl.pallas_call(kernel, out_shape=outs, in_specs=specs or [whole] * len(in...]
  transfers between devices with their start and end apart: 10 -> 10, of which waited for: 0 -> 0; matrix products, arithmetic and copies ran while one was open for 0% -> 0% of each run, Pallas kernels for 27% -> 26%
where the time goes in v9:
time: 29.8 us; the launch traced here: 29.6 us
  Pallas kernels  14.8 us (50%)
  starting transfers between devices  14.7 us (49%)
    pallas_call x7, Pallas kernels, call(): pl.pallas_call(kernel, out_shape=outs, in_specs=specs or [whole] * len(in...  14.8 us
    ppermute x2, starting transfers between devices, exchange(): lax.ppermute(chip, 'wrap', chips)  5.54 us
    ppermute x2, starting transfers between devices, exchange(): lax.ppermute(span_far, 'span', far)  4.95 us
    ppermute x2, starting transfers between devices, exchange(): lax.ppermute(span_near, 'span', near)  2.84 us
    ppermute x2, starting transfers between devices, exchange(): lax.ppermute(wake, 'wrap', mirror)  0.76 us
  transfers between devices with their start and end apart: 10, of which 0 were waited for; matrix products, arithmetic and copies ran while one was open for 0% of the time, Pallas kernels for 26%

profile of v9, /device:TPU:0, one launch (start us, length us, event | category | flops | bytes accessed | tf_op | source)
XLA Modules:
  0.0 29.6 jit_solution(17190097681965268385)
XLA Ops:
  0.0 1.7 %prepare.1 = (f32[5,256,128]{2,1,0:T(8,128)S(1)}, f32[8,256,128]{2,1,0:T(8,128)S(1)}, f32[9,256,128]{2,1,0:T(8,128)S(1)}, f32[8,48,128]{2,1,0:T(8,128)S(1)}, f32...) custom-call(f32[256,128]{1,0:T(8,128)} %bitcast.13, ...), custom_call_target="tpu_custom_call" | custom-call | tf_op jit(solution)/shard_map/prepare/pallas_call | solution.py:533
  1.7 0.5 %collective-permute-start.3 = (f32[8,48,128]{2,1,0:T(8,128)S(1)}, f32[8,48,128]{2,1,0:T(8,128)S(1)}, u32[]{:S(2)}, u32[]{:S(2)}) collective-permute-start(f32[8,48,128]{2,1,0:T(8,128)S(1)} %get-tuple-element.58), channel_id=1, source_target_pairs={{0,4},{4,0},{8,12},{12,8},{16,20},{20,16},{24,28},{28,24},{1,5},{5... | collective-permute-start | bytes 589832 | tf_op jit(solution)/shard_map/ppermute | solution.py:518
  2.2 3.6 %collective-permute-start.4 = (f32[8,48,128]{2,1,0:T(8,128)S(1)}, f32[8,48,128]{2,1,0:T(8,128)S(1)}, u32[]{:S(2)}, u32[]{:S(2)}) collective-permute-start(f32[8,48,128]{2,1,0:T(8,128)S(1)} %get-tuple-element.59), channel_id=1, source_target_pairs={{4,8},{8,4},{12,16},{16,12},{20,24},{24,20},{28,0},{0,28},{5,9},{9... | collective-permute-start | bytes 589832 | tf_op jit(solution)/shard_map/ppermute | solution.py:518
  5.7 0.0 collective-permute-start.2
  5.8 1.7 %collective-permute-start = (f32[8,8,128]{2,1,0:T(8,128)S(1)}, f32[8,8,128]{2,1,0:T(8,128)S(1)}, u32[]{:S(2)}, u32[]{:S(2)}) collective-permute-start(f32[8,8,128]{2,1,0:T(8,128)S(1)} %get-tuple-element.48), channel_id=1, source_target_pairs={{0,1},{1,0},{2,3},{3,2},{4,5},{5,4},{6,7},{7,6},{8,9},{9,8},{10,11... | collective-permute-start | bytes 98312 | tf_op jit(solution)/shard_map/ppermute | solution.py:519
  7.5 2.5 %collective-permute-start.1 = (f32[8,8,128]{2,1,0:T(8,128)S(1)}, f32[8,8,128]{2,1,0:T(8,128)S(1)}, u32[]{:S(2)}, u32[]{:S(2)}) collective-permute-start(f32[8,8,128]{2,1,0:T(8,128)S(1)} %get-tuple-element.49), channel_id=1, source_target_pairs={{1,2},{2,1},{3,0},{0,3},{5,6},{6,5},{7,4},{4,7},{9,10},{10,9},{11,... | collective-permute-start | bytes 98312 | tf_op jit(solution)/shard_map/ppermute | solution.py:519
  10.0 2.6 %early.2 = (f32[5,256,128]{2,1,0:T(8,128)S(1)}, f32[5,256,128]{2,1,0:T(8,128)S(1)}, f32[5,256,128]{2,1,0:T(8,128)S(1)}, f32[5,256,128]{2,1,0:T(8,128)S(1)}, f32[...) custom-call(f32[5,256,128]{2,1,0:T(8,128)S(1)} %get-tuple-element.50, ...), custom_call_target="tpu_custom_call" | custom-call | flops 100000000 | bytes 25000000 | tf_op jit(solution)/shard_map/early/pallas_call | solution.py:533
  12.5 0.0 collective-permute-done.3.core_ref.met_core_ref
  12.5 0.0 copy-start
  12.6 0.0 copy-start.1
  12.6 1.7 %chord.2.refs_17_ = f32[5,256,128]{2,1,0:T(8,128)S(1)} custom-call(f32[5,256,128]{2,1,0:T(8,128)S(1)} %get-tuple-element.50.state_ref.refs_12_.refs_23_, f32[9,256,128]{2,1,0:T(8,128)S(1)} %get-tuple-element.51.met_ref.refs_13_, f32[8,48,128]{2,1,0:T(8,128)S(1)} %collective-permute-done.3.core_ref.met_core_ref, ...), custom_call_target="tpu_custom_call" | custom-call | flops 100000000 | bytes 25000000 | tf_op jit(solution)/shard_map/chord/pallas_call | solution.py:533
  14.3 0.0 collective-permute-done.2.refs_16_
  14.3 2.7 %span.2 = (f32[5,256,128]{2,1,0:T(8,128)S(1)}, f32[5,256,128]{2,1,0:T(8,128)S(1)}, f32[5,48,128]{2,1,0:T(8,128)S(1)}, f32[5,48,128]{2,1,0:T(8,128)S(1)}, f32[256...) custom-call(f32[8,256,128]{2,1,0:T(8,128)S(1)} %get-tuple-element.47.span_ref.span_met_ref.refs_0_.refs_1_, ...), custom_call_target="tpu_custom_call" | custom-call | flops 100000000 | bytes 25000000 | tf_op jit(solution)/shard_map/span/pallas_call | solution.py:533
  17.1 0.1 collective-permute-start.8
  17.2 2.0 %collective-permute-start.9 = (f32[5,48,128]{2,1,0:T(8,128)S(1)}, f32[5,48,128]{2,1,0:T(8,128)S(1)}, u32[]{:S(2)}, u32[]{:S(2)}) collective-permute-start(f32[5,48,128]{2,1,0:T(8,128)S(1)} %get-tuple-element.80), channel_id=1, source_target_pairs={{4,8},{8,4},{12,16},{16,12},{20,24},{24,20},{28,0},{0,28},{5,9},{9... | collective-permute-start | bytes 368648 | tf_op jit(solution)/shard_map/ppermute | solution.py:518
  19.1 0.7 %collective-permute-start.7 = (f32[256,128]{1,0:T(8,128)S(1)}, f32[256,128]{1,0:T(8,128)S(1)}, u32[]{:S(2)}, u32[]{:S(2)}) collective-permute-start(f32[256,128]{1,0:T(8,128)S(1)} %get-tuple-element.78), channel_id=1, source_target_pairs={{0,28},{4,24},{8,20},{12,16},{16,12},{20,8},{24,4},{28,0},{1,29},{... | collective-permute-start | bytes 393224 | tf_op jit(solution)/shard_map/ppermute | solution.py:518
  19.9 1.1 %collective-permute-start.5 = (f32[5,8,128]{2,1,0:T(8,128)S(1)}, f32[5,8,128]{2,1,0:T(8,128)S(1)}, u32[]{:S(2)}, u32[]{:S(2)}) collective-permute-start(f32[5,8,128]{2,1,0:T(8,128)S(1)} %get-tuple-element.71), channel_id=1, source_target_pairs={{0,1},{1,0},{2,3},{3,2},{4,5},{5,4},{6,7},{7,6},{8,9},{9,8},{10,11... | collective-permute-start | bytes 61448 | tf_op jit(solution)/shard_map/ppermute | solution.py:519
  21.0 2.5 %collective-permute-start.6 = (f32[5,8,128]{2,1,0:T(8,128)S(1)}, f32[5,8,128]{2,1,0:T(8,128)S(1)}, u32[]{:S(2)}, u32[]{:S(2)}) collective-permute-start(f32[5,8,128]{2,1,0:T(8,128)S(1)} %get-tuple-element.72), channel_id=1, source_target_pairs={{1,2},{2,1},{3,0},{0,3},{5,6},{6,5},{7,4},{4,7},{9,10},{10,9},{11,... | collective-permute-start | bytes 61448 | tf_op jit(solution)/shard_map/ppermute | solution.py:519
  23.5 2.2 %early.3 = (f32[5,256,128]{2,1,0:T(8,128)S(1)}, f32[5,256,128]{2,1,0:T(8,128)S(1)}, f32[5,256,128]{2,1,0:T(8,128)S(1)}, f32[5,256,128]{2,1,0:T(8,128)S(1)}, f32[...) custom-call(f32[5,256,128]{2,1,0:T(8,128)S(1)} %get-tuple-element.73, ...), custom_call_target="tpu_custom_call" | custom-call | flops 100000000 | bytes 25000000 | tf_op jit(solution)/shard_map/early/pallas_call | solution.py:533
  25.7 0.0 collective-permute-done.8.core_ref
  25.7 1.2 %chord.3.refs_17_ = f32[5,256,128]{2,1,0:T(8,128)S(1)} custom-call(f32[5,256,128]{2,1,0:T(8,128)S(1)} %get-tuple-element.73.state_ref.refs_12_, f32[9,256,128]{2,1,0:T(8,128)S(1)} %get-tuple-element.51.met_ref.refs_13_, f32[5,48,128]{2,1,0:T(8,128)S(1)} %collective-permute-done.8.core_ref, f32[5,48,128]{2,1,0:T(8,128)S(1)} %collective-permute-done.9.chip_ref, ...), custom_call_target="tpu_custom_call" | custom-call | flops 100000000 | bytes 25000000 | tf_op jit(solution)/shard_map/chord/pallas_call | solution.py:533
  26.9 0.0 collective-permute-done.5.refs_2_
  27.0 0.0 collective-permute-done.6.refs_3_
  27.0 2.7 %span.3 = f32[5,256,128]{2,1,0:T(8,128)} custom-call(f32[5,256,128]{2,1,0:T(8,128)S(1)} %get-tuple-element.70.span_ref.refs_0_, f32[8,256,128]{2,1,0:T(8,128)S(1)} %get-tuple-element.47.span_ref.span_met_ref.refs_0_.refs_1_, f32[5,8,128]{2,1,0:T(8,128)S(1)} %collective-permute-done.5.refs_2_, f32[5,8,128]{2,1,0:T(8,128)S(1)} %collective-permute-done.6.refs_3_, ...), custom_call_target="tpu_custom_call" | custom-call | flops 100000000 | bytes 25000000 | tf_op jit(solution)/shard_map/span/pallas_call | solution.py:533
  (7 shorter events, 0.0 us)
Async XLA Ops:
  1.7 10.9 %collective-permute-start.3 = (f32[8,48,128]{2,1,0:T(8,128)S(1)}, f32[8,48,128]{2,1,0:T(8,128)S(1)}, u32[]{:S(2)}, u32[]{:S(2)}) collective-permute-start(f32[8,48,128]{2,1,0:T(8,128)S(1)} %get-tuple-element.58), channel_id=1, source_target_pairs={{0,4},{4,0},{8,12},{12,8},{16,20},{20,16},{24,28},{28,24},{1,5},{5... | collective-permute-start | bytes 589832 | tf_op jit(solution)/shard_map/ppermute | solution.py:518
  2.2 10.3 %collective-permute-start.4 = (f32[8,48,128]{2,1,0:T(8,128)S(1)}, f32[8,48,128]{2,1,0:T(8,128)S(1)}, u32[]{:S(2)}, u32[]{:S(2)}) collective-permute-start(f32[8,48,128]{2,1,0:T(8,128)S(1)} %get-tuple-element.59), channel_id=1, source_target_pairs={{4,8},{8,4},{12,16},{16,12},{20,24},{24,20},{28,0},{0,28},{5,9},{9... | collective-permute-start | bytes 589832 | tf_op jit(solution)/shard_map/ppermute | solution.py:518
  5.7 8.6 %collective-permute-start.2 = (f32[256,128]{1,0:T(8,128)S(1)}, f32[256,128]{1,0:T(8,128)S(1)}, u32[]{:S(2)}, u32[]{:S(2)}) collective-permute-start(f32[256,128]{1,0:T(8,128)S(1)} %get-tuple-element.57), channel_id=1, source_target_pairs={{0,28},{4,24},{8,20},{12,16},{16,12},{20,8},{24,4},{28,0},{1,29},{... | collective-permute-start | bytes 393224 | tf_op jit(solution)/shard_map/ppermute | solution.py:518
  5.8 8.5 %collective-permute-start = (f32[8,8,128]{2,1,0:T(8,128)S(1)}, f32[8,8,128]{2,1,0:T(8,128)S(1)}, u32[]{:S(2)}, u32[]{:S(2)}) collective-permute-start(f32[8,8,128]{2,1,0:T(8,128)S(1)} %get-tuple-element.48), channel_id=1, source_target_pairs={{0,1},{1,0},{2,3},{3,2},{4,5},{5,4},{6,7},{7,6},{8,9},{9,8},{10,11... | collective-permute-start | bytes 98312 | tf_op jit(solution)/shard_map/ppermute | solution.py:519
  7.5 6.8 %collective-permute-start.1 = (f32[8,8,128]{2,1,0:T(8,128)S(1)}, f32[8,8,128]{2,1,0:T(8,128)S(1)}, u32[]{:S(2)}, u32[]{:S(2)}) collective-permute-start(f32[8,8,128]{2,1,0:T(8,128)S(1)} %get-tuple-element.49), channel_id=1, source_target_pairs={{1,2},{2,1},{3,0},{0,3},{5,6},{6,5},{7,4},{4,7},{9,10},{10,9},{11,... | collective-permute-start | bytes 98312 | tf_op jit(solution)/shard_map/ppermute | solution.py:519
  12.5 1.8 %copy-start = (f32[16,16,128]{2,1,0:T(8,128)S(1)}, f32[16,16,128]{2,1,0:T(8,128)}, u32[]{:S(2)}) copy-start(f32[16,16,128]{2,1,0:T(8,128)} %param.11) | copy-start | bytes 393220
  12.6 1.8 %copy-start.1 = (s32[16,16,128]{2,1,0:T(8,128)S(1)}, s32[16,16,128]{2,1,0:T(8,128)}, u32[]{:S(2)}) copy-start(s32[16,16,128]{2,1,0:T(8,128)} %param.13) | copy-start | bytes 393220
  17.1 8.6 %collective-permute-start.8 = (f32[5,48,128]{2,1,0:T(8,128)S(1)}, f32[5,48,128]{2,1,0:T(8,128)S(1)}, u32[]{:S(2)}, u32[]{:S(2)}) collective-permute-start(f32[5,48,128]{2,1,0:T(8,128)S(1)} %get-tuple-element.79), channel_id=1, source_target_pairs={{0,4},{4,0},{8,12},{12,8},{16,20},{20,16},{24,28},{28,24},{1,5},{5... | collective-permute-start | bytes 368648 | tf_op jit(solution)/shard_map/ppermute | solution.py:518
  17.2 8.6 %collective-permute-start.9 = (f32[5,48,128]{2,1,0:T(8,128)S(1)}, f32[5,48,128]{2,1,0:T(8,128)S(1)}, u32[]{:S(2)}, u32[]{:S(2)}) collective-permute-start(f32[5,48,128]{2,1,0:T(8,128)S(1)} %get-tuple-element.80), channel_id=1, source_target_pairs={{4,8},{8,4},{12,16},{16,12},{20,24},{24,20},{28,0},{0,28},{5,9},{9... | collective-permute-start | bytes 368648 | tf_op jit(solution)/shard_map/ppermute | solution.py:518
  19.1 7.8 %collective-permute-start.7 = (f32[256,128]{1,0:T(8,128)S(1)}, f32[256,128]{1,0:T(8,128)S(1)}, u32[]{:S(2)}, u32[]{:S(2)}) collective-permute-start(f32[256,128]{1,0:T(8,128)S(1)} %get-tuple-element.78), channel_id=1, source_target_pairs={{0,28},{4,24},{8,20},{12,16},{16,12},{20,8},{24,4},{28,0},{1,29},{... | collective-permute-start | bytes 393224 | tf_op jit(solution)/shard_map/ppermute | solution.py:518
  19.9 7.1 %collective-permute-start.5 = (f32[5,8,128]{2,1,0:T(8,128)S(1)}, f32[5,8,128]{2,1,0:T(8,128)S(1)}, u32[]{:S(2)}, u32[]{:S(2)}) collective-permute-start(f32[5,8,128]{2,1,0:T(8,128)S(1)} %get-tuple-element.71), channel_id=1, source_target_pairs={{0,1},{1,0},{2,3},{3,2},{4,5},{5,4},{6,7},{7,6},{8,9},{9,8},{10,11... | collective-permute-start | bytes 61448 | tf_op jit(solution)/shard_map/ppermute | solution.py:519
  21.0 6.0 %collective-permute-start.6 = (f32[5,8,128]{2,1,0:T(8,128)S(1)}, f32[5,8,128]{2,1,0:T(8,128)S(1)}, u32[]{:S(2)}, u32[]{:S(2)}) collective-permute-start(f32[5,8,128]{2,1,0:T(8,128)S(1)} %get-tuple-element.72), channel_id=1, source_target_pairs={{1,2},{2,1},{3,0},{0,3},{5,6},{6,5},{7,4},{4,7},{9,10},{10,9},{11,... | collective-permute-start | bytes 61448 | tf_op jit(solution)/shard_map/ppermute | solution.py:519

commit v10 on v9

--- a/solution.py
+++ b/solution.py
@@ -282,7 +282,7 @@
         place((plus_j, minus_j, centre_j), metric_j, rows, state, prims, [unit(1, m, met_ref[3 + m, rows, :]) for m in range(3)])
         return carry
 
-    lax.fori_loop(0, rows_i, planes, 0, unroll=4)
+    lax.fori_loop(0, rows_i, planes, 0, unroll=8)
 
     def spans(n, carry):
         rows = aligned(n * 16, 16)
@@ -292,7 +292,7 @@
         place((plus_k, minus_k, centre_k), metric_k, rows, state, prims, [unit(2, m, span_met_ref[5 + m, rows, :]) for m in range(3)])
         return carry
 
-    lax.fori_loop(0, height // 2, spans, 0, unroll=4)
+    lax.fori_loop(0, height // 2, spans, 0, unroll=8)
 
     for n in range(2, rows_i - 1):
         low, high = (metric_j[pl.ds(m, rows_i, stride=rows_i), :] for m in (n, n + 1))

time: 29.8 us -> 30.1 us (1.010)
  no operation moved by 1% of the time
where the time goes in v10:
time: 30.1 us; the launch traced here: 29.9 us
  Pallas kernels  14.9 us (50%)
  starting transfers between devices  14.7 us (49%)
  between operations  0.32 us (1%)
    pallas_call x7, Pallas kernels, call(): pl.pallas_call(kernel, out_shape=outs, in_specs=specs or [whole] * len(in...  14.9 us
    ppermute x2, starting transfers between devices, exchange(): lax.ppermute(chip, 'wrap', chips)  5.55 us
    ppermute x2, starting transfers between devices, exchange(): lax.ppermute(span_far, 'span', far)  4.95 us
    ppermute x2, starting transfers between devices, exchange(): lax.ppermute(span_near, 'span', near)  2.88 us
    ppermute x2, starting transfers between devices, exchange(): lax.ppermute(wake, 'wrap', mirror)  0.75 us
  transfers between devices with their start and end apart: 10, of which 0 were waited for; matrix products, arithmetic and copies ran while one was open for 0% of the time, Pallas kernels for 26%

profile of v10, /device:TPU:0, one launch (start us, length us, event | category | flops | bytes accessed | tf_op | source)
XLA Modules:
  0.0 29.9 jit_solution(7209477684237554331)
XLA Ops:
  0.0 1.7 %prepare.1 = (f32[5,256,128]{2,1,0:T(8,128)S(1)}, f32[8,256,128]{2,1,0:T(8,128)S(1)}, f32[9,256,128]{2,1,0:T(8,128)S(1)}, f32[8,48,128]{2,1,0:T(8,128)S(1)}, f32...) custom-call(f32[256,128]{1,0:T(8,128)} %bitcast.13, ...), custom_call_target="tpu_custom_call" | custom-call | tf_op jit(solution)/shard_map/prepare/pallas_call | solution.py:533
  1.7 0.5 %collective-permute-start.3 = (f32[8,48,128]{2,1,0:T(8,128)S(1)}, f32[8,48,128]{2,1,0:T(8,128)S(1)}, u32[]{:S(2)}, u32[]{:S(2)}) collective-permute-start(f32[8,48,128]{2,1,0:T(8,128)S(1)} %get-tuple-element.58), channel_id=1, source_target_pairs={{0,4},{4,0},{8,12},{12,8},{16,20},{20,16},{24,28},{28,24},{1,5},{5... | collective-permute-start | bytes 589832 | tf_op jit(solution)/shard_map/ppermute | solution.py:518
  2.2 3.6 %collective-permute-start.4 = (f32[8,48,128]{2,1,0:T(8,128)S(1)}, f32[8,48,128]{2,1,0:T(8,128)S(1)}, u32[]{:S(2)}, u32[]{:S(2)}) collective-permute-start(f32[8,48,128]{2,1,0:T(8,128)S(1)} %get-tuple-element.59), channel_id=1, source_target_pairs={{4,8},{8,4},{12,16},{16,12},{20,24},{24,20},{28,0},{0,28},{5,9},{9... | collective-permute-start | bytes 589832 | tf_op jit(solution)/shard_map/ppermute | solution.py:518
  5.7 0.0 collective-permute-start.2
  5.8 1.7 %collective-permute-start = (f32[8,8,128]{2,1,0:T(8,128)S(1)}, f32[8,8,128]{2,1,0:T(8,128)S(1)}, u32[]{:S(2)}, u32[]{:S(2)}) collective-permute-start(f32[8,8,128]{2,1,0:T(8,128)S(1)} %get-tuple-element.48), channel_id=1, source_target_pairs={{0,1},{1,0},{2,3},{3,2},{4,5},{5,4},{6,7},{7,6},{8,9},{9,8},{10,11... | collective-permute-start | bytes 98312 | tf_op jit(solution)/shard_map/ppermute | solution.py:519
  7.5 2.5 %collective-permute-start.1 = (f32[8,8,128]{2,1,0:T(8,128)S(1)}, f32[8,8,128]{2,1,0:T(8,128)S(1)}, u32[]{:S(2)}, u32[]{:S(2)}) collective-permute-start(f32[8,8,128]{2,1,0:T(8,128)S(1)} %get-tuple-element.49), channel_id=1, source_target_pairs={{1,2},{2,1},{3,0},{0,3},{5,6},{6,5},{7,4},{4,7},{9,10},{10,9},{11,... | collective-permute-start | bytes 98312 | tf_op jit(solution)/shard_map/ppermute | solution.py:519
  10.0 2.5 %early.2 = (f32[5,256,128]{2,1,0:T(8,128)S(1)}, f32[5,256,128]{2,1,0:T(8,128)S(1)}, f32[5,256,128]{2,1,0:T(8,128)S(1)}, f32[5,256,128]{2,1,0:T(8,128)S(1)}, f32[...) custom-call(f32[5,256,128]{2,1,0:T(8,128)S(1)} %get-tuple-element.50, ...), custom_call_target="tpu_custom_call" | custom-call | flops 100000000 | bytes 25000000 | tf_op jit(solution)/shard_map/early/pallas_call | solution.py:533
  12.5 0.0 collective-permute-done.4.chip_ref.met_chip_ref
  12.5 0.0 copy-start
  12.5 0.0 copy-start.1
  12.5 1.7 %chord.2.refs_17_ = f32[5,256,128]{2,1,0:T(8,128)S(1)} custom-call(f32[5,256,128]{2,1,0:T(8,128)S(1)} %get-tuple-element.50.state_ref.refs_12_.refs_23_, f32[9,256,128]{2,1,0:T(8,128)S(1)} %get-tuple-element.51.met_ref.refs_13_, f32[8,48,128]{2,1,0:T(8,128)S(1)} %collective-permute-done.3.core_ref.met_core_ref, ...), custom_call_target="tpu_custom_call" | custom-call | flops 100000000 | bytes 25000000 | tf_op jit(solution)/shard_map/chord/pallas_call | solution.py:533
  14.2 0.0 collective-permute-done.1.refs_3_.refs_5_
  14.3 0.0 collective-permute-done.2.refs_16_
  14.3 2.7 %span.2 = (f32[5,256,128]{2,1,0:T(8,128)S(1)}, f32[5,256,128]{2,1,0:T(8,128)S(1)}, f32[5,48,128]{2,1,0:T(8,128)S(1)}, f32[5,48,128]{2,1,0:T(8,128)S(1)}, f32[256...) custom-call(f32[8,256,128]{2,1,0:T(8,128)S(1)} %get-tuple-element.47.span_ref.span_met_ref.refs_0_.refs_1_, ...), custom_call_target="tpu_custom_call" | custom-call | flops 100000000 | bytes 25000000 | tf_op jit(solution)/shard_map/span/pallas_call | solution.py:533
  17.0 0.1 collective-permute-start.8
  17.1 2.0 %collective-permute-start.9 = (f32[5,48,128]{2,1,0:T(8,128)S(1)}, f32[5,48,128]{2,1,0:T(8,128)S(1)}, u32[]{:S(2)}, u32[]{:S(2)}) collective-permute-start(f32[5,48,128]{2,1,0:T(8,128)S(1)} %get-tuple-element.80), channel_id=1, source_target_pairs={{4,8},{8,4},{12,16},{16,12},{20,24},{24,20},{28,0},{0,28},{5,9},{9... | collective-permute-start | bytes 368648 | tf_op jit(solution)/shard_map/ppermute | solution.py:518
  19.1 0.7 %collective-permute-start.7 = (f32[256,128]{1,0:T(8,128)S(1)}, f32[256,128]{1,0:T(8,128)S(1)}, u32[]{:S(2)}, u32[]{:S(2)}) collective-permute-start(f32[256,128]{1,0:T(8,128)S(1)} %get-tuple-element.78), channel_id=1, source_target_pairs={{0,28},{4,24},{8,20},{12,16},{16,12},{20,8},{24,4},{28,0},{1,29},{... | collective-permute-start | bytes 393224 | tf_op jit(solution)/shard_map/ppermute | solution.py:518
  19.8 1.2 %collective-permute-start.5 = (f32[5,8,128]{2,1,0:T(8,128)S(1)}, f32[5,8,128]{2,1,0:T(8,128)S(1)}, u32[]{:S(2)}, u32[]{:S(2)}) collective-permute-start(f32[5,8,128]{2,1,0:T(8,128)S(1)} %get-tuple-element.71), channel_id=1, source_target_pairs={{0,1},{1,0},{2,3},{3,2},{4,5},{5,4},{6,7},{7,6},{8,9},{9,8},{10,11... | collective-permute-start | bytes 61448 | tf_op jit(solution)/shard_map/ppermute | solution.py:519
  21.0 2.5 %collective-permute-start.6 = (f32[5,8,128]{2,1,0:T(8,128)S(1)}, f32[5,8,128]{2,1,0:T(8,128)S(1)}, u32[]{:S(2)}, u32[]{:S(2)}) collective-permute-start(f32[5,8,128]{2,1,0:T(8,128)S(1)} %get-tuple-element.72), channel_id=1, source_target_pairs={{1,2},{2,1},{3,0},{0,3},{5,6},{6,5},{7,4},{4,7},{9,10},{10,9},{11,... | collective-permute-start | bytes 61448 | tf_op jit(solution)/shard_map/ppermute | solution.py:519
  23.5 2.4 %early.3 = (f32[5,256,128]{2,1,0:T(8,128)S(1)}, f32[5,256,128]{2,1,0:T(8,128)S(1)}, f32[5,256,128]{2,1,0:T(8,128)S(1)}, f32[5,256,128]{2,1,0:T(8,128)S(1)}, f32[...) custom-call(f32[5,256,128]{2,1,0:T(8,128)S(1)} %get-tuple-element.73, ...), custom_call_target="tpu_custom_call" | custom-call | flops 100000000 | bytes 25000000 | tf_op jit(solution)/shard_map/early/pallas_call | solution.py:533
  25.9 1.2 %chord.3.refs_17_ = f32[5,256,128]{2,1,0:T(8,128)S(1)} custom-call(f32[5,256,128]{2,1,0:T(8,128)S(1)} %get-tuple-element.73.state_ref.refs_12_, f32[9,256,128]{2,1,0:T(8,128)S(1)} %get-tuple-element.51.met_ref.refs_13_, f32[5,48,128]{2,1,0:T(8,128)S(1)} %collective-permute-done.8.core_ref, f32[5,48,128]{2,1,0:T(8,128)S(1)} %collective-permute-done.9.chip_ref, ...), custom_call_target="tpu_custom_call" | custom-call | flops 100000000 | bytes 25000000 | tf_op jit(solution)/shard_map/chord/pallas_call | solution.py:533
  27.1 0.0 collective-permute-done.5.refs_2_
  27.1 0.0 collective-permute-done.7.refs_16_
  27.1 2.7 %span.3 = f32[5,256,128]{2,1,0:T(8,128)} custom-call(f32[5,256,128]{2,1,0:T(8,128)S(1)} %get-tuple-element.70.span_ref.refs_0_, f32[8,256,128]{2,1,0:T(8,128)S(1)} %get-tuple-element.47.span_ref.span_met_ref.refs_0_.refs_1_, f32[5,8,128]{2,1,0:T(8,128)S(1)} %collective-permute-done.5.refs_2_, f32[5,8,128]{2,1,0:T(8,128)S(1)} %collective-permute-done.6.refs_3_, ...), custom_call_target="tpu_custom_call" | custom-call | flops 100000000 | bytes 25000000 | tf_op jit(solution)/shard_map/span/pallas_call | solution.py:533
  (7 shorter events, 0.0 us)
Async XLA Ops:
  1.7 10.8 %collective-permute-start.3 = (f32[8,48,128]{2,1,0:T(8,128)S(1)}, f32[8,48,128]{2,1,0:T(8,128)S(1)}, u32[]{:S(2)}, u32[]{:S(2)}) collective-permute-start(f32[8,48,128]{2,1,0:T(8,128)S(1)} %get-tuple-element.58), channel_id=1, source_target_pairs={{0,4},{4,0},{8,12},{12,8},{16,20},{20,16},{24,28},{28,24},{1,5},{5... | collective-permute-start | bytes 589832 | tf_op jit(solution)/shard_map/ppermute | solution.py:518
  2.2 10.3 %collective-permute-start.4 = (f32[8,48,128]{2,1,0:T(8,128)S(1)}, f32[8,48,128]{2,1,0:T(8,128)S(1)}, u32[]{:S(2)}, u32[]{:S(2)}) collective-permute-start(f32[8,48,128]{2,1,0:T(8,128)S(1)} %get-tuple-element.59), channel_id=1, source_target_pairs={{4,8},{8,4},{12,16},{16,12},{20,24},{24,20},{28,0},{0,28},{5,9},{9... | collective-permute-start | bytes 589832 | tf_op jit(solution)/shard_map/ppermute | solution.py:518
  5.7 8.5 %collective-permute-start.2 = (f32[256,128]{1,0:T(8,128)S(1)}, f32[256,128]{1,0:T(8,128)S(1)}, u32[]{:S(2)}, u32[]{:S(2)}) collective-permute-start(f32[256,128]{1,0:T(8,128)S(1)} %get-tuple-element.57), channel_id=1, source_target_pairs={{0,28},{4,24},{8,20},{12,16},{16,12},{20,8},{24,4},{28,0},{1,29},{... | collective-permute-start | bytes 393224 | tf_op jit(solution)/shard_map/ppermute | solution.py:518
  5.8 8.5 %collective-permute-start = (f32[8,8,128]{2,1,0:T(8,128)S(1)}, f32[8,8,128]{2,1,0:T(8,128)S(1)}, u32[]{:S(2)}, u32[]{:S(2)}) collective-permute-start(f32[8,8,128]{2,1,0:T(8,128)S(1)} %get-tuple-element.48), channel_id=1, source_target_pairs={{0,1},{1,0},{2,3},{3,2},{4,5},{5,4},{6,7},{7,6},{8,9},{9,8},{10,11... | collective-permute-start | bytes 98312 | tf_op jit(solution)/shard_map/ppermute | solution.py:519
  7.5 6.8 %collective-permute-start.1 = (f32[8,8,128]{2,1,0:T(8,128)S(1)}, f32[8,8,128]{2,1,0:T(8,128)S(1)}, u32[]{:S(2)}, u32[]{:S(2)}) collective-permute-start(f32[8,8,128]{2,1,0:T(8,128)S(1)} %get-tuple-element.49), channel_id=1, source_target_pairs={{1,2},{2,1},{3,0},{0,3},{5,6},{6,5},{7,4},{4,7},{9,10},{10,9},{11,... | collective-permute-start | bytes 98312 | tf_op jit(solution)/shard_map/ppermute | solution.py:519
  12.5 1.8 %copy-start = (f32[16,16,128]{2,1,0:T(8,128)S(1)}, f32[16,16,128]{2,1,0:T(8,128)}, u32[]{:S(2)}) copy-start(f32[16,16,128]{2,1,0:T(8,128)} %param.11) | copy-start | bytes 393220
  12.5 1.8 %copy-start.1 = (s32[16,16,128]{2,1,0:T(8,128)S(1)}, s32[16,16,128]{2,1,0:T(8,128)}, u32[]{:S(2)}) copy-start(s32[16,16,128]{2,1,0:T(8,128)} %param.13) | copy-start | bytes 393220
  17.0 8.8 %collective-permute-start.8 = (f32[5,48,128]{2,1,0:T(8,128)S(1)}, f32[5,48,128]{2,1,0:T(8,128)S(1)}, u32[]{:S(2)}, u32[]{:S(2)}) collective-permute-start(f32[5,48,128]{2,1,0:T(8,128)S(1)} %get-tuple-element.79), channel_id=1, source_target_pairs={{0,4},{4,0},{8,12},{12,8},{16,20},{20,16},{24,28},{28,24},{1,5},{5... | collective-permute-start | bytes 368648 | tf_op jit(solution)/shard_map/ppermute | solution.py:518
  17.1 8.7 %collective-permute-start.9 = (f32[5,48,128]{2,1,0:T(8,128)S(1)}, f32[5,48,128]{2,1,0:T(8,128)S(1)}, u32[]{:S(2)}, u32[]{:S(2)}) collective-permute-start(f32[5,48,128]{2,1,0:T(8,128)S(1)} %get-tuple-element.80), channel_id=1, source_target_pairs={{4,8},{8,4},{12,16},{16,12},{20,24},{24,20},{28,0},{0,28},{5,9},{9... | collective-permute-start | bytes 368648 | tf_op jit(solution)/shard_map/ppermute | solution.py:518
  19.1 8.0 %collective-permute-start.7 = (f32[256,128]{1,0:T(8,128)S(1)}, f32[256,128]{1,0:T(8,128)S(1)}, u32[]{:S(2)}, u32[]{:S(2)}) collective-permute-start(f32[256,128]{1,0:T(8,128)S(1)} %get-tuple-element.78), channel_id=1, source_target_pairs={{0,28},{4,24},{8,20},{12,16},{16,12},{20,8},{24,4},{28,0},{1,29},{... | collective-permute-start | bytes 393224 | tf_op jit(solution)/shard_map/ppermute | solution.py:518
  19.8 7.3 %collective-permute-start.5 = (f32[5,8,128]{2,1,0:T(8,128)S(1)}, f32[5,8,128]{2,1,0:T(8,128)S(1)}, u32[]{:S(2)}, u32[]{:S(2)}) collective-permute-start(f32[5,8,128]{2,1,0:T(8,128)S(1)} %get-tuple-element.71), channel_id=1, source_target_pairs={{0,1},{1,0},{2,3},{3,2},{4,5},{5,4},{6,7},{7,6},{8,9},{9,8},{10,11... | collective-permute-start | bytes 61448 | tf_op jit(solution)/shard_map/ppermute | solution.py:519
  21.0 6.1 %collective-permute-start.6 = (f32[5,8,128]{2,1,0:T(8,128)S(1)}, f32[5,8,128]{2,1,0:T(8,128)S(1)}, u32[]{:S(2)}, u32[]{:S(2)}) collective-permute-start(f32[5,8,128]{2,1,0:T(8,128)S(1)} %get-tuple-element.72), channel_id=1, source_target_pairs={{1,2},{2,1},{3,0},{0,3},{5,6},{6,5},{7,4},{4,7},{9,10},{10,9},{11,... | collective-permute-start | bytes 61448 | tf_op jit(solution)/shard_map/ppermute | solution.py:519
